TPU v7x, 128 devices: a whole 4x4x4 slice. The times are simulated.
128 devices in a mesh: bx: 8 (over y, core), by: 16 (over z, x).
Axes of the slice: x: 4, y: 4, z: 4, core: 2. Of those that a mesh axis runs over, the one named last changes fastest.
Arguments:
- tracers: float32 [22, 2, 2048, 2048], P(None, None, 'bx', 'by'), may hold values from -6 to 6
- mixing: float32 [22, 2], replicated, may hold values from 0.003 to 0.025
- thickness: float32 [22], replicated, may hold values from 0.02 to 0.08
- levels: int32 [2048, 2048], P('bx', 'by'), may hold values from 1 to 22
- land: int32 [2048, 2048], P('bx', 'by'), may hold values 0 or 1
Outputs:
- tracers_new: float32 [22, 2, 2048, 2048], P(None, None, 'bx', 'by')
- surface: float32 [2048, 2048], P('bx', 'by')
- transports: float32 [2, 2048, 2048], P(None, 'bx', 'by')
All inputs are finite; a program needn't handle non-finite values. No bound on the sum of `land` on one device may be relied on, other than what follows from the above.
Results may differ from a plain program's by a relative error of at most 0.0003.
Values sent between devices are 32-bit elements; how exact they have to be, the bound alone decides.
No kernel may reach another device: no remote copies, remote signals or barrier semaphores. Data moves between devices by JAX's collectives and lax.ppermute only.
A program may use at most 320 MiB of HBM per device.

v0:
```python
import jax
import jax.numpy as jnp
from jax import lax
from jax.sharding import PartitionSpec as P

ITERS = 4


GRAVITY = 10.0
OFFSETS = (
    (-1, 0, 1.0),
    (1, 0, 1.0),
    (0, -1, 1.0),
    (0, 1, 1.0),
    (-1, -1, 0.25),
    (1, 1, 0.25),
    (-1, 1, 0.25),
    (1, -1, 0.25),
)


def padded(block, sides, width):
    for axis, dim in sides:
        count = lax.axis_size(axis)
        forward = [(i, i + 1) for i in range(count - 1)]
        forward.append((count - 1, 0))
        backward = [(target, source) for source, target in forward]
        low = lax.ppermute(
            lax.slice_in_dim(block, block.shape[dim] - width, None, axis=dim), axis, forward
        )
        high = lax.ppermute(lax.slice_in_dim(block, 0, width, axis=dim), axis, backward)
        block = jnp.concatenate([low, block, high], axis=dim)
    return block


def laplace(field, wet):
    centre = field[..., 1:-1, 1:-1]
    total = wet[..., :-2, 1:-1] * (field[..., :-2, 1:-1] - centre)
    total = total + wet[..., 2:, 1:-1] * (field[..., 2:, 1:-1] - centre)
    total = total + wet[..., 1:-1, :-2] * (field[..., 1:-1, :-2] - centre)
    total = total + wet[..., 1:-1, 2:] * (field[..., 1:-1, 2:] - centre)
    return wet[..., 1:-1, 1:-1] * total


def strip_extend(field):
    wider = padded(field, ((("bx", "by"), 0),), 1)
    return jnp.pad(wider, ((0, 0), (1, 1)))


def squares(residual):
    return lax.psum(jnp.sum(residual * residual), ("bx", "by"))


def solve(source, weights, extend):
    rows, cols = source.shape
    diagonal = 0.05 + weights[0]
    for extra in weights[1:]:
        diagonal = diagonal + extra
    surface_ext = jnp.zeros((rows + 2, cols + 2), jnp.float32)
    residual = source
    direction = source
    norm_now = squares(residual)
    for step in range(ITERS):
        direction_ext = extend(direction)
        result = diagonal * direction_ext[1:-1, 1:-1]
        for weight, (di, dj, factor) in zip(weights, OFFSETS):
            result = result - weight * direction_ext[1 + di : rows + 1 + di, 1 + dj : cols + 1 + dj]
        curve = lax.psum(jnp.sum(direction * result), ("bx", "by"))
        alpha = norm_now / curve
        surface_ext = surface_ext + alpha * direction_ext
        residual = residual - alpha * result
        norm_next = squares(residual)
        direction = residual + norm_next / norm_now * direction
        norm_now = norm_next
    surface = surface_ext[1:-1, 1:-1]
    east_flow = weights[0] * (surface_ext[0:-2, 1:-1] - surface)
    north_flow = weights[2] * (surface_ext[1:-1, 0:-2] - surface)
    return jnp.stack([surface, east_flow, north_flow])


def shards(tracers, mixing, thickness, levels, land):
    depth_count = tracers.shape[0]
    rows = tracers.shape[2]
    cols = tracers.shape[3]
    level_index = jnp.arange(depth_count, dtype=jnp.int32)
    lat_global = lax.axis_index("by") * cols - 3 + jnp.arange(cols + 6, dtype=jnp.int32)
    inside = jnp.logical_and(lat_global >= 0, lat_global < cols * lax.axis_size("by")).astype(
        jnp.float32
    )
    wet_cells = jnp.logical_and(
        (land == 0)[None], level_index[:, None, None] < levels[None]
    ).astype(jnp.float32)
    stacked = jnp.concatenate([tracers, wet_cells[:, None]], axis=1)
    extended = padded(stacked, (("bx", 2), ("by", 3)), 3)
    wet_ext = extended[:, 2] * inside[None, None, :]
    field_ext = extended[:, 0:2]
    first = laplace(field_ext, wet_ext[:, None])
    second = laplace(first, wet_ext[:, None, 1:-1, 1:-1])
    renewed = field_ext[:, :, 2:-2, 2:-2] - mixing[:, :, None, None] * second
    tracers_new = renewed[:, :, 1:-1, 1:-1]
    wet_cycle = wet_ext[:, 2:-2, 2:-2]
    layer = thickness[:, None, None]
    density = wet_cycle * (0.8 * renewed[:, 1] - 0.2 * renewed[:, 0])
    pressure = GRAVITY * jnp.cumsum(layer * density, axis=0)
    face_x = jnp.sum(
        layer
        * wet_cycle[:, 1:, 1:-1]
        * wet_cycle[:, :-1, 1:-1]
        * (pressure[:, 1:, 1:-1] - pressure[:, :-1, 1:-1]),
        axis=0,
    )
    face_y = jnp.sum(
        layer
        * wet_cycle[:, 1:-1, 1:]
        * wet_cycle[:, 1:-1, :-1]
        * (pressure[:, 1:-1, 1:] - pressure[:, 1:-1, :-1]),
        axis=0,
    )
    source = face_x[:-1] - face_x[1:] + face_y[:, :-1] - face_y[:, 1:]
    depth_cycle = jnp.sum(layer * wet_cycle, axis=0)
    centre = depth_cycle[1:-1, 1:-1]
    weights = [
        factor * jnp.minimum(centre, depth_cycle[1 + di : rows + 1 + di, 1 + dj : cols + 1 + dj])
        for di, dj, factor in OFFSETS
    ]
    coeffs = jnp.stack([source] + weights)
    moved = lax.all_to_all(coeffs, "by", split_axis=1, concat_axis=2, tiled=True)
    results = solve(moved[0], [moved[n + 1] for n in range(8)], strip_extend)
    back = lax.all_to_all(results, "by", split_axis=2, concat_axis=1, tiled=True)
    return (tracers_new, back[0], back[1:3])


def solution(mesh):
    in_specs = (P(None, None, "bx", "by"), P(), P(), P("bx", "by"), P("bx", "by"))
    out_specs = (P(None, None, "bx", "by"), P("bx", "by"), P(None, "bx", "by"))
    return jax.shard_map(shards, mesh=mesh, in_specs=in_specs, out_specs=out_specs, check_vma=False)
```

profile of v0, /device:TPU:1, one launch (start us, length us, event | category | flops | bytes accessed | tf_op | source)
XLA Modules:
  0.0 827.9 jit_solution(6364378944977695266)
XLA Ops:
  0.6 0.9 broadcast_compare_fusion
  1.6 1.5 fusion.35
  3.1 1.2 pad_maximum_fusion.4
  4.3 2.7 collective-permute-start
  7.0 2.0 collective-permute-done
  8.9 2.5 collective-permute-done.1
  11.4 3.2 pad_maximum_fusion.1
  14.6 7.6 fusion.82
  22.2 6.4 copy.26
  28.6 1.3 collective-permute-start.2
  29.9 7.1 copy.27
  37.0 4.9 collective-permute-start.3
  41.9 0.9 collective-permute-done.2
  42.9 6.0 copy.28
  49.4 6.0 copy.29
  55.4 18.6 %pad_maximum_fusion = f32[22,3,262,134]{3,2,0,1:T(8,128)S(1)} fusion(f32[22,3,262,3]{3,2,0,1:T(8,128)} %copy.29, f32[22,3,3,128]{3,2,0,1:T(4,128)S(1)} %collective-permute-done.1, f32[22,1,256,128]{3,2,0,1:T(8,128)S(1)} %fusion.35, f32[22,3,3,128]{3,2,0,1:T(4,128)S(1)} %collective-permute-done, f32[22,3,262,3]{3,2,0,1:T(8,128)} %copy.28, ...), kind=kLoop, calls=%fused_computation | loop fusion | flops 11585640 | bytes 18537024 | tf_op jit(solution)/shard_map/concatenate | solution.py:32
  74.1 3.3 slice_multiply_fusion.5
  77.3 4.6 copy-done
  81.9 3.0 bitcast_multiply_fusion
  85.0 23.7 %slice_bitcast_fusion.7 = (f32[22,260,132]{2,1,0:T(8,128)}, f32[22,260,132]{2,1,0:T(8,128)}, f32[22,260,132]{2,1,0:T(8,128)}, f32[22,260,132]{2,1,0:T(8,128)}, f32[22,260,132]{2,1,0:T(8,128)}) fusion(f32[22,1,262,134]{3,2,0,1:T(8,128)} %slice_multiply_fusion.5), kind=kLoop, calls=%fused_computation.42 | loop fusion | bytes 30201600 | tf_op jit(solution)/shard_map/mul | solution.py:42
  108.7 6.8 slice_bitcast_fusion.10
  115.6 23.7 %slice_bitcast_fusion.9 = (f32[22,258,130]{2,1,0:T(8,128)}, f32[22,258,130]{2,1,0:T(8,128)}, f32[22,258,130]{2,1,0:T(8,128)}, f32[22,258,130]{2,1,0:T(8,128)}, f32[22,258,130]{2,1,0:T(8,128)}) fusion(f32[22,1,260,132]{3,2,0,1:T(8,128)} %slice_bitcast_fusion.10), kind=kLoop, calls=%fused_computation.44 | loop fusion | bytes 29515200 | tf_op jit(solution)/shard_map/mul | solution.py:42
  139.2 35.5 %fusion.12 = f32[22,2,260,132]{3,2,0,1:T(8,128)} fusion(f32[22,3,262,134]{3,2,0,1:T(8,128)} %copy-done, f32[22,260,132]{2,1,0:T(8,128)} %get-tuple-element.35, f32[22,260,132]{2,1,0:T(8,128)} %get-tuple-element.36, f32[22,260,132]{2,1,0:T(8,128)} %get-tuple-element.37, f32[22,260,132]{2,1,0:T(8,128)} %get-tuple-element.38, f32[22,260,132]{2,1,0:T(8,128)} %get-tuple-element.34), kind=kLoop, calls=%fused_computation.18 | loop fusion | flops 18120960 | bytes 51342720 | tf_op jit(solution)/shard_map/mul | solution.py:42
  174.7 38.9 %fusion.4 = f32[22,2,258,130]{3,2,0,1:T(8,128)} fusion(f32[22,2,260,132]{3,2,0,1:T(8,128)} %fusion.12, f32[22,3,262,134]{3,2,0,1:T(8,128)} %copy-done, f32[22,258,130]{2,1,0:T(8,128)} %get-tuple-element.30, f32[22,258,130]{2,1,0:T(8,128)} %get-tuple-element.31, f32[22,258,130]{2,1,0:T(8,128)} %get-tuple-element.32, f32[22,258,130]{2,1,0:T(8,128)} %get-tuple-element.33, ...), kind=kLoop, calls=%fused_computation.6 | loop fusion | flops 20660640 | bytes 56079056 | tf_op jit(solution)/shard_map/sub | solution.py:99
  213.6 10.5 %broadcast_multiply_fusion = f32[22,258,130]{2,1,0:T(8,128)} fusion(f32[22,2,258,130]{3,2,0,1:T(8,128)} %fusion.4, f32[22,262,134]{2,1,0:T(8,128)} %bitcast_multiply_fusion, f32[22]{0:T(128)S(1)} %copy-done.1), kind=kOutput, calls=%fused_computation.60 | output fusion | flops 19922760 | bytes 11944152 | tf_op jit(solution)/shard_map/jit(cumsum)/reduce_window_sum | solution.py:104
  224.1 11.1 %fusion.28 = f32[257,128]{1,0:T(8,128)S(1)} fusion(f32[22,258,130]{2,1,0:T(8,128)} %broadcast_multiply_fusion, f32[22,262,134]{2,1,0:T(8,128)} %bitcast_multiply_fusion, f32[22]{0:T(128)S(1)} %copy-done.1), kind=kLoop, calls=%fused_computation.57 | loop fusion | flops 3585664 | bytes 11711064 | tf_op jit(solution)/shard_map/reduce_sum | solution.py:105
  235.2 13.5 %fusion.25 = f32[256,129]{1,0:T(8,128)S(1)} fusion(f32[22,258,130]{2,1,0:T(8,128)} %broadcast_multiply_fusion, f32[22,262,134]{2,1,0:T(8,128)} %bitcast_multiply_fusion, f32[22]{0:T(128)S(1)} %copy-done.1), kind=kLoop, calls=%fused_computation.50 | loop fusion | flops 3599616 | bytes 11756632 | tf_op jit(solution)/shard_map/reduce_sum | solution.py:112
  248.7 2.1 multiply_reduce_fusion
  251.2 1.9 stack.51
  253.1 34.0 %all_to_all.30 = f32[9,256,128]{2,0,1:T(8,128)S(1)} all-to-all(f32[9,256,128]{2,0,1:T(8,128)S(1)} %stack.51), channel_id=1, replica_groups=mesh['bx'=8,'by'=16] {'by'}, dimensions={1} | all-to-all | bytes 2359296 | tf_op jit(solution)/shard_map/all_to_all | solution.py:127
  287.9 4.8 collective-permute-start.5
  292.7 0.7 multiply_reduce_fusion.7
  294.1 1.1 multiply_reduce_fusion.6
  295.3 70.4 %all-reduce.4 = (f32[]{:T(128)}, f32[]{:T(128)}) all-reduce(f32[]{:T(128)} %get-tuple-element.39, f32[]{:T(128)} %get-tuple-element.23), channel_id=1, replica_groups=mesh['bx'=8,'by'=16] {'bx','by'}, use_global_device_ids=true, to_apply=%region_5.6 | all-reduce | flops 2 | bytes 16 | tf_op jit(solution)/shard_map/psum | solution.py:51
  367.0 0.6 multiply_reduce_fusion.5
  367.7 62.5 %psum.58 = f32[]{:T(128)} all-reduce(f32[]{:T(128)} %multiply_reduce_fusion.5), channel_id=1, replica_groups=mesh['bx'=8,'by'=16] {'bx','by'}, use_global_device_ids=true, to_apply=%region_9.10 | all-reduce | flops 1 | bytes 8 | tf_op jit(solution)/shard_map/psum | solution.py:51
  431.6 1.0 collective-permute-start.6
  432.6 4.3 collective-permute-start.7
  436.9 1.2 collective-permute-done.6
  438.3 1.1 multiply_reduce_fusion.4
  439.4 69.1 %psum.59 = f32[]{:T(128)} all-reduce(f32[]{:T(128)} %get-tuple-element.21), channel_id=1, replica_groups=mesh['bx'=8,'by'=16] {'bx','by'}, use_global_device_ids=true, to_apply=%region_11.12 | all-reduce | flops 1 | bytes 8 | tf_op jit(solution)/shard_map/psum | solution.py:68
  509.9 0.7 multiply_reduce_fusion.3
  510.5 62.5 %psum.60 = f32[]{:T(128)} all-reduce(f32[]{:T(128)} %get-tuple-element.19), channel_id=1, replica_groups=mesh['bx'=8,'by'=16] {'bx','by'}, use_global_device_ids=true, to_apply=%region_13.14 | all-reduce | flops 1 | bytes 8 | tf_op jit(solution)/shard_map/psum | solution.py:51
  574.4 1.0 collective-permute-start.8
  575.4 4.1 collective-permute-start.9
  579.6 1.3 collective-permute-done.8
  581.1 1.1 multiply_reduce_fusion.2
  582.2 68.9 %psum.61 = f32[]{:T(128)} all-reduce(f32[]{:T(128)} %get-tuple-element.17), channel_id=1, replica_groups=mesh['bx'=8,'by'=16] {'bx','by'}, use_global_device_ids=true, to_apply=%region_15.16 | all-reduce | flops 1 | bytes 8 | tf_op jit(solution)/shard_map/psum | solution.py:68
  653.1 62.5 %psum.62 = f32[]{:T(128)} all-reduce(f32[]{:T(128)} %multiply_reduce_fusion.1), channel_id=1, replica_groups=mesh['bx'=8,'by'=16] {'bx','by'}, use_global_device_ids=true, to_apply=%region_17.18 | all-reduce | flops 1 | bytes 8 | tf_op jit(solution)/shard_map/psum | solution.py:51
  717.1 1.0 collective-permute-start.10
  718.1 4.1 collective-permute-start.11
  722.2 1.3 collective-permute-done.10
  723.7 1.1 fusion.42
  724.8 68.9 %psum.63 = f32[]{:T(128)} all-reduce(f32[]{:T(128)} %fusion.42), channel_id=1, replica_groups=mesh['bx'=8,'by'=16] {'bx','by'}, use_global_device_ids=true, to_apply=%region_19.20 | all-reduce | flops 1 | bytes 8 | tf_op jit(solution)/shard_map/psum | solution.py:68
  795.8 3.0 copy.47
  798.8 5.1 reshape.58
  803.9 4.1 all-to-all-start.1
  808.1 6.0 slice.508
  814.0 2.9 copy.51
  817.8 1.6 reduce.1
  819.3 4.2 reshape.59
  823.5 2.7 copy.52
  826.2 0.8 copy.50
  827.0 0.7 copy.49
  (56 shorter events, 5.1 us)
Async XLA Ops:
  1.6 9.8 %slice-start.2 = ((s8[5767168]{0:T(1024)(128)(4,1)}), s8[4194304]{0:T(1024)(128)(4,1)S(1)}, s32[]{:S(2)}) async-start(s8[5767168]{0:T(1024)(128)(4,1)} %bitcast.387), calls=%async_computation.4 | async-start | bytes 8388608
  3.1 8.3 %slice-start.3 = ((s8[5767168]{0:T(1024)(128)(4,1)}), s8[1572864]{0:T(1024)(128)(4,1)S(1)}, s32[]{:S(2)}) async-start(s8[5767168]{0:T(1024)(128)(4,1)} %bitcast.387), calls=%async_computation.5 | async-start | bytes 3145728
  4.3 4.7 collective-permute-start
  7.0 4.4 collective-permute-start.1
  28.6 14.2 %collective-permute-start.2 = (f32[22,3,262,3]{2,0,3,1:T(8,128)S(1)}, f32[22,3,262,3]{2,0,3,1:T(8,128)}, u32[]{:S(2)}, u32[]{:S(2)}) collective-permute-start(f32[22,3,262,3]{2,0,3,1:T(8,128)S(1)} %copy.26), channel_id=1, source_target_pairs={{0,1},{1,2},{2,3},{3,4},{4,5},{5,6},{6,7},{7,8},{8,9},{9,10},{10,1... | collective-permute-start | bytes 622520 | tf_op jit(solution)/shard_map/ppermute | solution.py:28
  37.0 12.4 %collective-permute-start.3 = (f32[22,3,262,3]{2,0,3,1:T(8,128)}, f32[22,3,262,3]{2,0,3,1:T(8,128)}, u32[]{:S(2)}, u32[]{:S(2)}) collective-permute-start(f32[22,3,262,3]{2,0,3,1:T(8,128)} %copy.27), channel_id=1, source_target_pairs={{1,0},{2,1},{3,2},{4,3},{5,4},{6,5},{7,6},{8,7},{9,8},{10,9},{11,1... | collective-permute-start | bytes 622520 | tf_op jit(solution)/shard_map/ppermute | solution.py:31
  74.0 7.9 copy-start
  139.2 35.5 %copy-start.2 = (f32[22,2]{0,1:T(2,128)S(1)}, f32[22,2]{0,1:T(2,128)}, u32[]{:S(2)}) copy-start(f32[22,2]{0,1:T(2,128)} %param.6) | copy-start | bytes 532
  174.7 38.9 %copy-start.1 = (f32[22]{0:T(128)S(1)}, f32[22]{0:T(128)}, u32[]{:S(2)}) copy-start(f32[22]{0:T(128)} %param.7) | copy-start | bytes 268
  224.1 24.6 %slice-start = ((s8[5947392]{0:T(1024)(128)(4,1)}), s8[1753088]{0:T(1024)(128)(4,1)S(1)}, s32[]{:S(2)}) async-start(s8[5947392]{0:T(1024)(128)(4,1)} %bitcast.385), calls=%async_computation.2 | async-start | bytes 3506176
  235.2 13.5 %slice-start.1 = ((s8[5947392]{0:T(1024)(128)(4,1)}), s8[4194304]{0:T(1024)(128)(4,1)S(1)}, s32[]{:S(2)}) async-start(s8[5947392]{0:T(1024)(128)(4,1)} %bitcast.385), calls=%async_computation.3 | async-start | bytes 8388608
  287.5 6.5 collective-permute-start.4
  287.9 6.1 collective-permute-start.5
  431.6 6.5 collective-permute-start.6
  432.6 5.5 collective-permute-start.7
  574.4 6.5 collective-permute-start.8
  575.4 5.5 collective-permute-start.9
  717.1 6.5 collective-permute-start.10
  718.1 5.5 collective-permute-start.11
  803.9 13.3 %all-to-all-start.1 = ((f32[16,1,6144]{2,1,0:T(1,128)}), f32[16,1,6144]{2,1,0:T(1,128)S(1)}, u32[]{:S(2)}, u32[]{:S(2)}) async-start(f32[16,1,6144]{2,1,0:T(1,128)} %reshape.58), calls=%async_computation.1 | async-start | bytes 786432 | tf_op jit(solution)/shard_map/all_to_all | solution.py:129
where the time goes:
time: 834 us; the launch traced here: 828 us
  blocking collectives  499 us (60%)
  other arithmetic  154 us (18%)
  local copies, waits for them, and re-layouts  121 us (15%)
  starting transfers between devices  33.7 us (4%)
  between operations  10.6 us (1%)
  waiting for transfers between devices  10.1 us (1%)
    psum x4, blocking collectives, squares(): return lax.psum(jnp.sum(residual * residual), ('bx', 'by'))  258 us
    psum x3, blocking collectives, solve(): curve = lax.psum(jnp.sum(direction * result), ('bx', 'by'))  207 us
    mul x2, local copies, waits for them, and re-layouts, laplace(): return wet[..., 1:-1, 1:-1] * total  47.4 us
    sub x1, other arithmetic, shards(): renewed = field_ext[:, :, 2:-2, 2:-2] - mixing[:, :, None, None] * second  38.9 us
    mul x1, other arithmetic, laplace(): return wet[..., 1:-1, 1:-1] * total  35.5 us
    all_to_all x1, blocking collectives, shards(): lax.all_to_all(coeffs, 'by', split_axis=1, concat_axis=2, tiled=True)  34 us
    concatenate x6, other arithmetic, padded(): block = jnp.concatenate([low, block, high], axis=dim)  22.5 us
    ppermute x6, starting transfers between devices, padded(): lax.ppermute(lax.slice_in_dim(block, 0, width, axis=dim), axis, backward)  22.3 us
  transfers between devices with their start and end apart: 13, of which 9 were waited for; matrix products, arithmetic and copies ran while one was open for 3% of the time, Pallas kernels for 0%

commit v1 on v0

v1 whole, which is shorter than its diff:
```python
import functools

import jax
import jax.numpy as jnp
from jax import lax
from jax.experimental import pallas as pl
from jax.experimental.pallas import tpu as pltpu
from jax.sharding import PartitionSpec as P

KL = 22
ROWS = 256
LANES = 128
HALO = 8
EXT = ROWS + 2 * HALO
PAD = 8
BUF = EXT + 2 * PAD
GROUP = 16
TILES = 3
HALF_STEPS = 2
MOMENTS = 8
F32 = jnp.float32
I32 = jnp.int32
VMEM_LIMIT = 48 * 1024 * 1024


def lane_iota(rows):
    return lax.broadcasted_iota(I32, (rows, LANES), 1)


def roll(x, shift):
    return pltpu.roll(x, shift % LANES, 1)


def blocks(start, stop, size):
    out = []
    while start < stop:
        out.append((start, min(size, stop - start)))
        start += size
    return out


CHUNKS = [(0, HALO)] + blocks(HALO, HALO + ROWS, 32) + [(HALO + ROWS, HALO)]


def ext_rows(ref, top_ref, bottom_ref, place, plane, r0, n):
    if r0 < HALO:
        return top_ref[plane]
    if r0 >= HALO + ROWS:
        return bottom_ref[plane]
    return ref[place + (pl.ds(r0 - HALO, n),)]


def wet_levels(levels, land):
    return jnp.where(land == 0, levels, 0)


def pack_kernel(t_ref, top_ref, bottom_ref, levels_ref, land_ref, right_ref, left_ref):
    for r0, n in CHUNKS:
        lane = lane_iota(n)
        group = lane // GROUP
        first = (lane & 8) == 0
        for tile in range(TILES):
            to_right = jnp.zeros((n, LANES), F32)
            to_left = jnp.zeros((n, LANES), F32)
            for g in range(LANES // GROUP):
                k = tile * (LANES // GROUP) + g
                if k < KL:
                    a = ext_rows(t_ref, top_ref, bottom_ref, (k, 0), 2 * k, r0, n)
                    b = ext_rows(t_ref, top_ref, bottom_ref, (k, 1), 2 * k + 1, r0, n)
                elif k == KL:
                    if r0 < HALO:
                        a = top_ref[2 * KL]
                    elif r0 >= HALO + ROWS:
                        a = bottom_ref[2 * KL]
                    else:
                        own = pl.ds(r0 - HALO, n)
                        a = wet_levels(levels_ref[own], land_ref[own]).astype(F32)
                    b = a
                else:
                    continue
                here = group == g
                pair_right = jnp.where(first, roll(a, 8 + GROUP * g), roll(b, GROUP + GROUP * g))
                pair_left = jnp.where(first, roll(a, GROUP * g), roll(b, 8 + GROUP * g))
                to_right = jnp.where(here, pair_right, to_right)
                to_left = jnp.where(here, pair_left, to_left)
            right_ref[tile, pl.ds(r0, n)] = to_right
            left_ref[tile, pl.ds(r0, n)] = to_left


def count_word(effs, word):
    total = None
    for eff in effs:
        bits = jnp.clip(eff - 10 * word, 0, 10) * 3
        mask = (lax.shift_left(jnp.full_like(bits, 1), bits) - 1) & 0o1111111111
        total = mask if total is None else total + mask
    return total


def wet_setup(eff_ref, min_ref, word_ref, top_ref, bottom_ref, levels_ref, land_ref):
    eff_ref[...] = jnp.zeros(eff_ref.shape, I32)
    eff_ref[pl.ds(PAD, HALO)] = top_ref[2 * KL].astype(I32)
    eff_ref[pl.ds(PAD + HALO, ROWS)] = wet_levels(levels_ref[...], land_ref[...])
    eff_ref[pl.ds(PAD + HALO + ROWS, HALO)] = bottom_ref[2 * KL].astype(I32)
    for r0, n in CHUNKS:
        e = eff_ref[pl.ds(PAD + r0, n)]
        up = eff_ref[pl.ds(PAD + r0 - 1, n)]
        down = eff_ref[pl.ds(PAD + r0 + 1, n)]
        west = roll(e, 1)
        east = roll(e, -1)
        if min_ref is not None:
            min_ref[0, pl.ds(r0, n)] = jnp.minimum(e, up)
            min_ref[1, pl.ds(r0, n)] = jnp.minimum(e, west)
        for word in range(3):
            word_ref[word, pl.ds(r0, n)] = count_word((up, down, west, east), word)


def wet_count(word_ref, k, r0, n):
    words = word_ref[k // 10, pl.ds(r0, n)]
    shift = jnp.full((n, LANES), 3 * (k % 10), I32)
    return (lax.shift_right_logical(words, shift) & 7).astype(F32)


def neighbours(ref, r0, n):
    x = ref[pl.ds(PAD + r0, n)]
    around = ref[pl.ds(PAD + r0 - 1, n)] + ref[pl.ds(PAD + r0 + 1, n)]
    return x, around + (roll(x, 1) + roll(x, -1))


def density_kernel(
    mixing_ref,
    thick_ref,
    t_ref,
    top_ref,
    bottom_ref,
    levels_ref,
    land_ref,
    fx_ref,
    fy_ref,
    eff_ref,
    min_ref,
    word_ref,
    u_ref,
    l_ref,
    acc_ref,
):
    part = pl.program_id(0)

    @pl.when(part == 0)
    def _():
        wet_setup(eff_ref, min_ref, word_ref, top_ref, bottom_ref, levels_ref, land_ref)
        u_ref[...] = jnp.zeros(u_ref.shape, F32)
        l_ref[...] = jnp.zeros(l_ref.shape, F32)
        acc_ref[...] = jnp.zeros(acc_ref.shape, F32)
        fx_ref[...] = jnp.zeros(fx_ref.shape, F32)
        fy_ref[...] = jnp.zeros(fy_ref.shape, F32)

    def level(step, carry):
        k = part * (KL // HALF_STEPS) + step
        m0 = 0.2 * mixing_ref[k, 0]
        m1 = 0.8 * mixing_ref[k, 1]
        thick = thick_ref[k]
        for r0, n in CHUNKS:
            a = ext_rows(t_ref, top_ref, bottom_ref, (step, 0), 2 * k, r0, n)
            b = ext_rows(t_ref, top_ref, bottom_ref, (step, 1), 2 * k + 1, r0, n)
            wet = eff_ref[pl.ds(PAD + r0, n)] > k
            u_ref[pl.ds(PAD + r0, n)] = jnp.where(wet, m1 * b - m0 * a, 0.0)
        for r0, n in CHUNKS:
            wet = eff_ref[pl.ds(PAD + r0, n)] > k
            x, around = neighbours(u_ref, r0, n)
            l_ref[pl.ds(PAD + r0, n)] = jnp.where(wet, around, 0.0) - wet_count(word_ref, k, r0, n) * x
        for r0, n in CHUNKS:
            a = ext_rows(t_ref, top_ref, bottom_ref, (step, 0), 2 * k, r0, n)
            b = ext_rows(t_ref, top_ref, bottom_ref, (step, 1), 2 * k + 1, r0, n)
            wet = eff_ref[pl.ds(PAD + r0, n)] > k
            x, around = neighbours(l_ref, r0, n)
            plain = 0.8 * b - 0.2 * a
            density = jnp.where(wet, plain - around, 0.0) + wet_count(word_ref, k, r0, n) * x
            acc_ref[pl.ds(PAD + r0, n)] += thick * density
        for r0, n in CHUNKS:
            here = acc_ref[pl.ds(PAD + r0, n)]
            up = acc_ref[pl.ds(PAD + r0 - 1, n)]
            face_x = min_ref[0, pl.ds(r0, n)] > k
            face_y = min_ref[1, pl.ds(r0, n)] > k
            fx_ref[pl.ds(r0, n)] += thick * jnp.where(face_x, here - up, 0.0)
            fy_ref[pl.ds(r0, n)] += thick * jnp.where(face_y, here - roll(here, 1), 0.0)
        return carry

    lax.fori_loop(0, KL // HALF_STEPS, level, 0)


def two_sum(a, b):
    s = a + b
    v = s - a
    return s, (a - (s - v)) + (b - v)


def quick_sum(a, b):
    s = a + b
    return s, b - (s - a)


def split(a):
    t = a * 4097.0
    high = t - (t - a)
    return high, a - high


def two_prod(a, b, parts_a, parts_b):
    p = a * b
    ah, al = parts_a
    bh, bl = parts_b
    return p, ((ah * bh - p) + ah * bl + al * bh) + al * bl


def pair_add(x, y):
    s, e = two_sum(x[0], y[0])
    return quick_sum(s, e + (x[1] + y[1]))


def pair_mul(x, y):
    p, e = two_prod(x[0], y[0], split(x[0]), split(y[0]))
    return quick_sum(p, e + (x[0] * y[1] + x[1] * y[0]))


def pair_neg(x):
    return -x[0], -x[1]


def pair_div(x, y):
    q = x[0] / y[0]
    rest = pair_add(x, pair_neg(pair_mul(y, (q, jnp.zeros_like(q)))))
    return quick_sum(q, rest[0] / y[0])


def pair_clip(x, top):
    inside = jnp.logical_and(x[0] >= 0.0, x[0] <= top)
    high = jnp.where(inside, x[0], jnp.where(x[0] > top, top, 0.0))
    return high, jnp.where(inside, x[1], 0.0)


def group_totals(x):
    x = x + roll(x, GROUP)
    x = x + roll(x, 2 * GROUP)
    return x + roll(x, 4 * GROUP)


def strip_side(
    side,
    near_ref,
    far_ref,
    keep,
    mixing_ref,
    thick_ref,
    eff_ref,
    min_ref,
    u_ref,
    l_ref,
    acc_ref,
    carry_ref,
    fx_ref,
    fy_ref,
):
    chunks = blocks(0, EXT, 32)

    def field(tile, which, r0, n):
        first = (lane_iota(n) & 8) == 0
        near = near_ref[tile, pl.ds(r0, n)]
        far = far_ref[tile, pl.ds(r0, n)]
        if side == 0:
            low, high = far, near
        else:
            low, high = near, far
        if which == 0:
            return jnp.where(first, low, roll(high, 8))
        return jnp.where(first, roll(low, -8), high)

    for r0, n in chunks:
        lane = lane_iota(n)
        slot = KL - 2 * (LANES // GROUP)
        x = field(2, 0, r0, n)
        outer = (lane & 8) == (0 if side == 0 else 8)
        x = jnp.where(jnp.logical_and(lane // GROUP == slot, jnp.logical_or(jnp.logical_not(outer), keep)), x, 0.0)
        eff_ref[pl.ds(PAD + r0, n)] = group_totals(x).astype(I32)
    for r0, n in chunks:
        e = eff_ref[pl.ds(PAD + r0, n)]
        min_ref[0, pl.ds(r0, n)] = jnp.minimum(e, eff_ref[pl.ds(PAD + r0 - 1, n)])
        min_ref[1, pl.ds(r0, n)] = jnp.minimum(e, roll(e, 1))
    for tile in range(TILES):
        group8 = lane_iota(8) // GROUP
        m0 = jnp.zeros((8, LANES), F32)
        m1 = m0
        thick8 = m0
        for g in range(LANES // GROUP):
            k = tile * (LANES // GROUP) + g
            if k < KL:
                m0 = jnp.where(group8 == g, 0.2 * mixing_ref[k, 0], m0)
                m1 = jnp.where(group8 == g, 0.8 * mixing_ref[k, 1], m1)
                thick8 = jnp.where(group8 == g, thick_ref[k], thick8)
        m0, m1, thick8 = m0[0:1], m1[0:1], thick8[0:1]
        level_of = group8[0:1] + tile * (LANES // GROUP)

        for r0, n in chunks:
            wet = eff_ref[pl.ds(PAD + r0, n)] > level_of
            u_ref[pl.ds(PAD + r0, n)] = jnp.where(
                wet, m1 * field(tile, 1, r0, n) - m0 * field(tile, 0, r0, n), 0.0
            )

        def count(r0, n):
            e = eff_ref[pl.ds(PAD + r0, n)]
            total = jnp.where(eff_ref[pl.ds(PAD + r0 - 1, n)] > level_of, 1.0, 0.0)
            total += jnp.where(eff_ref[pl.ds(PAD + r0 + 1, n)] > level_of, 1.0, 0.0)
            total += jnp.where(roll(e, 1) > level_of, 1.0, 0.0)
            return total + jnp.where(roll(e, -1) > level_of, 1.0, 0.0)

        for r0, n in chunks:
            wet = eff_ref[pl.ds(PAD + r0, n)] > level_of
            x, around = neighbours(u_ref, r0, n)
            l_ref[pl.ds(PAD + r0, n)] = jnp.where(wet, around, 0.0) - count(r0, n) * x
        for r0, n in chunks:
            lane = lane_iota(n)
            wet = eff_ref[pl.ds(PAD + r0, n)] > level_of
            x, around = neighbours(l_ref, r0, n)
            plain = 0.8 * field(tile, 1, r0, n) - 0.2 * field(tile, 0, r0, n)
            density = jnp.where(wet, plain - around, 0.0) + count(r0, n) * x
            layer = thick8 * density
            run = layer
            for step in (1, 2, 4):
                run = run + jnp.where(lane >= step * GROUP, roll(run, step * GROUP), 0.0)
            if tile > 0:
                run = run + carry_ref[pl.ds(r0, n)]
            acc_ref[pl.ds(PAD + r0, n)] = run
            if tile == 0:
                carry_ref[pl.ds(r0, n)] = group_totals(layer)
            elif tile < TILES - 1:
                carry_ref[pl.ds(r0, n)] += group_totals(layer)
        for r0, n in chunks:
            here = acc_ref[pl.ds(PAD + r0, n)]
            up = acc_ref[pl.ds(PAD + r0 - 1, n)]
            face_x = thick8 * jnp.where(min_ref[0, pl.ds(r0, n)] > level_of, here - up, 0.0)
            face_y = thick8 * jnp.where(min_ref[1, pl.ds(r0, n)] > level_of, here - roll(here, 1), 0.0)
            if tile > 0:
                face_x += fx_ref[side, pl.ds(r0, n)]
                face_y += fy_ref[side, pl.ds(r0, n)]
            if tile == TILES - 1:
                face_x = roll(group_totals(face_x), 8)
                face_y = roll(group_totals(face_y), 8)
            fx_ref[side, pl.ds(r0, n)] = face_x
            fy_ref[side, pl.ds(r0, n)] = face_y


def lane_left(main, side):
    lane = lane_iota(main.shape[0])
    a, b = roll(main, 1), roll(side, 1)
    return jnp.where(lane == 0, b, a), jnp.where(lane == 0, a, b)


def lane_right(main, side):
    lane = lane_iota(main.shape[0])
    a, b = roll(main, -1), roll(side, -1)
    return jnp.where(lane == LANES - 1, b, a), jnp.where(lane == LANES - 1, a, b)


def solve_kernel(
    mixing_ref,
    thick_ref,
    fx_ref,
    fy_ref,
    from_left_ref,
    from_right_ref,
    to_right_ref,
    to_left_ref,
    top_ref,
    bottom_ref,
    levels_ref,
    land_ref,
    v_ref,
    d_ref,
    sums_ref,
    eff_ref,
    min_ref,
    u_ref,
    l_ref,
    acc_ref,
    carry_ref,
    sfx_ref,
    sfy_ref,
    full_fx_ref,
    full_fy_ref,
    dl_ref,
    dr_ref,
    w_ref,
    p_ref,
    q_ref,
):
    chunks = blocks(0, EXT, 32)
    by = lax.axis_index("by")
    last = lax.axis_size("by") - 1
    for ref in (eff_ref, u_ref, l_ref, acc_ref, d_ref, v_ref, dl_ref, dr_ref, p_ref, q_ref, full_fx_ref):
        ref[...] = jnp.zeros(ref.shape, ref.dtype)

    common = (mixing_ref, thick_ref)
    rest = (min_ref, u_ref, l_ref, acc_ref, carry_ref, sfx_ref, sfy_ref)
    strip_side(0, to_left_ref, from_left_ref, by != 0, *common, eff_ref.at[0], *rest)
    strip_side(1, to_right_ref, from_right_ref, by != last, *common, eff_ref.at[1], *rest)

    for r0, n in chunks:
        lane = lane_iota(n)
        own = pl.ds(r0, n)
        for full, main, strip in ((full_fx_ref, fx_ref, sfx_ref), (full_fy_ref, fy_ref, sfy_ref)):
            west, east = strip[0, own], strip[1, own]
            full[0, pl.ds(PAD + r0, n)] = jnp.where(
                lane < 4, west, jnp.where(lane >= LANES - 4, east, main[own])
            )
            full[1, pl.ds(PAD + r0, n)] = jnp.where(
                lane < 8, east, jnp.where(lane >= LANES - 8, west, 0.0)
            )
    for r0, n in CHUNKS:
        lane = lane_iota(n)
        if r0 < HALO:
            e_main = top_ref[2 * KL].astype(I32)
        elif r0 >= HALO + ROWS:
            e_main = bottom_ref[2 * KL].astype(I32)
        else:
            own = pl.ds(r0 - HALO, n)
            e_main = wet_levels(levels_ref[own], land_ref[own])
        west = roll(eff_ref[0, pl.ds(PAD + r0, n)], 8)
        east = roll(eff_ref[1, pl.ds(PAD + r0, n)], 8)
        e_side = jnp.where(lane < 8, east, jnp.where(lane >= LANES - 8, west, 0))
        d_main = jnp.zeros((n, LANES), F32)
        d_side = d_main
        for k in range(KL):
            thick = thick_ref[k]
            d_main += jnp.where(e_main > k, thick, 0.0)
            d_side += jnp.where(e_side > k, thick, 0.0)
        here = pl.ds(PAD + r0, n)
        d_ref[0, here], d_ref[1, here] = d_main, d_side
        dl_ref[0, here], dl_ref[1, here] = lane_left(d_main, d_side)
        dr_ref[0, here], dr_ref[1, here] = lane_right(d_main, d_side)

    for r0, n in chunks:
        here = pl.ds(PAD + r0, n)
        above = pl.ds(PAD + r0 - 1, n)
        below = pl.ds(PAD + r0 + 1, n)
        east = lane_right(full_fy_ref[0, here], full_fy_ref[1, here])
        for t in range(2):
            fx = full_fx_ref[t, here] - full_fx_ref[t, below]
            fy = full_fy_ref[t, here] - east[t]
            v_ref[0, t, here] = 10.0 * (fx + fy)
            d = d_ref[t, here]
            left, right = dl_ref[t, here], dr_ref[t, here]
            up, down = d_ref[t, above], d_ref[t, below]
            w_west, w_east = jnp.minimum(d, left), jnp.minimum(d, right)
            w_up, w_down = jnp.minimum(d, up), jnp.minimum(d, down)
            corners = (
                jnp.minimum(d, dl_ref[t, above])
                + jnp.minimum(d, dr_ref[t, below])
                + jnp.minimum(d, dr_ref[t, above])
                + jnp.minimum(d, dl_ref[t, below])
            )
            at = pl.ds(r0, n)
            w_ref[0, t, at] = 0.05 + w_up + w_down + w_west + w_east + 0.25 * corners
            w_ref[1, t, at] = w_west
            w_ref[2, t, at] = w_east
            w_ref[3, t, at] = w_down
            w_ref[4, t, at] = 0.25 * jnp.minimum(down, left)
            w_ref[5, t, at] = 0.25 * jnp.minimum(down, right)
            w_ref[6, t, at] = w_up
            w_ref[7, t, at] = 0.25 * jnp.minimum(up, left)
            w_ref[8, t, at] = 0.25 * jnp.minimum(up, right)

    def power(step, carry):
        for r0, n in chunks:
            here = pl.ds(PAD + r0, n)
            at = pl.ds(r0, n)
            v = (v_ref[step, 0, here], v_ref[step, 1, here])
            left = lane_left(*v)
            right = lane_right(*v)
            for t in range(2):
                w = [w_ref[m, t, at] for m in range(9)]
                p_ref[t, here] = w[3] * v[t] + w[4] * left[t] + w[5] * right[t]
                q_ref[t, here] = w[6] * v[t] + w[7] * left[t] + w[8] * right[t]
                v_ref[step + 1, t, here] = w[0] * v[t] - (w[1] * left[t] + w[2] * right[t])
        for r0, n in chunks:
            here = pl.ds(PAD + r0, n)
            for t in range(2):
                beside = p_ref[t, pl.ds(PAD + r0 - 1, n)] + q_ref[t, pl.ds(PAD + r0 + 1, n)]
                v_ref[step + 1, t, here] -= beside
        return carry

    lax.fori_loop(0, 4, power, 0)

    def dots(step, carry):
        at = pl.ds(pl.multiple_of(PAD + HALO + 8 * step, 8), 8)
        v = [v_ref[i, 0, at] for i in range(5)]
        parts = [split(x) for x in v]
        out = []
        for m in range(MOMENTS):
            i, j = m // 2, (m + 1) // 2
            p, e = two_prod(v[i], v[j], parts[i], parts[j])
            s, f = two_sum(carry[2 * m], p)
            out += [s, carry[2 * m + 1] + (e + f)]
        return tuple(out)

    zero = jnp.zeros((8, LANES), F32)
    sums = lax.fori_loop(0, ROWS // 8, dots, (zero,) * (2 * MOMENTS))
    sub = lax.broadcasted_iota(I32, (8, LANES), 0)
    pairs = [(sums[2 * m], sums[2 * m + 1]) for m in range(MOMENTS)]
    for half in (4, 2, 1):
        merged = []
        for m in range(half):
            a, b = pairs[m], pairs[m + half]
            upper = (sub & half) == 0
            keep = tuple(jnp.where(upper, x, y) for x, y in zip(a, b))
            other = tuple(jnp.where(upper, pltpu.roll(x, 8 - half, 0), pltpu.roll(y, half, 0)) for x, y in zip(a, b))
            merged.append(pair_add(keep, other))
        pairs = merged
    total = pairs[0]
    for shift in (1, 2, 4, 8, 16, 32, 64):
        total = pair_add(total, tuple(roll(x, shift) for x in total))
    lane = lane_iota(8)
    row = jnp.where(lane == sub, total[0], jnp.where(lane == sub + MOMENTS, total[1], 0.0))
    for shift in (4, 2, 1):
        row = row + pltpu.roll(row, shift, 0)
    for at in range(0, sums_ref.shape[0], 8):
        sums_ref[pl.ds(at, 8)] = row


def tracer_kernel(
    mixing_ref,
    t_ref,
    top_ref,
    bottom_ref,
    levels_ref,
    land_ref,
    from_left_ref,
    from_right_ref,
    to_right_ref,
    to_left_ref,
    out_ref,
    eff_ref,
    word_ref,
    u_ref,
    l_ref,
    edge_ref,
    seff_ref,
    su_ref,
    sl_ref,
):
    part = pl.program_id(0)
    by = lax.axis_index("by")
    last = lax.axis_size("by") - 1
    own_chunks = blocks(HALO, HALO + ROWS, 32)

    @pl.when(part == 0)
    def _():
        wet_setup(eff_ref, None, word_ref, top_ref, bottom_ref, levels_ref, land_ref)
        for ref in (u_ref, l_ref, seff_ref, su_ref, sl_ref):
            ref[...] = jnp.zeros(ref.shape, ref.dtype)
        chunks = blocks(0, EXT, 32)
        slot = KL - 2 * (LANES // GROUP)
        for side in range(2):
            near_ref, far_ref = (to_left_ref, from_left_ref) if side == 0 else (to_right_ref, from_right_ref)
            keep = (by != 0) if side == 0 else (by != last)

            def field(tile, which, r0, n):
                first = (lane_iota(n) & 8) == 0
                near = near_ref[tile, pl.ds(r0, n)]
                far = far_ref[tile, pl.ds(r0, n)]
                low, high = (far, near) if side == 0 else (near, far)
                if which == 0:
                    return jnp.where(first, low, roll(high, 8))
                return jnp.where(first, roll(low, -8), high)

            for r0, n in chunks:
                lane = lane_iota(n)
                x = field(2, 0, r0, n)
                inner = (lane & 8) == (8 if side == 0 else 0)
                x = jnp.where(jnp.logical_and(lane // GROUP == slot, jnp.logical_or(inner, keep)), x, 0.0)
                seff_ref[pl.ds(PAD + r0, n)] = group_totals(x).astype(I32)
            for tile in range(TILES):
                group8 = lane_iota(8) // GROUP
                level_of = group8[0:1] + tile * (LANES // GROUP)
                mix = []
                for c in range(2):
                    m = jnp.zeros((8, LANES), F32)
                    for g in range(LANES // GROUP):
                        k = tile * (LANES // GROUP) + g
                        if k < KL:
                            m = jnp.where(group8 == g, mixing_ref[k, c], m)
                    mix.append(m[0:1])

                def count(r0, n):
                    e = seff_ref[pl.ds(PAD + r0, n)]
                    total = jnp.where(seff_ref[pl.ds(PAD + r0 - 1, n)] > level_of, 1.0, 0.0)
                    total += jnp.where(seff_ref[pl.ds(PAD + r0 + 1, n)] > level_of, 1.0, 0.0)
                    total += jnp.where(roll(e, 1) > level_of, 1.0, 0.0)
                    return total + jnp.where(roll(e, -1) > level_of, 1.0, 0.0)

                for c in range(2):
                    for r0, n in chunks:
                        wet = seff_ref[pl.ds(PAD + r0, n)] > level_of
                        su_ref[pl.ds(PAD + r0, n)] = jnp.where(wet, field(tile, c, r0, n), 0.0)
                    for r0, n in chunks:
                        wet = seff_ref[pl.ds(PAD + r0, n)] > level_of
                        x, around = neighbours(su_ref, r0, n)
                        sl_ref[pl.ds(PAD + r0, n)] = jnp.where(wet, around, 0.0) - count(r0, n) * x
                    for r0, n in own_chunks:
                        first = (lane_iota(n) & 8) == 0
                        wet = seff_ref[pl.ds(PAD + r0, n)] > level_of
                        x, around = neighbours(sl_ref, r0, n)
                        second = jnp.where(wet, around, 0.0) - count(r0, n) * x
                        new = field(tile, c, r0, n) - mix[c] * second
                        own = pl.ds(r0 - HALO, n)
                        if side == 0:
                            edge_ref[c, tile, own] = new
                        else:
                            edge_ref[c, tile, own] = jnp.where(first, new, edge_ref[c, tile, own])

    def level(step, carry):
        k = part * (KL // HALF_STEPS) + step
        tile = k // (LANES // GROUP)
        back = (2 * LANES - 8 - GROUP * (k % (LANES // GROUP))) % LANES
        for r0, n in CHUNKS:
            wet = eff_ref[pl.ds(PAD + r0, n)] > k
            for c in range(2):
                a = ext_rows(t_ref, top_ref, bottom_ref, (step, c), 2 * k + c, r0, n)
                u_ref[c, pl.ds(PAD + r0, n)] = jnp.where(wet, a, 0.0)
        for r0, n in CHUNKS:
            wet = eff_ref[pl.ds(PAD + r0, n)] > k
            number = wet_count(word_ref, k, r0, n)
            for c in range(2):
                x, around = neighbours(u_ref.at[c], r0, n)
                l_ref[c, pl.ds(PAD + r0, n)] = jnp.where(wet, around, 0.0) - number * x
        for r0, n in own_chunks:
            lane = lane_iota(n)
            middle = jnp.logical_and(lane >= 4, lane < LANES - 4)
            wet = eff_ref[pl.ds(PAD + r0, n)] > k
            number = wet_count(word_ref, k, r0, n)
            own = pl.ds(r0 - HALO, n)
            for c in range(2):
                x, around = neighbours(l_ref.at[c], r0, n)
                second = jnp.where(wet, around, 0.0) - number * x
                new = t_ref[step, c, own] - mixing_ref[k, c] * second
                edge = pltpu.roll(edge_ref[c, tile, own], back, 1)
                out_ref[step, c, own] = jnp.where(middle, new, edge)
        return carry

    lax.fori_loop(0, KL // HALF_STEPS, level, 0)


def finish_kernel(all_ref, v_ref, d_ref, surface_ref, flow_ref, s_ref):
    zero = jnp.zeros((8, LANES), F32)
    high, low = zero, zero
    for at in range(0, all_ref.shape[0], 8):
        high, e = two_sum(high, all_ref[pl.ds(at, 8)])
        low = low + e
    total = (high, low)
    for shift in (4, 2, 1):
        total = pair_add(total, tuple(pltpu.roll(x, shift, 0) for x in total))
    total = pair_add(total, tuple(roll(x, -MOMENTS) for x in total))
    lane = lane_iota(8)

    def moment(m):
        return tuple(
            jnp.broadcast_to(jnp.sum(jnp.where(lane == m, x, 0.0), axis=1, keepdims=True), (8, LANES))
            for x in total
        )

    rho = [moment(m) for m in range(MOMENTS)]
    pi = list(rho)
    nought = (zero, zero)
    one = (zero + 1.0, zero)
    surface = [nought] * 4
    residual = [one] + [nought] * 3
    direction = list(residual)
    for step in range(4):
        alpha = pair_clip(pair_div(rho[step], pi[step + 1]), 20.0)
        for i in range(step + 1):
            surface[i] = pair_add(surface[i], pair_mul(alpha, direction[i]))
        if step == 3:
            break
        minus = pair_neg(alpha)
        new_rho = list(rho)
        for m in range(step + 1, MOMENTS - 1 - step):
            new_rho[m] = pair_add(rho[m], pair_mul(minus, pi[m + 1]))
        beta = pair_clip(pair_div(pair_mul(minus, new_rho[step + 1]), rho[step]), 400.0)
        for m in range(step + 2, MOMENTS - 1 - step):
            pi[m] = pair_add(new_rho[m], pair_mul(beta, pi[m]))
        rho = new_rho
        for i in range(step + 1, 0, -1):
            residual[i] = pair_add(residual[i], pair_mul(minus, direction[i - 1]))
        for i in range(step + 2):
            direction[i] = pair_add(residual[i], pair_mul(beta, direction[i]))
    weight = [s[0][0:1] for s in surface]

    def combine(side, r0, n):
        at = pl.ds(PAD + r0, n)
        total = weight[0] * v_ref[0, side, at]
        for i in range(1, 4):
            total = total + weight[i] * v_ref[i, side, at]
        return total

    chunks = [(0, HALO)] + blocks(HALO, HALO + ROWS, 32)
    for r0, n in chunks:
        s_ref[pl.ds(r0, n)] = combine(0, r0, n)
    for r0, n in chunks[1:]:
        s = s_ref[pl.ds(r0, n)]
        own = pl.ds(r0 - HALO, n)
        here = pl.ds(PAD + r0, n)
        west, _ = lane_left(s, combine(1, r0, n))
        d_west, _ = lane_left(d_ref[0, here], d_ref[1, here])
        d = d_ref[0, here]
        surface_ref[own] = s
        flow_ref[0, own] = jnp.minimum(d, d_ref[0, pl.ds(PAD + r0 - 1, n)]) * (s_ref[pl.ds(r0 - 1, n)] - s)
        flow_ref[1, own] = jnp.minimum(d, d_west) * (west - s)


VM = pl.BlockSpec(memory_space=pltpu.VMEM)
SM = pl.BlockSpec(memory_space=pltpu.SMEM)


def params(**kwargs):
    return pltpu.CompilerParams(vmem_limit_bytes=VMEM_LIMIT, **kwargs)


def ring(x, axis, step):
    count = lax.axis_size(axis)
    return lax.ppermute(x, axis, [(i, (i + step) % count) for i in range(count)])


def shards(tracers, mixing, thickness, levels, land):
    devices = lax.axis_size("bx") * lax.axis_size("by")
    wet = wet_levels(levels, land).astype(F32)
    flat = tracers.reshape(2 * KL, ROWS, LANES)
    with jax.named_scope("rows"):
        to_up = jnp.concatenate([flat[:, :HALO], wet[None, :HALO]])
        to_down = jnp.concatenate([flat[:, -HALO:], wet[None, -HALO:]])
        top = ring(to_down, "bx", 1)
        bottom = ring(to_up, "bx", -1)
    edge_shape = jax.ShapeDtypeStruct((TILES, EXT, LANES), F32)
    with jax.named_scope("columns"):
        to_right, to_left = pl.pallas_call(
            pack_kernel,
            out_shape=(edge_shape, edge_shape),
            in_specs=[VM] * 5,
            out_specs=(VM, VM),
            compiler_params=params(),
            cost_estimate=pl.CostEstimate(flops=10_000_000, bytes_accessed=7_000_000, transcendentals=0),
        )(tracers, top, bottom, levels, land)
        from_left = ring(to_right, "by", 1)
        from_right = ring(to_left, "by", -1)
    level_block = pl.BlockSpec((KL // HALF_STEPS, 2, ROWS, LANES), lambda i: (i, 0, 0, 0))
    plane = jax.ShapeDtypeStruct((EXT, LANES), F32)
    buf = pltpu.VMEM((BUF, LANES), F32)
    buf2 = pltpu.VMEM((2, BUF, LANES), F32)
    with jax.named_scope("density"):
        fx, fy = pl.pallas_call(
            density_kernel,
            grid=(HALF_STEPS,),
            out_shape=(plane, plane),
            in_specs=[SM, SM, level_block, VM, VM, VM, VM],
            out_specs=(VM, VM),
            scratch_shapes=[
                pltpu.VMEM((BUF, LANES), I32),
                pltpu.VMEM((2, EXT, LANES), I32),
                pltpu.VMEM((3, EXT, LANES), I32),
                buf,
                buf,
                buf,
            ],
            compiler_params=params(),
            cost_estimate=pl.CostEstimate(flops=50_000_000, bytes_accessed=7_000_000, transcendentals=0),
        )(mixing, thickness, tracers, top, bottom, levels, land)
    edges = (from_left, from_right, to_right, to_left)
    with jax.named_scope("powers"):
        powers, depth, sums = pl.pallas_call(
            solve_kernel,
            out_shape=(
                jax.ShapeDtypeStruct((5, 2, BUF, LANES), F32),
                jax.ShapeDtypeStruct((2, BUF, LANES), F32),
                jax.ShapeDtypeStruct((devices, LANES), F32),
            ),
            in_specs=[SM, SM] + [VM] * 10,
            out_specs=(VM, VM, VM),
            scratch_shapes=[
                pltpu.VMEM((2, BUF, LANES), I32),
                pltpu.VMEM((2, EXT, LANES), I32),
                buf,
                buf,
                buf,
                pltpu.VMEM((EXT, LANES), F32),
                pltpu.VMEM((2, EXT, LANES), F32),
                pltpu.VMEM((2, EXT, LANES), F32),
                buf2,
                buf2,
                buf2,
                buf2,
                pltpu.VMEM((9, 2, EXT, LANES), F32),
                buf2,
                buf2,
            ],
            compiler_params=params(),
            cost_estimate=pl.CostEstimate(flops=50_000_000, bytes_accessed=6_000_000, transcendentals=0),
        )(mixing, thickness, fx, fy, *edges, top, bottom, levels, land)
    with jax.named_scope("sums"):
        everyone = lax.all_to_all(sums, ("bx", "by"), 0, 0, tiled=True)
    with jax.named_scope("tracers"):
        tracers_new = pl.pallas_call(
            tracer_kernel,
            grid=(HALF_STEPS,),
            out_shape=jax.ShapeDtypeStruct(tracers.shape, F32),
            in_specs=[SM, level_block] + [VM] * 8,
            out_specs=level_block,
            scratch_shapes=[
                pltpu.VMEM((BUF, LANES), I32),
                pltpu.VMEM((3, EXT, LANES), I32),
                buf2,
                buf2,
                pltpu.VMEM((2, TILES, ROWS, LANES), F32),
                pltpu.VMEM((BUF, LANES), I32),
                buf,
                buf,
            ],
            compiler_params=params(),
            cost_estimate=pl.CostEstimate(flops=80_000_000, bytes_accessed=13_000_000, transcendentals=0),
        )(mixing, tracers, top, bottom, levels, land, *edges)
    with jax.named_scope("surface"):
        surface, transports = pl.pallas_call(
            finish_kernel,
            out_shape=(
                jax.ShapeDtypeStruct((ROWS, LANES), F32),
                jax.ShapeDtypeStruct((2, ROWS, LANES), F32),
            ),
            in_specs=[VM] * 3,
            out_specs=(VM, VM),
            scratch_shapes=[pltpu.VMEM((HALO + ROWS, LANES), F32)],
            compiler_params=params(),
            cost_estimate=pl.CostEstimate(flops=1_000_000, bytes_accessed=3_000_000, transcendentals=0),
        )(everyone, powers, depth)
    return tracers_new, surface, transports


def solution(mesh):
    in_specs = (P(None, None, "bx", "by"), P(), P(), P("bx", "by"), P("bx", "by"))
    out_specs = (P(None, None, "bx", "by"), P("bx", "by"), P(None, "bx", "by"))
    return jax.shard_map(shards, mesh=mesh, in_specs=in_specs, out_specs=out_specs, check_vma=False)
```

time: 834 us -> 99.7 us (0.12)
  blocking collectives: 499 us -> 0 us
  other arithmetic: 154 us -> 1.09 us
  local copies, waits for them, and re-layouts: 121 us -> 5.47 us
  Pallas kernels: 0 us -> 70.2 us
  starting transfers between devices: 33.7 us -> 17 us
  between operations: 10.6 us -> 0.74 us
    psum x7 -> x0, blocking collectives: 465 us -> none  [the longest x4 258 us: squares(): return lax.psum(jnp.sum(residual * residual), ('bx', 'by'))]
    pallas_call x0 -> x5, Pallas kernels: none -> 70.2 us  [the longest x1 31.6 us: shards(): pl.pallas_call(solve_kernel, out_shape=(jax.ShapeDtypeStruct((5, 2, BUF,...]
    mul x2 -> x0, local copies, waits for them, and re-layouts: 47.4 us -> none  [laplace(): return wet[..., 1:-1, 1:-1] * total]
    mul x4 -> x0, other arithmetic: 42 us -> none  [the longest x1 35.5 us: laplace(): return wet[..., 1:-1, 1:-1] * total]
    sub x2 -> x0, other arithmetic: 39 us -> none  [the longest x1 38.9 us: shards(): renewed = field_ext[:, :, 2:-2, 2:-2] - mixing[:, :, None, None] * second]
    all_to_all x1 -> x0, blocking collectives: 34 us -> none  [shards(): lax.all_to_all(coeffs, 'by', split_axis=1, concat_axis=2, tiled=True)]
    reduce_sum x11 -> x0, other arithmetic: 33.9 us -> none  [the longest x1 13.5 us: shards(): jnp.sum(layer * wet_cycle[:, 1:-1, 1:] * wet_cycle[:, 1:-1, :-1] * (press...]
    slice x21 -> x1, local copies, waits for them, and re-layouts: 29.1 us -> 1.04 us  [shards(): to_up = jnp.concatenate([flat[:, :HALO], wet[None, :HALO]])]
  transfers between devices with their start and end apart: 13 -> 5, of which waited for: 9 -> 2; matrix products, arithmetic and copies ran while one was open for 3% -> 0% of each run, Pallas kernels for 0% -> 32%
where the time goes in v1:
time: 99.7 us; the launch traced here: 99.4 us
  Pallas kernels  70.2 us (70%)
  starting transfers between devices  17 us (17%)
  local copies, waits for them, and re-layouts  5.47 us (5%)
  waiting for transfers between devices  4.96 us (5%)
  other arithmetic  1.09 us (1%)
    pallas_call x1, Pallas kernels, shards(): pl.pallas_call(solve_kernel, out_shape=(jax.ShapeDtypeStruct((5, 2, BUF,...  31.6 us
    pallas_call x1, Pallas kernels, shards(): pl.pallas_call(tracer_kernel, grid=(HALF_STEPS,), out_shape=jax.ShapeDtyp...  21.3 us
    pallas_call x1, Pallas kernels, shards(): pl.pallas_call(density_kernel, grid=(HALF_STEPS,), out_shape=(plane, plan...  10 us
    ppermute x4, starting transfers between devices, ring(): lax.ppermute(x, axis, [(i, (i + step) % count) for i in range(count)])  9 us
    all_to_all x1, starting transfers between devices, shards(): everyone = lax.all_to_all(sums, ('bx', 'by'), 0, 0, tiled=True)  7.96 us
    pallas_call x1, Pallas kernels, shards(): pl.pallas_call(pack_kernel, out_shape=(edge_shape, edge_shape), in_specs=...  5.79 us
    ppermute x4, waiting for transfers between devices, ring(): lax.ppermute(x, axis, [(i, (i + step) % count) for i in range(count)])  4.95 us
    unnamed x17, local copies, waits for them, and re-layouts  4.42 us
  transfers between devices with their start and end apart: 5, of which 2 were waited for; matrix products, arithmetic and copies ran while one was open for 0% of the time, Pallas kernels for 32%

profile of v1, /device:TPU:1, one launch (start us, length us, event | category | flops | bytes accessed | tf_op | source)
XLA Modules:
  0.0 99.4 jit_solution(744677614862175677)
XLA Ops:
  0.6 0.0 copy-start.3
  0.6 0.0 copy-start.1
  0.7 0.0 copy-start.7
  0.7 0.0 copy-start.6
  0.7 1.1 %select_convert_fusion = f32[256,128]{1,0:T(8,128)S(1)} fusion(s32[256,128]{1,0:T(8,128)} %levels_ref.7, s32[256,128]{1,0:T(8,128)} %land_ref.7), kind=kLoop, calls=%fused_computation.2 | loop fusion | flops 98304 | bytes 393216 | tf_op jit(solution)/shard_map/convert_element_type | solution.py:733
  1.7 1.0 %fusion = (f32[44,8,128]{2,1,0:T(8,128)S(1)}, f32[44,8,128]{2,1,0:T(8,128)S(1)}) fusion(f32[44,256,128]{2,1,0:T(8,128)} %bitcast.10), kind=kLoop, calls=%fused_computation.5 | loop fusion | bytes 720896 | tf_op jit(solution)/shard_map/rows/slice | solution.py:736
  2.8 2.7 %collective-permute-start = (f32[45,8,128]{2,1,0:T(8,128)S(1)}, f32[45,8,128]{2,1,0:T(8,128)S(1)}, u32[]{:S(2)}, u32[]{:S(2)}) collective-permute-start(f32[45,8,128]{2,1,0:T(8,128)S(1)} %pad_maximum_fusion), channel_id=1, source_target_pairs={{0,16},{16,32},{32,48},{48,64},{64,80},{80,96},{96,112},{112,0},{1... | collective-permute-start | bytes 552968 | tf_op jit(solution)/shard_map/rows/ppermute | solution.py:728
  5.5 0.0 collective-permute-start.1
  5.6 2.4 %collective-permute-done.top_ref = f32[45,8,128]{2,1,0:T(8,128)S(1)} collective-permute-done((f32[45,8,128]{2,1,0:T(8,128)S(1)}, f32[45,8,128]{2,1,0:T(8,128)S(1)}, u32[]{:S(2)}, u32[]{:S(2)}) %collective-permute-start) | collective-permute-done | bytes 184352 | tf_op jit(solution)/shard_map/rows/ppermute | solution.py:728
  8.0 2.5 %collective-permute-done.1.bottom_ref = f32[45,8,128]{2,1,0:T(8,128)S(1)} collective-permute-done((f32[45,8,128]{2,1,0:T(8,128)S(1)}, f32[45,8,128]{2,1,0:T(8,128)S(1)}, u32[]{:S(2)}, u32[]{:S(2)}) %collective-permute-start.1) | collective-permute-done | bytes 184352 | tf_op jit(solution)/shard_map/rows/ppermute | solution.py:728
  10.5 0.0 copy-start
  10.5 0.9 copy-done
  11.4 0.0 copy-start.2
  11.4 0.9 copy-done.2
  12.3 5.8 %columns.1 = (f32[3,272,128]{2,1,0:T(8,128)S(1)}, f32[3,272,128]{2,1,0:T(8,128)S(1)}) custom-call(f32[22,2,256,128]{3,2,1,0:T(8,128)} %t_ref.5, f32[45,8,128]{2,1,0:T(8,128)S(1)} %collective-permute-done.top_ref, f32[45,8,128]{2,1,0:T(8,128)S(1)} %collective-permute-done.1.bottom_ref, s32[256,128]{1,0:T(8,128)S(1)} %copy-done, s32[256,128]{1,0:T(8,128)S(1)} %copy-done.2), custom_call_target="tpu_custom_call" | custom-call | flops 10000000 | bytes 7000000 | tf_op jit(solution)/shard_map/columns/pallas_call | solution.py:742
  18.1 1.3 %collective-permute-start.2 = (f32[3,272,128]{2,1,0:T(8,128)S(1)}, f32[3,272,128]{2,1,0:T(8,128)S(1)}, u32[]{:S(2)}, u32[]{:S(2)}) collective-permute-start(f32[3,272,128]{2,1,0:T(8,128)S(1)} %get-tuple-element.12.to_right_ref), channel_id=1, source_target_pairs={{0,1},{1,2},{2,3},{3,4},{4,5},{5,6},{6,7},{7,8},{8,9},{9,10},{10,1... | collective-permute-start | bytes 1253384 | tf_op jit(solution)/shard_map/columns/ppermute | solution.py:728
  19.4 5.0 %collective-permute-start.3 = (f32[3,272,128]{2,1,0:T(8,128)S(1)}, f32[3,272,128]{2,1,0:T(8,128)S(1)}, u32[]{:S(2)}, u32[]{:S(2)}) collective-permute-start(f32[3,272,128]{2,1,0:T(8,128)S(1)} %get-tuple-element.13.to_left_ref), channel_id=1, source_target_pairs={{0,15},{1,0},{2,1},{3,2},{4,3},{5,4},{6,5},{7,6},{8,7},{9,8},{10,9... | collective-permute-start | bytes 1253384 | tf_op jit(solution)/shard_map/columns/ppermute | solution.py:728
  24.4 0.0 copy-done.7
  24.4 0.1 copy.11.mixing_ref
  24.5 0.0 copy-done.3
  24.5 0.0 copy-done.1
  24.5 0.0 copy-done.6
  24.5 10.0 %density.1 = (f32[272,128]{1,0:T(8,128)S(1)}, f32[272,128]{1,0:T(8,128)S(1)}) custom-call(f32[22,2]{1,0:T(8,128)S(1)} %copy.11.mixing_ref, f32[22]{0:T(128)S(1)} %copy-done.6, f32[22,2,256,128]{3,2,1,0:T(8,128)} %t_ref.5, f32[45,8,128]{2,1,0:T(8,128)S(1)} %collective-permute-done.top_ref, f32[45,8,128]{2,1,0:T(8,128)S(1)} %collective-permute-done.1.bottom_ref, ...), custom_call_target="tpu_custom_call" | custom-call | flops 50000000 | bytes 7000000 | tf_op jit(solution)/shard_map/density/pallas_call | solution.py:757
  34.5 0.0 collective-permute-done.2.from_left_ref
  34.6 0.0 collective-permute-done.3.from_right_ref
  34.6 31.6 %powers.1 = (f32[5,2,288,128]{3,2,1,0:T(8,128)S(1)}, f32[2,288,128]{2,1,0:T(8,128)S(1)}, f32[128,128]{1,0:T(8,128)}) custom-call(f32[22,2]{1,0:T(8,128)S(1)} %copy.11.mixing_ref, f32[22]{0:T(128)S(1)} %copy-done.6, f32[272,128]{1,0:T(8,128)S(1)} %get-tuple-element.14.fx_ref, f32[272,128]{1,0:T(8,128)S(1)} %get-tuple-element.15.fy_ref, ...), custom_call_target="tpu_custom_call" | custom-call | flops 50000000 | bytes 6000000 | tf_op jit(solution)/shard_map/powers/pallas_call | solution.py:776
  66.1 0.0 copy-start.4
  66.1 1.1 %copy-done.4 = f32[5,2,288,128]{3,2,1,0:T(8,128)} copy-done((f32[5,2,288,128]{3,2,1,0:T(8,128)}, f32[5,2,288,128]{3,2,1,0:T(8,128)S(1)}, u32[]{:S(2)}) %copy-start.4) | copy-done | bytes 1474584
  67.3 8.0 %all-to-all-start = ((f32[128,1,128]{2,1,0:T(1,128)}), f32[128,1,128]{2,1,0:T(1,128)S(1)}, u32[]{:S(2)}, u32[]{:S(2)}) async-start(f32[128,1,128]{2,1,0:T(1,128)} %bitcast.4), calls=%async_computation | async-start | bytes 131072 | tf_op jit(solution)/shard_map/sums/all_to_all | solution.py:806
  75.2 21.3 %tracers.1 = f32[22,2,256,128]{3,2,1,0:T(8,128)} custom-call(f32[22,2]{1,0:T(8,128)S(1)} %copy.11.mixing_ref, f32[22,2,256,128]{3,2,1,0:T(8,128)} %t_ref.5, f32[45,8,128]{2,1,0:T(8,128)S(1)} %collective-permute-done.top_ref, f32[45,8,128]{2,1,0:T(8,128)S(1)} %collective-permute-done.1.bottom_ref, s32[256,128]{1,0:T(8,128)S(1)} %copy-done.1, ...), custom_call_target="tpu_custom_call" | custom-call | flops 80000000 | bytes 13000000 | tf_op jit(solution)/shard_map/tracers/pallas_call | solution.py:808
  96.6 0.0 all-to-all-done
  96.6 0.0 copy-start.5
  96.6 1.4 %copy-done.5 = f32[5,2,288,128]{3,2,1,0:T(8,128)S(1)} copy-done((f32[5,2,288,128]{3,2,1,0:T(8,128)S(1)}, f32[5,2,288,128]{3,2,1,0:T(8,128)}, u32[]{:S(2)}) %copy-start.5) | copy-done | bytes 1474584
  97.9 1.4 %surface.1 = (f32[256,128]{1,0:T(8,128)}, f32[2,256,128]{2,1,0:T(8,128)}) custom-call(f32[128,128]{1,0:T(8,128)S(1)} %bitcast.9, f32[5,2,288,128]{3,2,1,0:T(8,128)S(1)} %copy-done.5, f32[2,288,128]{2,1,0:T(8,128)S(1)} %get-tuple-element.18.d_ref), custom_call_target="tpu_custom_call" | custom-call | flops 1000000 | bytes 3000000 | tf_op jit(solution)/shard_map/surface/pallas_call | solution.py:828
  (3 shorter events, 0.0 us)
Async XLA Ops:
  0.6 23.9 %copy-start.3 = (s32[256,128]{1,0:T(8,128)S(1)}, s32[256,128]{1,0:T(8,128)}, u32[]{:S(2)}) copy-start(s32[256,128]{1,0:T(8,128)} %land_ref.7) | copy-start | bytes 393220
  0.6 23.9 %copy-start.1 = (s32[256,128]{1,0:T(8,128)S(1)}, s32[256,128]{1,0:T(8,128)}, u32[]{:S(2)}) copy-start(s32[256,128]{1,0:T(8,128)} %levels_ref.7) | copy-start | bytes 393220
  0.7 23.7 %copy-start.7 = (f32[22,2]{0,1:T(2,128)S(1)}, f32[22,2]{0,1:T(2,128)}, u32[]{:S(2)}) copy-start(f32[22,2]{0,1:T(2,128)} %param.6) | copy-start | bytes 532
  0.7 23.8 %copy-start.6 = (f32[22]{0:T(128)S(1)}, f32[22]{0:T(128)}, u32[]{:S(2)}) copy-start(f32[22]{0:T(128)} %thick_ref.3) | copy-start | bytes 268
  2.8 5.2 %collective-permute-start = (f32[45,8,128]{2,1,0:T(8,128)S(1)}, f32[45,8,128]{2,1,0:T(8,128)S(1)}, u32[]{:S(2)}, u32[]{:S(2)}) collective-permute-start(f32[45,8,128]{2,1,0:T(8,128)S(1)} %pad_maximum_fusion), channel_id=1, source_target_pairs={{0,16},{16,32},{32,48},{48,64},{64,80},{80,96},{96,112},{112,0},{1... | collective-permute-start | bytes 552968 | tf_op jit(solution)/shard_map/rows/ppermute | solution.py:728
  5.5 5.0 %collective-permute-start.1 = (f32[45,8,128]{2,1,0:T(8,128)S(1)}, f32[45,8,128]{2,1,0:T(8,128)S(1)}, u32[]{:S(2)}, u32[]{:S(2)}) collective-permute-start(f32[45,8,128]{2,1,0:T(8,128)S(1)} %pad_maximum_fusion.1), channel_id=1, source_target_pairs={{0,112},{16,0},{32,16},{48,32},{64,48},{80,64},{96,80},{112,96},{1... | collective-permute-start | bytes 552968 | tf_op jit(solution)/shard_map/rows/ppermute | solution.py:728
  10.5 0.9 copy-start
  11.4 0.9 copy-start.2
  18.1 16.4 %collective-permute-start.2 = (f32[3,272,128]{2,1,0:T(8,128)S(1)}, f32[3,272,128]{2,1,0:T(8,128)S(1)}, u32[]{:S(2)}, u32[]{:S(2)}) collective-permute-start(f32[3,272,128]{2,1,0:T(8,128)S(1)} %get-tuple-element.12.to_right_ref), channel_id=1, source_target_pairs={{0,1},{1,2},{2,3},{3,4},{4,5},{5,6},{6,7},{7,8},{8,9},{9,10},{10,1... | collective-permute-start | bytes 1253384 | tf_op jit(solution)/shard_map/columns/ppermute | solution.py:728
  19.4 15.2 %collective-permute-start.3 = (f32[3,272,128]{2,1,0:T(8,128)S(1)}, f32[3,272,128]{2,1,0:T(8,128)S(1)}, u32[]{:S(2)}, u32[]{:S(2)}) collective-permute-start(f32[3,272,128]{2,1,0:T(8,128)S(1)} %get-tuple-element.13.to_left_ref), channel_id=1, source_target_pairs={{0,15},{1,0},{2,1},{3,2},{4,3},{5,4},{6,5},{7,6},{8,7},{9,8},{10,9... | collective-permute-start | bytes 1253384 | tf_op jit(solution)/shard_map/columns/ppermute | solution.py:728
  66.1 1.1 %copy-start.4 = (f32[5,2,288,128]{3,2,1,0:T(8,128)}, f32[5,2,288,128]{3,2,1,0:T(8,128)S(1)}, u32[]{:S(2)}) copy-start(f32[5,2,288,128]{3,2,1,0:T(8,128)S(1)} %get-tuple-element.17.v_ref) | copy-start | bytes 4423684
  67.3 29.3 %all-to-all-start = ((f32[128,1,128]{2,1,0:T(1,128)}), f32[128,1,128]{2,1,0:T(1,128)S(1)}, u32[]{:S(2)}, u32[]{:S(2)}) async-start(f32[128,1,128]{2,1,0:T(1,128)} %bitcast.4), calls=%async_computation | async-start | bytes 131072 | tf_op jit(solution)/shard_map/sums/all_to_all | solution.py:806
  96.6 1.4 %copy-start.5 = (f32[5,2,288,128]{3,2,1,0:T(8,128)S(1)}, f32[5,2,288,128]{3,2,1,0:T(8,128)}, u32[]{:S(2)}) copy-start(f32[5,2,288,128]{3,2,1,0:T(8,128)} %copy-done.4) | copy-start | bytes 4423684

commit v2 on v0

v2 whole, which is shorter than its diff:
```python
import jax
import jax.numpy as jnp
from jax import lax
from jax.experimental import pallas as pl
from jax.experimental.pallas import tpu as pltpu
from jax.sharding import PartitionSpec as P

KL = 22
ROWS = 256
LANES = 128
HALO = 8
EXT = ROWS + 2 * HALO
PAD = 8
BUF = EXT + 2 * PAD
GROUP = 16
GROUPS = LANES // GROUP
TILES = 3
LOADS = 4
MOMENTS = 8
F32 = jnp.float32
I32 = jnp.int32
VMEM_LIMIT = 20 * 1024 * 1024


def lane_iota(rows):
    return lax.broadcasted_iota(I32, (rows, LANES), 1)


def first_half(rows):
    return (lane_iota(rows) & 8) == 0


def roll(x, shift):
    return pltpu.roll(x, shift % LANES, 1)


def blocks(start, stop, size):
    out = []
    while start < stop:
        out.append((start, min(size, stop - start)))
        start += size
    return out


CHUNKS = blocks(0, EXT, 32)
OWN_CHUNKS = blocks(HALO, HALO + ROWS, 32)


def wet_levels(levels, land):
    return jnp.where(land == 0, levels, 0)


def edge_slot(k):
    return k % TILES, k // TILES


def place(x, k, old):
    _, g = edge_slot(k)
    return jnp.where(lane_iota(x.shape[0]) // GROUP == g, roll(x, 8 + GROUP * g), old)


def to_neighbours(a, b):
    first = first_half(a.shape[0])
    return jnp.where(first, a, roll(b, 8)), jnp.where(first, roll(b, -8), a)


def own_edges_kernel(t_ref, levels_ref, land_ref, ext_ref, eff_ref, edge_ref, right_ref, left_ref, sems):
    parts = blocks(0, KL, -(-KL // LOADS))

    def copy(i):
        start, count = parts[i]
        return pltpu.make_async_copy(
            t_ref.at[pl.ds(2 * start, 2 * count)],
            ext_ref.at[pl.ds(2 * start, 2 * count), pl.ds(HALO, ROWS)],
            sems.at[i],
        )

    for i in range(len(parts)):
        copy(i).start()
    eff_ref[pl.ds(HALO, ROWS)] = wet_levels(levels_ref[...], land_ref[...])
    size = 64
    tile_eff, _ = edge_slot(KL)

    def clear(step, carry):
        at = pl.ds(pl.multiple_of(HALO + size * step, 8), size)
        zero = jnp.zeros((size, LANES), F32)
        for c in range(2):
            for tile in range(TILES):
                edge_ref[c, tile, at] = zero
            edge_ref[c, tile_eff, at] = place(eff_ref[at].astype(F32), KL, zero)
        return carry

    lax.fori_loop(0, ROWS // size, clear, 0)
    for i, (start, count) in enumerate(parts):
        copy(i).wait()

        def rows(step, carry):
            at = pl.ds(pl.multiple_of(HALO + size * step, 8), size)
            for k in range(start, start + count):
                tile, _ = edge_slot(k)
                for c in range(2):
                    edge_ref[c, tile, at] = place(ext_ref[2 * k + c, at], k, edge_ref[c, tile, at])
            return carry

        lax.fori_loop(0, ROWS // size, rows, 0)

    def send(step, carry):
        at = pl.ds(pl.multiple_of(HALO + size * step, 8), size)
        for tile in range(TILES):
            right_ref[tile, at], left_ref[tile, at] = to_neighbours(edge_ref[0, tile, at], edge_ref[1, tile, at])
        return carry

    lax.fori_loop(0, ROWS // size, send, 0)


def halo_edges_kernel(
    top_ref, bottom_ref, ext_in, eff_in, edge_in, right_in, left_in, ext_ref, eff_ref, edge_ref, right_ref, left_ref
):
    for r0, ref in ((0, top_ref), (HALO + ROWS, bottom_ref)):
        at = pl.ds(r0, HALO)
        eff = ref[2 * KL]
        eff_ref[at] = eff.astype(I32)
        held = [[jnp.zeros((HALO, LANES), F32) for _ in range(TILES)] for _ in range(2)]
        for k in range(KL + 1):
            tile, _ = edge_slot(k)
            for c in range(2):
                if k < KL:
                    x = ref[2 * k + c]
                    ext_ref[2 * k + c, at] = x
                else:
                    x = eff
                held[c][tile] = place(x, k, held[c][tile])
        for tile in range(TILES):
            for c in range(2):
                edge_ref[c, tile, at] = held[c][tile]
            right_ref[tile, at], left_ref[tile, at] = to_neighbours(held[0][tile], held[1][tile])


def count_word(effs, word):
    total = None
    for eff in effs:
        bits = jnp.clip(eff - 10 * word, 0, 10) * 3
        mask = (lax.shift_left(jnp.full_like(bits, 1), bits) - 1) & 0o1111111111
        total = mask if total is None else total + mask
    return total


def neighbours(ref, r0, n):
    x = ref[pl.ds(PAD + r0, n)]
    around = ref[pl.ds(PAD + r0 - 1, n)] + ref[pl.ds(PAD + r0 + 1, n)]
    return x, around + (roll(x, 1) + roll(x, -1))


def block_kernel(
    mixing_ref,
    thick_ref,
    ext_ref,
    eff_in,
    new_ref,
    fx_ref,
    fy_ref,
    eff_ref,
    min_ref,
    word_ref,
    u_ref,
    l_ref,
    acc_ref,
):
    eff_ref[...] = jnp.zeros(eff_ref.shape, I32)
    eff_ref[pl.ds(PAD, EXT)] = eff_in[...]
    for ref in (u_ref, l_ref, acc_ref, fx_ref, fy_ref):
        ref[...] = jnp.zeros(ref.shape, F32)
    for r0, n in CHUNKS:
        e = eff_ref[pl.ds(PAD + r0, n)]
        min_ref[0, pl.ds(r0, n)] = jnp.minimum(e, eff_ref[pl.ds(PAD + r0 - 1, n)])
        min_ref[1, pl.ds(r0, n)] = jnp.minimum(e, roll(e, 1))
        effs = (eff_ref[pl.ds(PAD + r0 - 1, n)], eff_ref[pl.ds(PAD + r0 + 1, n)], roll(e, 1), roll(e, -1))
        for word in range(3):
            word_ref[word, pl.ds(r0, n)] = count_word(effs, word)

    def count(k, r0, n):
        words = word_ref[k // 10, pl.ds(r0, n)]
        shift = jnp.full((n, LANES), 3 * (k % 10), I32)
        return (lax.shift_right_logical(words, shift) & 7).astype(F32)

    def stage(step, late):
        k = jnp.clip(step - late, 0, KL - 1)
        valid = jnp.logical_and(step >= late, step < KL + late)
        return k, jnp.where(valid, thick_ref[k], 0.0)

    def body(step, carry):
        ku, _ = stage(step, 0)
        kl, _ = stage(step, 1)
        kd, thick_d = stage(step, 2)
        kf, thick_f = stage(step, 3)

        def flux(r0, n):
            here = acc_ref[pl.ds(PAD + r0, n)]
            up = acc_ref[pl.ds(PAD + r0 - 1, n)]
            face_x = min_ref[0, pl.ds(r0, n)] > kf
            face_y = min_ref[1, pl.ds(r0, n)] > kf
            fx_ref[pl.ds(r0, n)] += thick_f * jnp.where(face_x, here - up, 0.0)
            fy_ref[pl.ds(r0, n)] += thick_f * jnp.where(face_y, here - roll(here, 1), 0.0)

        def density(r0, n):
            wet = eff_ref[pl.ds(PAD + r0, n)] > kd
            number = count(kd, r0, n)
            new = []
            for c in range(2):
                x, around = neighbours(l_ref.at[c], r0, n)
                second = jnp.where(wet, around, 0.0) - number * x
                value = ext_ref[2 * kd + c, pl.ds(r0, n)] - mixing_ref[kd, c] * second
                low, high = max(r0, HALO), min(r0 + n, HALO + ROWS)
                new_ref[2 * kd + c, pl.ds(low - HALO, high - low)] = value[low - r0 : high - r0]
                new.append(value)
            plain = 0.8 * new[1] - 0.2 * new[0]
            acc_ref[pl.ds(PAD + r0, n)] += thick_d * jnp.where(wet, plain, 0.0)

        def first(r0, n):
            wet = eff_ref[pl.ds(PAD + r0, n)] > kl
            number = count(kl, r0, n)
            for c in range(2):
                x, around = neighbours(u_ref.at[c], r0, n)
                l_ref[c, pl.ds(PAD + r0, n)] = jnp.where(wet, around, 0.0) - number * x

        def masked(r0, n):
            wet = eff_ref[pl.ds(PAD + r0, n)] > ku
            for c in range(2):
                u_ref[c, pl.ds(PAD + r0, n)] = jnp.where(wet, ext_ref[2 * ku + c, pl.ds(r0, n)], 0.0)

        work = (flux, density, first, masked)
        for turn in range(len(CHUNKS) + len(work) - 1):
            for late, part in enumerate(work):
                if 0 <= turn - late < len(CHUNKS):
                    part(*CHUNKS[turn - late])
        return carry

    lax.fori_loop(0, KL + 3, body, 0)


def patch_kernel(new_in, edge_ref, new_ref):
    size = 32

    def level(k, carry):
        tile = k % TILES
        back = (2 * LANES - 8 - GROUP * (k // TILES)) % LANES
        for r0, n in blocks(0, ROWS, size):
            lane = lane_iota(n)
            middle = jnp.logical_and(lane >= 4, lane < LANES - 4)
            own = pl.ds(r0, n)
            for c in range(2):
                edge = pltpu.roll(edge_ref[c, tile, own], back, 1)
                new_ref[2 * k + c, own] = jnp.where(middle, new_in[2 * k + c, own], edge)
        return carry

    lax.fori_loop(0, KL, level, 0)


def two_sum(a, b):
    s = a + b
    v = s - a
    return s, (a - (s - v)) + (b - v)


def quick_sum(a, b):
    s = a + b
    return s, b - (s - a)


def split(a):
    t = a * 4097.0
    high = t - (t - a)
    return high, a - high


def two_prod(a, b, parts_a, parts_b):
    p = a * b
    ah, al = parts_a
    bh, bl = parts_b
    return p, ((ah * bh - p) + ah * bl + al * bh) + al * bl


def pair_add(x, y):
    s, e = two_sum(x[0], y[0])
    return quick_sum(s, e + (x[1] + y[1]))


def pair_mul(x, y):
    p, e = two_prod(x[0], y[0], split(x[0]), split(y[0]))
    return quick_sum(p, e + (x[0] * y[1] + x[1] * y[0]))


def pair_neg(x):
    return -x[0], -x[1]


def pair_div(x, y):
    q = x[0] / y[0]
    rest = pair_add(x, pair_neg(pair_mul(y, (q, jnp.zeros_like(q)))))
    return quick_sum(q, rest[0] / y[0])


def pair_clip(x, top):
    inside = jnp.logical_and(x[0] >= 0.0, x[0] <= top)
    high = jnp.where(inside, x[0], jnp.where(x[0] > top, top, 0.0))
    return high, jnp.where(inside, x[1], 0.0)


def group_totals(x):
    x = x + roll(x, GROUP)
    x = x + roll(x, 2 * GROUP)
    return x + roll(x, 4 * GROUP)


def lane_left(main, side):
    lane = lane_iota(main.shape[0])
    a, b = roll(main, 1), roll(side, 1)
    return jnp.where(lane == 0, b, a), jnp.where(lane == 0, a, b)


def lane_right(main, side):
    lane = lane_iota(main.shape[0])
    a, b = roll(main, -1), roll(side, -1)
    return jnp.where(lane == LANES - 1, b, a), jnp.where(lane == LANES - 1, a, b)


SIDES = (0, 1)


def solve_kernel(
    mixing_ref,
    thick_ref,
    fx_ref,
    fy_ref,
    from_left_ref,
    from_right_ref,
    edge_ref,
    eff_in,
    v_ref,
    d_ref,
    sums_ref,
    new_ref,
    e_ref,
    west_ref,
    east_ref,
    f_ref,
    u_ref,
    l_ref,
    n_ref,
    acc_ref,
    eff_ref,
    full_fx_ref,
    full_fy_ref,
    dl_ref,
    dr_ref,
    w_ref,
    p_ref,
    q_ref,
):
    by = lax.axis_index("by")
    open_side = (by != 0, by != lax.axis_size("by") - 1)

    def clear(ref):
        ref[...] = jnp.zeros(ref.shape, ref.dtype)

    for ref in (e_ref, west_ref, east_ref):
        clear(ref)
    for ref in (u_ref, l_ref, acc_ref, d_ref, v_ref, dl_ref, dr_ref, p_ref, q_ref, full_fx_ref, full_fy_ref):
        rank = len(ref.shape) - 2
        lead = [()]
        for size in ref.shape[:rank]:
            lead = [i + (j,) for i in lead for j in range(size)]
        for i in lead:
            for r0 in (0, BUF - PAD):
                ref[i + (pl.ds(r0, PAD),)] = jnp.zeros((PAD, LANES), F32)

    def field(side, c, tile, r0, n):
        own = edge_ref[c, tile, pl.ds(r0, n)]
        first = first_half(n)
        if side == 0:
            far = from_left_ref[tile, pl.ds(r0, n)]
            return jnp.where(first, roll(far, -8) if c else far, own)
        far = from_right_ref[tile, pl.ds(r0, n)]
        return jnp.where(first, own, roll(far, 8) if c else far)

    tile_eff, slot = edge_slot(KL)
    for side in SIDES:
        for r0, n in CHUNKS:
            lane = lane_iota(n)
            x = field(side, 0, tile_eff, r0, n)
            inner = (lane & 8) == (8 if side == 0 else 0)
            keep = jnp.logical_and(lane // GROUP == slot, jnp.logical_or(inner, open_side[side]))
            e = group_totals(jnp.where(keep, x, 0.0)).astype(I32)
            at = pl.ds(PAD + r0, n)
            e_ref[side, at] = e
            west_ref[side, at] = roll(e, 1)
            east_ref[side, at] = roll(e, -1)

    group8 = lane_iota(8) // GROUP

    def by_group(tile, values):
        out = jnp.zeros((8, LANES), F32)
        for g in range(GROUPS):
            k = TILES * g + tile
            value = values(jnp.minimum(k, KL - 1))
            out = jnp.where(group8 == g, jnp.where(k < KL, value, 0.0), out)
        return out[0:1]

    def level_lanes(tile):
        return (group8 * TILES + tile)[0:1]

    def tile_step(tile, carry):
        level_of = level_lanes(tile)
        mix = [by_group(tile, lambda k, c=c: mixing_ref[k, c]) for c in range(2)]
        thick = by_group(tile, lambda k: thick_ref[k])

        def masked(side, r0, n):
            at = pl.ds(PAD + r0, n)
            wet = e_ref[side, at] > level_of
            for c in range(2):
                x = field(side, c, tile, r0, n)
                f_ref[side, c, pl.ds(r0, n)] = x
                u_ref[side, c, at] = jnp.where(wet, x, 0.0)

        def first(side, r0, n):
            at = pl.ds(PAD + r0, n)
            wet = e_ref[side, at] > level_of
            number = jnp.where(e_ref[side, pl.ds(PAD + r0 - 1, n)] > level_of, 1.0, 0.0)
            number += jnp.where(e_ref[side, pl.ds(PAD + r0 + 1, n)] > level_of, 1.0, 0.0)
            number += jnp.where(west_ref[side, at] > level_of, 1.0, 0.0)
            number += jnp.where(east_ref[side, at] > level_of, 1.0, 0.0)
            n_ref[side, pl.ds(r0, n)] = number
            for c in range(2):
                x, around = neighbours(u_ref.at[side, c], r0, n)
                l_ref[side, c, at] = jnp.where(wet, around, 0.0) - number * x

        def density(side, r0, n):
            at = pl.ds(PAD + r0, n)
            wet = e_ref[side, at] > level_of
            number = n_ref[side, pl.ds(r0, n)]
            new = []
            for c in range(2):
                x, around = neighbours(l_ref.at[side, c], r0, n)
                second = jnp.where(wet, around, 0.0) - number * x
                new.append(f_ref[side, c, pl.ds(r0, n)] - mix[c] * second)
            acc_ref[side, tile, at] = thick * jnp.where(wet, 0.8 * new[1] - 0.2 * new[0], 0.0)
            low, high = max(r0, HALO), min(r0 + n, HALO + ROWS)
            own = pl.ds(low - HALO, high - low)
            for c in range(2):
                value = new[c][low - r0 : high - r0]
                if side == 1:
                    value = jnp.where(first_half(high - low), value, new_ref[c, tile, own])
                new_ref[c, tile, own] = value

        for part in (masked, first, density):
            for side in SIDES:
                for r0, n in CHUNKS:
                    part(side, r0, n)
        return carry

    lax.fori_loop(0, TILES, tile_step, 0)

    for side in SIDES:
        for r0, n in CHUNKS:
            lane = lane_iota(n)
            at = pl.ds(PAD + r0, n)
            layers = [acc_ref[side, tile, at] for tile in range(TILES)]
            run = (layers[0] + layers[1]) + layers[2]
            run = jnp.where(lane >= GROUP, roll(run, GROUP), 0.0)
            for step in (1, 2, 4):
                run = run + jnp.where(lane >= step * GROUP, roll(run, step * GROUP), 0.0)
            for tile in range(TILES):
                run = run + layers[tile]
                acc_ref[side, tile, at] = run
    thick = [by_group(tile, lambda k: thick_ref[k]) for tile in range(TILES)]
    for r0, n in CHUNKS:
        lane = lane_iota(n)
        own = pl.ds(r0, n)
        at = pl.ds(PAD + r0, n)
        totals = []
        for side in SIDES:
            e = e_ref[side, at]
            min_x = jnp.minimum(e, e_ref[side, pl.ds(PAD + r0 - 1, n)])
            min_y = jnp.minimum(e, west_ref[side, at])
            face_x = jnp.zeros((n, LANES), F32)
            face_y = face_x
            for tile in range(TILES):
                here = acc_ref[side, tile, at]
                up = acc_ref[side, tile, pl.ds(PAD + r0 - 1, n)]
                level_of = level_lanes(tile)
                face_x += thick[tile] * jnp.where(min_x > level_of, here - up, 0.0)
                face_y += thick[tile] * jnp.where(min_y > level_of, here - roll(here, 1), 0.0)
            totals.append([roll(group_totals(x), 8) for x in (face_x, face_y)])
        for full, main, west, east in (
            (full_fx_ref, fx_ref, totals[0][0], totals[1][0]),
            (full_fy_ref, fy_ref, totals[0][1], totals[1][1]),
        ):
            full[0, at] = jnp.where(lane < 4, west, jnp.where(lane >= LANES - 4, east, main[own]))
            full[1, at] = jnp.where(lane < 8, east, jnp.where(lane >= LANES - 8, west, 0.0))
        west = roll(e_ref[0, at], 8)
        east = roll(e_ref[1, at], 8)
        eff_ref[0, own] = eff_in[own]
        eff_ref[1, own] = jnp.where(lane < 8, east, jnp.where(lane >= LANES - 8, west, 0))

    def depths(step, carry):
        n = 16
        r0 = pl.multiple_of(step * n, 8)
        for t in range(2):
            e = eff_ref[t, pl.ds(r0, n)]
            d = jnp.zeros((n, LANES), F32)
            for k in range(KL):
                d += jnp.where(e > k, thick_ref[k], 0.0)
            d_ref[t, pl.ds(pl.multiple_of(PAD + r0, 8), n)] = d
        return carry

    lax.fori_loop(0, EXT // 16, depths, 0)
    for r0, n in CHUNKS:
        here = pl.ds(PAD + r0, n)
        d_main, d_side = d_ref[0, here], d_ref[1, here]
        dl_ref[0, here], dl_ref[1, here] = lane_left(d_main, d_side)
        dr_ref[0, here], dr_ref[1, here] = lane_right(d_main, d_side)

    for r0, n in CHUNKS:
        here = pl.ds(PAD + r0, n)
        east = lane_right(full_fy_ref[0, here], full_fy_ref[1, here])
        for t in range(2):
            fx = full_fx_ref[t, here] - full_fx_ref[t, pl.ds(PAD + r0 + 1, n)]
            fy = full_fy_ref[t, here] - east[t]
            v_ref[0, t, here] = 10.0 * (fx + fy)

    def weights(t, carry):
        for r0, n in CHUNKS:
            here = pl.ds(PAD + r0, n)
            above = pl.ds(PAD + r0 - 1, n)
            below = pl.ds(PAD + r0 + 1, n)
            d = d_ref[t, here]
            left, right = dl_ref[t, here], dr_ref[t, here]
            up, down = d_ref[t, above], d_ref[t, below]
            w_west, w_east = jnp.minimum(d, left), jnp.minimum(d, right)
            w_up, w_down = jnp.minimum(d, up), jnp.minimum(d, down)
            corners = (
                jnp.minimum(d, dl_ref[t, above])
                + jnp.minimum(d, dr_ref[t, below])
                + jnp.minimum(d, dr_ref[t, above])
                + jnp.minimum(d, dl_ref[t, below])
            )
            at = pl.ds(r0, n)
            w_ref[0, t, at] = 0.05 + w_up + w_down + w_west + w_east + 0.25 * corners
            w_ref[1, t, at] = w_west
            w_ref[2, t, at] = w_east
            w_ref[3, t, at] = w_down
            w_ref[4, t, at] = 0.25 * jnp.minimum(down, left)
            w_ref[5, t, at] = 0.25 * jnp.minimum(down, right)
            w_ref[6, t, at] = w_up
            w_ref[7, t, at] = 0.25 * jnp.minimum(up, left)
            w_ref[8, t, at] = 0.25 * jnp.minimum(up, right)
        return carry

    lax.fori_loop(0, 2, weights, 0)

    def power(step, carry):
        for r0, n in CHUNKS:
            here = pl.ds(PAD + r0, n)
            at = pl.ds(r0, n)
            v = (v_ref[step, 0, here], v_ref[step, 1, here])
            left = lane_left(*v)
            right = lane_right(*v)
            for t in range(2):
                w = [w_ref[m, t, at] for m in range(9)]
                p_ref[t, here] = w[3] * v[t] + w[4] * left[t] + w[5] * right[t]
                q_ref[t, here] = w[6] * v[t] + w[7] * left[t] + w[8] * right[t]
                v_ref[step + 1, t, here] = w[0] * v[t] - (w[1] * left[t] + w[2] * right[t])
        for r0, n in CHUNKS:
            here = pl.ds(PAD + r0, n)
            for t in range(2):
                beside = p_ref[t, pl.ds(PAD + r0 - 1, n)] + q_ref[t, pl.ds(PAD + r0 + 1, n)]
                v_ref[step + 1, t, here] -= beside
        return carry

    lax.fori_loop(0, 4, power, 0)

    def dots(step, carry):
        at = pl.ds(pl.multiple_of(PAD + HALO + 8 * step, 8), 8)
        v = [v_ref[i, 0, at] for i in range(5)]
        parts = [split(x) for x in v]
        out = []
        for m in range(MOMENTS):
            i, j = m // 2, (m + 1) // 2
            p, e = two_prod(v[i], v[j], parts[i], parts[j])
            s, f = two_sum(carry[2 * m], p)
            out += [s, carry[2 * m + 1] + (e + f)]
        return tuple(out)

    zero = jnp.zeros((8, LANES), F32)
    sums = lax.fori_loop(0, ROWS // 8, dots, (zero,) * (2 * MOMENTS), unroll=4)
    sub = lax.broadcasted_iota(I32, (8, LANES), 0)
    pairs = [(sums[2 * m], sums[2 * m + 1]) for m in range(MOMENTS)]
    for half in (4, 2, 1):
        merged = []
        for m in range(half):
            a, b = pairs[m], pairs[m + half]
            upper = (sub & half) == 0
            keep = tuple(jnp.where(upper, x, y) for x, y in zip(a, b))
            other = tuple(jnp.where(upper, pltpu.roll(x, 8 - half, 0), pltpu.roll(y, half, 0)) for x, y in zip(a, b))
            merged.append(pair_add(keep, other))
        pairs = merged
    total = pairs[0]
    for shift in (1, 2, 4, 8, 16, 32, 64):
        total = pair_add(total, tuple(roll(x, shift) for x in total))
    lane = lane_iota(8)
    row = jnp.where(lane == sub, total[0], jnp.where(lane == sub + MOMENTS, total[1], 0.0))
    for shift in (4, 2, 1):
        row = row + pltpu.roll(row, shift, 0)
    for at in range(0, sums_ref.shape[0], 8):
        sums_ref[pl.ds(at, 8)] = row


def finish_kernel(all_ref, v_ref, d_ref, surface_ref, flow_ref, s_ref):
    zero = jnp.zeros((8, LANES), F32)
    high, low = zero, zero
    for at in range(0, all_ref.shape[0], 8):
        high, e = two_sum(high, all_ref[pl.ds(at, 8)])
        low = low + e
    total = (high, low)
    for shift in (4, 2, 1):
        total = pair_add(total, tuple(pltpu.roll(x, shift, 0) for x in total))
    total = pair_add(total, tuple(roll(x, -MOMENTS) for x in total))
    lane = lane_iota(8)

    def moment(m):
        return tuple(
            jnp.broadcast_to(jnp.sum(jnp.where(lane == m, x, 0.0), axis=1, keepdims=True), (8, LANES))
            for x in total
        )

    rho = [moment(m) for m in range(MOMENTS)]
    pi = list(rho)
    nought = (zero, zero)
    one = (zero + 1.0, zero)
    surface = [nought] * 4
    residual = [one] + [nought] * 3
    direction = list(residual)
    for step in range(4):
        alpha = pair_clip(pair_div(rho[step], pi[step + 1]), 20.0)
        for i in range(step + 1):
            surface[i] = pair_add(surface[i], pair_mul(alpha, direction[i]))
        if step == 3:
            break
        minus = pair_neg(alpha)
        new_rho = list(rho)
        for m in range(step + 1, MOMENTS - 1 - step):
            new_rho[m] = pair_add(rho[m], pair_mul(minus, pi[m + 1]))
        beta = pair_clip(pair_div(pair_mul(minus, new_rho[step + 1]), rho[step]), 400.0)
        for m in range(step + 2, MOMENTS - 1 - step):
            pi[m] = pair_add(new_rho[m], pair_mul(beta, pi[m]))
        rho = new_rho
        for i in range(step + 1, 0, -1):
            residual[i] = pair_add(residual[i], pair_mul(minus, direction[i - 1]))
        for i in range(step + 2):
            direction[i] = pair_add(residual[i], pair_mul(beta, direction[i]))
    weight = [s[0][0:1] for s in surface]

    def combine(side, r0, n):
        at = pl.ds(PAD + r0, n)
        total = weight[0] * v_ref[0, side, at]
        for i in range(1, 4):
            total = total + weight[i] * v_ref[i, side, at]
        return total

    chunks = [(0, HALO)] + blocks(HALO, HALO + ROWS, 32)
    for r0, n in chunks:
        s_ref[pl.ds(r0, n)] = combine(0, r0, n)
    for r0, n in chunks[1:]:
        s = s_ref[pl.ds(r0, n)]
        own = pl.ds(r0 - HALO, n)
        here = pl.ds(PAD + r0, n)
        west, _ = lane_left(s, combine(1, r0, n))
        d_west, _ = lane_left(d_ref[0, here], d_ref[1, here])
        d = d_ref[0, here]
        surface_ref[own] = s
        flow_ref[0, own] = jnp.minimum(d, d_ref[0, pl.ds(PAD + r0 - 1, n)]) * (s_ref[pl.ds(r0 - 1, n)] - s)
        flow_ref[1, own] = jnp.minimum(d, d_west) * (west - s)


VM = pl.BlockSpec(memory_space=pltpu.VMEM)
SM = pl.BlockSpec(memory_space=pltpu.SMEM)
ANY = pl.BlockSpec(memory_space=pl.ANY)


def params(**kwargs):
    return pltpu.CompilerParams(vmem_limit_bytes=VMEM_LIMIT, **kwargs)


def cost(flops, moved):
    return pl.CostEstimate(flops=flops, bytes_accessed=moved, transcendentals=0)


def ring(x, axis, step):
    count = lax.axis_size(axis)
    return lax.ppermute(x, axis, [(i, (i + step) % count) for i in range(count)])


def shape(*sizes, dtype=F32):
    return jax.ShapeDtypeStruct(sizes, dtype)


def scratch(*lead, rows=BUF, dtype=F32):
    return pltpu.VMEM(lead + (rows, LANES), dtype)


def shards(tracers, mixing, thickness, levels, land):
    devices = lax.axis_size("bx") * lax.axis_size("by")
    planes = 2 * KL
    wet = wet_levels(levels, land).astype(F32)
    flat = tracers.reshape(planes, ROWS, LANES)
    with jax.named_scope("rows"):
        to_up = jnp.concatenate([flat[:, :HALO], wet[None, :HALO]])
        to_down = jnp.concatenate([flat[:, -HALO:], wet[None, -HALO:]])
        top = ring(to_down, "bx", 1)
        bottom = ring(to_up, "bx", -1)
    with jax.named_scope("columns"):
        edges = (
            shape(planes, EXT, LANES),
            shape(EXT, LANES, dtype=I32),
            shape(2, TILES, EXT, LANES),
            shape(TILES, EXT, LANES),
            shape(TILES, EXT, LANES),
        )
        own = pl.pallas_call(
            own_edges_kernel,
            out_shape=edges,
            in_specs=[ANY, VM, VM],
            out_specs=(VM,) * 5,
            scratch_shapes=[pltpu.SemaphoreType.DMA((LOADS,))],
            compiler_params=params(),
            cost_estimate=cost(10_000_000, 7_000_000),
        )(flat, levels, land)
        ext, eff, edge, to_right, to_left = pl.pallas_call(
            halo_edges_kernel,
            out_shape=edges,
            in_specs=[VM] * 7,
            out_specs=(VM,) * 5,
            input_output_aliases={i + 2: i for i in range(5)},
            compiler_params=params(),
            cost_estimate=cost(1_000_000, 700_000),
        )(top, bottom, *own)
        from_left = ring(to_right, "by", 1)
        from_right = ring(to_left, "by", -1)
    with jax.named_scope("block"):
        new, fx, fy = pl.pallas_call(
            block_kernel,
            out_shape=(shape(planes, ROWS, LANES), shape(EXT, LANES), shape(EXT, LANES)),
            in_specs=[SM, SM, VM, VM],
            out_specs=(VM,) * 3,
            scratch_shapes=[
                scratch(dtype=I32),
                scratch(2, rows=EXT, dtype=I32),
                scratch(3, rows=EXT, dtype=I32),
                scratch(2),
                scratch(2),
                scratch(),
            ],
            compiler_params=params(),
            cost_estimate=cost(50_000_000, 12_000_000),
        )(mixing, thickness, ext, eff)
    with jax.named_scope("powers"):
        powers, depth, sums, new_edge = pl.pallas_call(
            solve_kernel,
            out_shape=(
                shape(5, 2, BUF, LANES),
                shape(2, BUF, LANES),
                shape(devices, LANES),
                shape(2, TILES, ROWS, LANES),
            ),
            in_specs=[SM, SM] + [VM] * 6,
            out_specs=(VM,) * 4,
            scratch_shapes=[
                scratch(2, dtype=I32),
                scratch(2, dtype=I32),
                scratch(2, dtype=I32),
                scratch(2, 2, rows=EXT),
                scratch(2, 2),
                scratch(2, 2),
                scratch(2, rows=EXT),
                scratch(2, TILES),
                scratch(2, rows=EXT, dtype=I32),
                scratch(2),
                scratch(2),
                scratch(2),
                scratch(2),
                scratch(9, 2, rows=EXT),
                scratch(2),
                scratch(2),
            ],
            compiler_params=params(),
            cost_estimate=cost(50_000_000, 6_000_000),
        )(mixing, thickness, fx, fy, from_left, from_right, edge, eff)
    with jax.named_scope("sums"):
        everyone = lax.all_to_all(sums, ("bx", "by"), 0, 0, tiled=True)
    with jax.named_scope("patch"):
        tracers_new = pl.pallas_call(
            patch_kernel,
            out_shape=shape(planes, ROWS, LANES),
            in_specs=[VM, VM],
            out_specs=VM,
            input_output_aliases={0: 0},
            compiler_params=params(),
            cost_estimate=cost(10_000_000, 12_000_000),
        )(new, new_edge)
    with jax.named_scope("surface"):
        surface, transports = pl.pallas_call(
            finish_kernel,
            out_shape=(shape(ROWS, LANES), shape(2, ROWS, LANES)),
            in_specs=[VM] * 3,
            out_specs=(VM, VM),
            scratch_shapes=[scratch(rows=HALO + ROWS)],
            compiler_params=params(),
            cost_estimate=cost(1_000_000, 3_000_000),
        )(everyone, powers, depth)
    return tracers_new.reshape(tracers.shape), surface, transports


def solution(mesh):
    in_specs = (P(None, None, "bx", "by"), P(), P(), P("bx", "by"), P("bx", "by"))
    out_specs = (P(None, None, "bx", "by"), P("bx", "by"), P(None, "bx", "by"))
    return jax.shard_map(shards, mesh=mesh, in_specs=in_specs, out_specs=out_specs, check_vma=False)
```

time: 834 us -> 76.5 us (0.09)
  blocking collectives: 499 us -> 0 us
  other arithmetic: 154 us -> 1.02 us
  local copies, waits for them, and re-layouts: 121 us -> 15.1 us
  Pallas kernels: 0 us -> 42.5 us
  starting transfers between devices: 33.7 us -> 15.3 us
  between operations: 10.6 us -> 0.73 us
  waiting for transfers between devices: 10.1 us -> 1.41 us
    psum x7 -> x0, blocking collectives: 465 us -> none  [the longest x4 258 us: squares(): return lax.psum(jnp.sum(residual * residual), ('bx', 'by'))]
    mul x2 -> x0, local copies, waits for them, and re-layouts: 47.4 us -> none  [laplace(): return wet[..., 1:-1, 1:-1] * total]
    pallas_call x0 -> x6, Pallas kernels: none -> 42.5 us  [the longest x1 14.7 us: shards(): pl.pallas_call(block_kernel, out_shape=(shape(planes, ROWS, LANES), shape...]
    mul x4 -> x0, other arithmetic: 42 us -> none  [the longest x1 35.5 us: laplace(): return wet[..., 1:-1, 1:-1] * total]
    sub x2 -> x0, other arithmetic: 39 us -> none  [the longest x1 38.9 us: shards(): renewed = field_ext[:, :, 2:-2, 2:-2] - mixing[:, :, None, None] * second]
    all_to_all x1 -> x0, blocking collectives: 34 us -> none  [shards(): lax.all_to_all(coeffs, 'by', split_axis=1, concat_axis=2, tiled=True)]
    reduce_sum x11 -> x0, other arithmetic: 33.9 us -> none  [the longest x1 13.5 us: shards(): jnp.sum(layer * wet_cycle[:, 1:-1, 1:] * wet_cycle[:, 1:-1, :-1] * (press...]
    slice x21 -> x1, local copies, waits for them, and re-layouts: 29.1 us -> 1.04 us  [shards(): to_up = jnp.concatenate([flat[:, :HALO], wet[None, :HALO]])]
  transfers between devices with their start and end apart: 13 -> 5, of which waited for: 9 -> 1; matrix products, arithmetic and copies ran while one was open for 3% -> 0% of each run, Pallas kernels for 0% -> 35%
where the time goes in v2:
time: 76.5 us; the launch traced here: 76 us
  Pallas kernels  42.5 us (56%)
  starting transfers between devices  15.3 us (20%)
  local copies, waits for them, and re-layouts  15.1 us (20%)
  waiting for transfers between devices  1.41 us (2%)
  other arithmetic  1.02 us (1%)
    pallas_call x1, Pallas kernels, shards(): pl.pallas_call(block_kernel, out_shape=(shape(planes, ROWS, LANES), shape...  14.7 us
    pallas_call x1, Pallas kernels, shards(): pl.pallas_call(solve_kernel, out_shape=(shape(5, 2, BUF, LANES), shape(2,...  14.1 us
    unnamed x25, local copies, waits for them, and re-layouts  14 us
    ppermute x4, starting transfers between devices, ring(): lax.ppermute(x, axis, [(i, (i + step) % count) for i in range(count)])  8.67 us
    pallas_call x1, Pallas kernels, shards(): pl.pallas_call(patch_kernel, out_shape=shape(planes, ROWS, LANES), in_spe...  8.31 us
    all_to_all x1, starting transfers between devices, shards(): everyone = lax.all_to_all(sums, ('bx', 'by'), 0, 0, tiled=True)  6.61 us
    pallas_call x1, Pallas kernels, shards(): pl.pallas_call(own_edges_kernel, out_shape=edges, in_specs=[ANY, VM, VM],...  3.83 us
  transfers between devices with their start and end apart: 5, of which 1 were waited for; matrix products, arithmetic and copies ran while one was open for 0% of the time, Pallas kernels for 35%

profile of v2, /device:TPU:1, one launch (start us, length us, event | category | flops | bytes accessed | tf_op | source)
XLA Modules:
  0.0 76.0 jit_solution(4743921878039376094)
XLA Ops:
  0.6 1.0 %fusion = (f32[44,8,128]{2,1,0:T(8,128)S(1)}, f32[44,8,128]{2,1,0:T(8,128)S(1)}) fusion(f32[44,256,128]{2,1,0:T(8,128)} %bitcast.10), kind=kLoop, calls=%fused_computation.5 | loop fusion | bytes 720896 | tf_op jit(solution)/shard_map/rows/slice | solution.py:717
  1.7 1.0 %select_convert_fusion = f32[256,128]{1,0:T(8,128)S(1)} fusion(s32[256,128]{1,0:T(8,128)} %levels_ref.1, s32[256,128]{1,0:T(8,128)} %land_ref.1), kind=kLoop, calls=%fused_computation.2 | loop fusion | flops 98304 | bytes 393216 | tf_op jit(solution)/shard_map/convert_element_type | solution.py:714
  2.7 2.7 %collective-permute-start = (f32[45,8,128]{2,1,0:T(8,128)S(1)}, f32[45,8,128]{2,1,0:T(8,128)S(1)}, u32[]{:S(2)}, u32[]{:S(2)}) collective-permute-start(f32[45,8,128]{2,1,0:T(8,128)S(1)} %pad_maximum_fusion), channel_id=1, source_target_pairs={{0,16},{16,32},{32,48},{48,64},{64,80},{80,96},{96,112},{112,0},{1... | collective-permute-start | bytes 552968 | tf_op jit(solution)/shard_map/rows/ppermute | solution.py:700
  5.4 0.0 collective-permute-start.1
  5.4 0.0 copy-start.2
  5.4 2.6 %copy-done.2 = f32[22,2,256,128]{3,2,1,0:T(8,128)S(1)} copy-done((f32[22,2,256,128]{3,2,1,0:T(8,128)S(1)}, f32[22,2,256,128]{3,2,1,0:T(8,128)}, u32[]{:S(2)}) %copy-start.2) | copy-done | bytes 5767192
  8.1 0.0 copy-start.3
  8.1 0.9 %copy-done.3 = s32[256,128]{1,0:T(8,128)S(1)} copy-done((s32[256,128]{1,0:T(8,128)S(1)}, s32[256,128]{1,0:T(8,128)}, u32[]{:S(2)}) %copy-start.3) | copy-done | bytes 131096
  9.0 0.0 copy-start.4
  9.0 0.9 %copy-done.4 = s32[256,128]{1,0:T(8,128)S(1)} copy-done((s32[256,128]{1,0:T(8,128)S(1)}, s32[256,128]{1,0:T(8,128)}, u32[]{:S(2)}) %copy-start.4) | copy-done | bytes 131096
  9.9 0.0 copy-start.11
  9.9 0.0 copy-start.10
  9.9 3.8 %columns.2 = (f32[44,272,128]{2,1,0:T(8,128)S(1)}, s32[272,128]{1,0:T(8,128)S(1)}, f32[2,3,272,128]{3,2,1,0:T(8,128)S(1)}, f32[3,272,128]{2,1,0:T(8,128)S(1)}, f32[3,272,128]{2,1,0:T(8,128)S(1)}) custom-call(f32[44,256,128]{2,1,0:T(8,128)S(1)} %bitcast.11, s32[256,128]{1,0:T(8,128)S(1)} %copy-done.3, s32[256,128]{1,0:T(8,128)S(1)} %copy-done.4), custom_call_target="tpu_custom_call" | custom-call | flops 10000000 | bytes 7000000 | tf_op jit(solution)/shard_map/columns/pallas_call | solution.py:729
  13.7 0.0 collective-permute-done.top_ref
  13.7 0.0 collective-permute-done.1.bottom_ref
  13.7 0.2 columns.3
  14.0 0.0 copy-start
  14.0 2.6 %copy-done = f32[44,272,128]{2,1,0:T(8,128)} copy-done((f32[44,272,128]{2,1,0:T(8,128)}, f32[44,272,128]{2,1,0:T(8,128)S(1)}, u32[]{:S(2)}) %copy-start) | copy-done | bytes 6127640
  16.6 1.2 %collective-permute-start.2 = (f32[3,272,128]{2,1,0:T(8,128)S(1)}, f32[3,272,128]{2,1,0:T(8,128)S(1)}, u32[]{:S(2)}, u32[]{:S(2)}) collective-permute-start(f32[3,272,128]{2,1,0:T(8,128)S(1)} %get-tuple-element.32), channel_id=1, source_target_pairs={{0,1},{1,2},{2,3},{3,4},{4,5},{5,6},{6,7},{7,8},{8,9},{9,10},{10,1... | collective-permute-start | bytes 1253384 | tf_op jit(solution)/shard_map/columns/ppermute | solution.py:700
  17.8 4.7 %collective-permute-start.3 = (f32[3,272,128]{2,1,0:T(8,128)S(1)}, f32[3,272,128]{2,1,0:T(8,128)S(1)}, u32[]{:S(2)}, u32[]{:S(2)}) collective-permute-start(f32[3,272,128]{2,1,0:T(8,128)S(1)} %get-tuple-element.33), channel_id=1, source_target_pairs={{0,15},{1,0},{2,1},{3,2},{4,3},{5,4},{6,5},{7,6},{8,7},{9,8},{10,9... | collective-permute-start | bytes 1253384 | tf_op jit(solution)/shard_map/columns/ppermute | solution.py:700
  22.5 0.0 copy-done.11
  22.5 0.1 copy.16.mixing_ref
  22.6 0.0 copy-done.10
  22.6 0.0 copy-start.1
  22.6 2.7 %copy-done.1 = f32[44,272,128]{2,1,0:T(8,128)S(1)} copy-done((f32[44,272,128]{2,1,0:T(8,128)S(1)}, f32[44,272,128]{2,1,0:T(8,128)}, u32[]{:S(2)}) %copy-start.1) | copy-done | bytes 6127640
  25.4 14.7 %block.1 = (f32[44,256,128]{2,1,0:T(8,128)}, f32[272,128]{1,0:T(8,128)S(1)}, f32[272,128]{1,0:T(8,128)S(1)}) custom-call(f32[22,2]{1,0:T(8,128)S(1)} %copy.16.mixing_ref, f32[22]{0:T(128)S(1)} %copy-done.10, f32[44,272,128]{2,1,0:T(8,128)S(1)} %copy-done.1, s32[272,128]{1,0:T(8,128)S(1)} %get-tuple-element.28.eff_in), custom_call_target="tpu_custom_call" | custom-call | flops 50000000 | bytes 12000000 | tf_op jit(solution)/shard_map/block/pallas_call | solution.py:750
  40.0 0.0 collective-permute-done.2.from_left_ref
  40.0 0.0 copy-start.5
  40.0 0.8 %copy-done.5 = f32[3,272,128]{2,1,0:T(8,128)} copy-done((f32[3,272,128]{2,1,0:T(8,128)}, f32[3,272,128]{2,1,0:T(8,128)S(1)}, u32[]{:S(2)}) %copy-start.5) | copy-done | bytes 417816
  40.8 0.0 collective-permute-done.3.from_right_ref
  40.8 0.0 copy-start.7
  40.8 0.8 %copy-done.7 = f32[3,272,128]{2,1,0:T(8,128)} copy-done((f32[3,272,128]{2,1,0:T(8,128)}, f32[3,272,128]{2,1,0:T(8,128)S(1)}, u32[]{:S(2)}) %copy-start.7) | copy-done | bytes 417816
  41.6 0.0 copy-start.6
  41.6 1.0 %copy-done.6 = f32[3,272,128]{2,1,0:T(8,128)S(1)} copy-done((f32[3,272,128]{2,1,0:T(8,128)S(1)}, f32[3,272,128]{2,1,0:T(8,128)}, u32[]{:S(2)}) %copy-start.6) | copy-done | bytes 417816
  42.6 0.0 copy-start.8
  42.6 1.0 %copy-done.8 = f32[3,272,128]{2,1,0:T(8,128)S(1)} copy-done((f32[3,272,128]{2,1,0:T(8,128)S(1)}, f32[3,272,128]{2,1,0:T(8,128)}, u32[]{:S(2)}) %copy-start.8) | copy-done | bytes 417816
  43.6 14.1 %powers.1 = (f32[5,2,288,128]{3,2,1,0:T(8,128)S(1)}, f32[2,288,128]{2,1,0:T(8,128)S(1)}, f32[128,128]{1,0:T(8,128)S(1)}, f32[2,3,256,128]{3,2,1,0:T(8,128)S(1)}) custom-call(f32[22,2]{1,0:T(8,128)S(1)} %copy.16.mixing_ref, f32[22]{0:T(128)S(1)} %copy-done.10, f32[272,128]{1,0:T(8,128)S(1)} %get-tuple-element.30.fx_ref, ...), custom_call_target="tpu_custom_call" | custom-call | flops 50000000 | bytes 6000000 | tf_op jit(solution)/shard_map/powers/pallas_call | solution.py:767
  57.7 0.0 copy-start.9
  57.7 0.6 copy-done.9
  58.3 6.6 %all-to-all-start = ((f32[128,1,128]{2,1,0:T(1,128)}), f32[128,1,128]{2,1,0:T(1,128)S(1)}, u32[]{:S(2)}, u32[]{:S(2)}) async-start(f32[128,1,128]{2,1,0:T(1,128)} %bitcast.13), calls=%async_computation | async-start | bytes 131072 | tf_op jit(solution)/shard_map/sums/all_to_all | solution.py:799
  64.9 8.3 %patch.1 = f32[44,256,128]{2,1,0:T(8,128)} custom-call(f32[44,256,128]{2,1,0:T(8,128)} %get-tuple-element.29.new_in, f32[2,3,256,128]{3,2,1,0:T(8,128)S(1)} %get-tuple-element.35.edge_ref), custom_call_target="tpu_custom_call", output_to_operand_aliasing={{}: (0, {})} | custom-call | flops 10000000 | bytes 12000000 | tf_op jit(solution)/shard_map/patch/pallas_call | solution.py:801
  73.2 1.4 %all-to-all-done = f32[128,1,128]{2,1,0:T(1,128)S(1)} async-done(((f32[128,1,128]{2,1,0:T(1,128)}), f32[128,1,128]{2,1,0:T(1,128)S(1)}, u32[]{:S(2)}, u32[]{:S(2)}) %all-to-all-start) | async-done | bytes 65568 | tf_op jit(solution)/shard_map/sums/all_to_all | solution.py:799
  74.6 1.4 %surface.1 = (f32[256,128]{1,0:T(8,128)}, f32[2,256,128]{2,1,0:T(8,128)}) custom-call(f32[128,128]{1,0:T(8,128)S(1)} %bitcast.12, f32[5,2,288,128]{3,2,1,0:T(8,128)S(1)} %get-tuple-element.37.v_ref, f32[2,288,128]{2,1,0:T(8,128)S(1)} %get-tuple-element.38.d_ref), custom_call_target="tpu_custom_call" | custom-call | flops 1000000 | bytes 3000000 | tf_op jit(solution)/shard_map/surface/pallas_call | solution.py:811
  (3 shorter events, 0.0 us)
Async XLA Ops:
  2.7 11.0 %collective-permute-start = (f32[45,8,128]{2,1,0:T(8,128)S(1)}, f32[45,8,128]{2,1,0:T(8,128)S(1)}, u32[]{:S(2)}, u32[]{:S(2)}) collective-permute-start(f32[45,8,128]{2,1,0:T(8,128)S(1)} %pad_maximum_fusion), channel_id=1, source_target_pairs={{0,16},{16,32},{32,48},{48,64},{64,80},{80,96},{96,112},{112,0},{1... | collective-permute-start | bytes 552968 | tf_op jit(solution)/shard_map/rows/ppermute | solution.py:700
  5.4 8.3 %collective-permute-start.1 = (f32[45,8,128]{2,1,0:T(8,128)S(1)}, f32[45,8,128]{2,1,0:T(8,128)S(1)}, u32[]{:S(2)}, u32[]{:S(2)}) collective-permute-start(f32[45,8,128]{2,1,0:T(8,128)S(1)} %pad_maximum_fusion.1), channel_id=1, source_target_pairs={{0,112},{16,0},{32,16},{48,32},{64,48},{80,64},{96,80},{112,96},{1... | collective-permute-start | bytes 552968 | tf_op jit(solution)/shard_map/rows/ppermute | solution.py:700
  5.4 2.6 %copy-start.2 = (f32[22,2,256,128]{3,2,1,0:T(8,128)S(1)}, f32[22,2,256,128]{3,2,1,0:T(8,128)}, u32[]{:S(2)}) copy-start(f32[22,2,256,128]{3,2,1,0:T(8,128)} %param.5) | copy-start | bytes 17301508
  8.1 0.9 %copy-start.3 = (s32[256,128]{1,0:T(8,128)S(1)}, s32[256,128]{1,0:T(8,128)}, u32[]{:S(2)}) copy-start(s32[256,128]{1,0:T(8,128)} %levels_ref.1) | copy-start | bytes 393220
  9.0 0.9 %copy-start.4 = (s32[256,128]{1,0:T(8,128)S(1)}, s32[256,128]{1,0:T(8,128)}, u32[]{:S(2)}) copy-start(s32[256,128]{1,0:T(8,128)} %land_ref.1) | copy-start | bytes 393220
  9.9 12.6 %copy-start.11 = (f32[22,2]{0,1:T(2,128)S(1)}, f32[22,2]{0,1:T(2,128)}, u32[]{:S(2)}) copy-start(f32[22,2]{0,1:T(2,128)} %param.6) | copy-start | bytes 532
  9.9 12.7 %copy-start.10 = (f32[22]{0:T(128)S(1)}, f32[22]{0:T(128)}, u32[]{:S(2)}) copy-start(f32[22]{0:T(128)} %thick_ref.3) | copy-start | bytes 268
  14.0 2.6 %copy-start = (f32[44,272,128]{2,1,0:T(8,128)}, f32[44,272,128]{2,1,0:T(8,128)S(1)}, u32[]{:S(2)}) copy-start(f32[44,272,128]{2,1,0:T(8,128)S(1)} %get-tuple-element.27.ext_ref) | copy-start | bytes 18382852
  16.6 23.5 %collective-permute-start.2 = (f32[3,272,128]{2,1,0:T(8,128)S(1)}, f32[3,272,128]{2,1,0:T(8,128)S(1)}, u32[]{:S(2)}, u32[]{:S(2)}) collective-permute-start(f32[3,272,128]{2,1,0:T(8,128)S(1)} %get-tuple-element.32), channel_id=1, source_target_pairs={{0,1},{1,2},{2,3},{3,4},{4,5},{5,6},{6,7},{7,8},{8,9},{9,10},{10,1... | collective-permute-start | bytes 1253384 | tf_op jit(solution)/shard_map/columns/ppermute | solution.py:700
  17.8 23.0 %collective-permute-start.3 = (f32[3,272,128]{2,1,0:T(8,128)S(1)}, f32[3,272,128]{2,1,0:T(8,128)S(1)}, u32[]{:S(2)}, u32[]{:S(2)}) collective-permute-start(f32[3,272,128]{2,1,0:T(8,128)S(1)} %get-tuple-element.33), channel_id=1, source_target_pairs={{0,15},{1,0},{2,1},{3,2},{4,3},{5,4},{6,5},{7,6},{8,7},{9,8},{10,9... | collective-permute-start | bytes 1253384 | tf_op jit(solution)/shard_map/columns/ppermute | solution.py:700
  22.6 2.7 %copy-start.1 = (f32[44,272,128]{2,1,0:T(8,128)S(1)}, f32[44,272,128]{2,1,0:T(8,128)}, u32[]{:S(2)}) copy-start(f32[44,272,128]{2,1,0:T(8,128)} %copy-done) | copy-start | bytes 18382852
  40.0 0.8 %copy-start.5 = (f32[3,272,128]{2,1,0:T(8,128)}, f32[3,272,128]{2,1,0:T(8,128)S(1)}, u32[]{:S(2)}) copy-start(f32[3,272,128]{2,1,0:T(8,128)S(1)} %collective-permute-done.2.from_left_ref) | copy-start | bytes 1253380
  40.8 0.8 %copy-start.7 = (f32[3,272,128]{2,1,0:T(8,128)}, f32[3,272,128]{2,1,0:T(8,128)S(1)}, u32[]{:S(2)}) copy-start(f32[3,272,128]{2,1,0:T(8,128)S(1)} %collective-permute-done.3.from_right_ref) | copy-start | bytes 1253380
  41.6 1.0 %copy-start.6 = (f32[3,272,128]{2,1,0:T(8,128)S(1)}, f32[3,272,128]{2,1,0:T(8,128)}, u32[]{:S(2)}) copy-start(f32[3,272,128]{2,1,0:T(8,128)} %copy-done.5) | copy-start | bytes 1253380
  42.6 1.0 %copy-start.8 = (f32[3,272,128]{2,1,0:T(8,128)S(1)}, f32[3,272,128]{2,1,0:T(8,128)}, u32[]{:S(2)}) copy-start(f32[3,272,128]{2,1,0:T(8,128)} %copy-done.7) | copy-start | bytes 1253380
  57.7 0.6 copy-start.9
  58.3 16.3 %all-to-all-start = ((f32[128,1,128]{2,1,0:T(1,128)}), f32[128,1,128]{2,1,0:T(1,128)S(1)}, u32[]{:S(2)}, u32[]{:S(2)}) async-start(f32[128,1,128]{2,1,0:T(1,128)} %bitcast.13), calls=%async_computation | async-start | bytes 131072 | tf_op jit(solution)/shard_map/sums/all_to_all | solution.py:799

commit v3 on v2

--- a/solution.py
+++ b/solution.py
@@ -17,9 +17,10 @@
 TILES = 3
 LOADS = 4
 MOMENTS = 8
+PATCH_LEVELS = 2
 F32 = jnp.float32
 I32 = jnp.int32
-VMEM_LIMIT = 20 * 1024 * 1024
+VMEM_LIMIT = 48 * 1024 * 1024
 
 
 def lane_iota(rows):
@@ -50,6 +51,12 @@
     return jnp.where(land == 0, levels, 0)
 
 
+def extend_eff(ref, base, top_ref, bottom_ref, wet_ref):
+    ref[pl.ds(base, HALO)] = top_ref[2 * KL].astype(I32)
+    ref[pl.ds(base + HALO, ROWS)] = wet_ref[...].astype(I32)
+    ref[pl.ds(base + HALO + ROWS, HALO)] = bottom_ref[2 * KL].astype(I32)
+
+
 def edge_slot(k):
     return k % TILES, k // TILES
 
@@ -64,30 +71,30 @@
     return jnp.where(first, a, roll(b, 8)), jnp.where(first, roll(b, -8), a)
 
 
-def own_edges_kernel(t_ref, levels_ref, land_ref, ext_ref, eff_ref, edge_ref, right_ref, left_ref, sems):
+def own_edges_kernel(t_ref, wet_ref, edge_ref, right_ref, left_ref, own_ref, sems):
     parts = blocks(0, KL, -(-KL // LOADS))
 
     def copy(i):
         start, count = parts[i]
-        return pltpu.make_async_copy(
-            t_ref.at[pl.ds(2 * start, 2 * count)],
-            ext_ref.at[pl.ds(2 * start, 2 * count), pl.ds(HALO, ROWS)],
-            sems.at[i],
-        )
+        planes = pl.ds(2 * start, 2 * count)
+        return pltpu.make_async_copy(t_ref.at[planes], own_ref.at[planes], sems.at[i])
 
     for i in range(len(parts)):
         copy(i).start()
-    eff_ref[pl.ds(HALO, ROWS)] = wet_levels(levels_ref[...], land_ref[...])
     size = 64
     tile_eff, _ = edge_slot(KL)
 
+    def rows_of(step):
+        own = pl.ds(pl.multiple_of(size * step, 8), size)
+        return own, pl.ds(pl.multiple_of(HALO + size * step, 8), size)
+
     def clear(step, carry):
-        at = pl.ds(pl.multiple_of(HALO + size * step, 8), size)
+        own, at = rows_of(step)
         zero = jnp.zeros((size, LANES), F32)
         for c in range(2):
             for tile in range(TILES):
                 edge_ref[c, tile, at] = zero
-            edge_ref[c, tile_eff, at] = place(eff_ref[at].astype(F32), KL, zero)
+            edge_ref[c, tile_eff, at] = place(wet_ref[own], KL, zero)
         return carry
 
     lax.fori_loop(0, ROWS // size, clear, 0)
@@ -95,17 +102,17 @@
         copy(i).wait()
 
         def rows(step, carry):
-            at = pl.ds(pl.multiple_of(HALO + size * step, 8), size)
+            own, at = rows_of(step)
             for k in range(start, start + count):
                 tile, _ = edge_slot(k)
                 for c in range(2):
-                    edge_ref[c, tile, at] = place(ext_ref[2 * k + c, at], k, edge_ref[c, tile, at])
+                    edge_ref[c, tile, at] = place(own_ref[2 * k + c, own], k, edge_ref[c, tile, at])
             return carry
 
         lax.fori_loop(0, ROWS // size, rows, 0)
 
     def send(step, carry):
-        at = pl.ds(pl.multiple_of(HALO + size * step, 8), size)
+        _, at = rows_of(step)
         for tile in range(TILES):
             right_ref[tile, at], left_ref[tile, at] = to_neighbours(edge_ref[0, tile, at], edge_ref[1, tile, at])
         return carry
@@ -113,22 +120,14 @@
     lax.fori_loop(0, ROWS // size, send, 0)
 
 
-def halo_edges_kernel(
-    top_ref, bottom_ref, ext_in, eff_in, edge_in, right_in, left_in, ext_ref, eff_ref, edge_ref, right_ref, left_ref
-):
+def halo_edges_kernel(top_ref, bottom_ref, edge_in, right_in, left_in, edge_ref, right_ref, left_ref):
     for r0, ref in ((0, top_ref), (HALO + ROWS, bottom_ref)):
         at = pl.ds(r0, HALO)
-        eff = ref[2 * KL]
-        eff_ref[at] = eff.astype(I32)
         held = [[jnp.zeros((HALO, LANES), F32) for _ in range(TILES)] for _ in range(2)]
         for k in range(KL + 1):
             tile, _ = edge_slot(k)
             for c in range(2):
-                if k < KL:
-                    x = ref[2 * k + c]
-                    ext_ref[2 * k + c, at] = x
-                else:
-                    x = eff
+                x = ref[2 * k + c] if k < KL else ref[2 * KL]
                 held[c][tile] = place(x, k, held[c][tile])
         for tile in range(TILES):
             for c in range(2):
@@ -154,20 +153,44 @@
 def block_kernel(
     mixing_ref,
     thick_ref,
-    ext_ref,
-    eff_in,
+    t_ref,
+    top_ref,
+    bottom_ref,
+    wet_ref,
     new_ref,
     fx_ref,
     fy_ref,
+    ext_ref,
     eff_ref,
     min_ref,
     word_ref,
     u_ref,
     l_ref,
     acc_ref,
+    in_sems,
+    out_sems,
 ):
+    def held(k):
+        return ext_ref.at[pl.ds(2 * k, 2), pl.ds(HALO, ROWS)]
+
+    def load(k):
+        return pltpu.make_async_copy(t_ref.at[pl.ds(2 * k, 2)], held(k), in_sems.at[k])
+
+    def store(k):
+        return pltpu.make_async_copy(held(k), new_ref.at[pl.ds(2 * k, 2)], out_sems.at[k])
+
+    def each(body):
+        def step(k, carry):
+            body(k)
+            return carry
+
+        lax.fori_loop(0, KL, step, 0)
+
+    each(lambda k: load(k).start())
     eff_ref[...] = jnp.zeros(eff_ref.shape, I32)
-    eff_ref[pl.ds(PAD, EXT)] = eff_in[...]
+    extend_eff(eff_ref, PAD, top_ref, bottom_ref, wet_ref)
+    ext_ref[:, pl.ds(0, HALO)] = top_ref[pl.ds(0, 2 * KL)]
+    ext_ref[:, pl.ds(HALO + ROWS, HALO)] = bottom_ref[pl.ds(0, 2 * KL)]
     for ref in (u_ref, l_ref, acc_ref, fx_ref, fy_ref):
         ref[...] = jnp.zeros(ref.shape, F32)
     for r0, n in CHUNKS:
@@ -189,10 +212,19 @@
         return k, jnp.where(valid, thick_ref[k], 0.0)
 
     def body(step, carry):
+        @pl.when(step < KL)
+        def _():
+            load(step).wait()
+
+        @pl.when(step >= 4)
+        def _():
+            store(step - 4).start()
+
         ku, _ = stage(step, 0)
         kl, _ = stage(step, 1)
         kd, thick_d = stage(step, 2)
         kf, thick_f = stage(step, 3)
+        mix = [jnp.where(step < KL + 2, mixing_ref[kd, c], 0.0) for c in range(2)]
 
         def flux(r0, n):
             here = acc_ref[pl.ds(PAD + r0, n)]
@@ -209,9 +241,9 @@
             for c in range(2):
                 x, around = neighbours(l_ref.at[c], r0, n)
                 second = jnp.where(wet, around, 0.0) - number * x
-                value = ext_ref[2 * kd + c, pl.ds(r0, n)] - mixing_ref[kd, c] * second
+                value = ext_ref[2 * kd + c, pl.ds(r0, n)] - mix[c] * second
                 low, high = max(r0, HALO), min(r0 + n, HALO + ROWS)
-                new_ref[2 * kd + c, pl.ds(low - HALO, high - low)] = value[low - r0 : high - r0]
+                ext_ref[2 * kd + c, pl.ds(low, high - low)] = value[low - r0 : high - r0]
                 new.append(value)
             plain = 0.8 * new[1] - 0.2 * new[0]
             acc_ref[pl.ds(PAD + r0, n)] += thick_d * jnp.where(wet, plain, 0.0)
@@ -236,24 +268,22 @@
         return carry
 
     lax.fori_loop(0, KL + 3, body, 0)
+    store(KL - 1).start()
+    each(lambda k: store(k).wait())
 
 
 def patch_kernel(new_in, edge_ref, new_ref):
-    size = 32
-
-    def level(k, carry):
+    for part in range(PATCH_LEVELS):
+        k = pl.program_id(0) * PATCH_LEVELS + part
         tile = k % TILES
         back = (2 * LANES - 8 - GROUP * (k // TILES)) % LANES
-        for r0, n in blocks(0, ROWS, size):
+        for r0, n in blocks(0, ROWS, 64):
             lane = lane_iota(n)
             middle = jnp.logical_and(lane >= 4, lane < LANES - 4)
             own = pl.ds(r0, n)
             for c in range(2):
                 edge = pltpu.roll(edge_ref[c, tile, own], back, 1)
-                new_ref[2 * k + c, own] = jnp.where(middle, new_in[2 * k + c, own], edge)
-        return carry
-
-    lax.fori_loop(0, KL, level, 0)
+                new_ref[2 * part + c, own] = jnp.where(middle, new_in[2 * part + c, own], edge)
 
 
 def two_sum(a, b):
@@ -335,7 +365,9 @@
     from_left_ref,
     from_right_ref,
     edge_ref,
-    eff_in,
+    top_ref,
+    bottom_ref,
+    wet_ref,
     v_ref,
     d_ref,
     sums_ref,
@@ -473,11 +505,15 @@
                 run = run + layers[tile]
                 acc_ref[side, tile, at] = run
     thick = [by_group(tile, lambda k: thick_ref[k]) for tile in range(TILES)]
-    for r0, n in CHUNKS:
+    extend_eff(eff_ref.at[0], 0, top_ref, bottom_ref, wet_ref)
+    table = jnp.zeros((8, LANES), F32)
+    for k in range(KL):
+        table += jnp.where(lane_iota(8) > k, thick_ref[k], 0.0)
+    for r0, n in blocks(0, EXT, EXT // 2):
         lane = lane_iota(n)
         own = pl.ds(r0, n)
         at = pl.ds(PAD + r0, n)
-        totals = []
+        faces = []
         for side in SIDES:
             e = e_ref[side, at]
             min_x = jnp.minimum(e, e_ref[side, pl.ds(PAD + r0 - 1, n)])
@@ -490,30 +526,22 @@
                 level_of = level_lanes(tile)
                 face_x += thick[tile] * jnp.where(min_x > level_of, here - up, 0.0)
                 face_y += thick[tile] * jnp.where(min_y > level_of, here - roll(here, 1), 0.0)
-            totals.append([roll(group_totals(x), 8) for x in (face_x, face_y)])
+            faces += [face_x, face_y]
+        for shift in (GROUP, 2 * GROUP, 4 * GROUP):
+            faces = [x + roll(x, shift) for x in faces]
+        faces = [roll(x, 8) for x in faces]
         for full, main, west, east in (
-            (full_fx_ref, fx_ref, totals[0][0], totals[1][0]),
-            (full_fy_ref, fy_ref, totals[0][1], totals[1][1]),
+            (full_fx_ref, fx_ref, faces[0], faces[2]),
+            (full_fy_ref, fy_ref, faces[1], faces[3]),
         ):
             full[0, at] = jnp.where(lane < 4, west, jnp.where(lane >= LANES - 4, east, main[own]))
             full[1, at] = jnp.where(lane < 8, east, jnp.where(lane >= LANES - 8, west, 0.0))
         west = roll(e_ref[0, at], 8)
         east = roll(e_ref[1, at], 8)
-        eff_ref[0, own] = eff_in[own]
         eff_ref[1, own] = jnp.where(lane < 8, east, jnp.where(lane >= LANES - 8, west, 0))
-
-    def depths(step, carry):
-        n = 16
-        r0 = pl.multiple_of(step * n, 8)
-        for t in range(2):
-            e = eff_ref[t, pl.ds(r0, n)]
-            d = jnp.zeros((n, LANES), F32)
-            for k in range(KL):
-                d += jnp.where(e > k, thick_ref[k], 0.0)
-            d_ref[t, pl.ds(pl.multiple_of(PAD + r0, 8), n)] = d
-        return carry
-
-    lax.fori_loop(0, EXT // 16, depths, 0)
+    for t in range(2):
+        for r0, n in blocks(0, EXT, 8):
+            d_ref[t, pl.ds(PAD + r0, n)] = jnp.take_along_axis(table, eff_ref[t, pl.ds(r0, n)], axis=1)
     for r0, n in CHUNKS:
         here = pl.ds(PAD + r0, n)
         d_main, d_side = d_ref[0, here], d_ref[1, here]
@@ -604,13 +632,14 @@
             other = tuple(jnp.where(upper, pltpu.roll(x, 8 - half, 0), pltpu.roll(y, half, 0)) for x, y in zip(a, b))
             merged.append(pair_add(keep, other))
         pairs = merged
-    total = pairs[0]
-    for shift in (1, 2, 4, 8, 16, 32, 64):
-        total = pair_add(total, tuple(roll(x, shift) for x in total))
-    lane = lane_iota(8)
-    row = jnp.where(lane == sub, total[0], jnp.where(lane == sub + MOMENTS, total[1], 0.0))
+    wide = [jnp.concatenate([x, jnp.zeros((LANES - 8, LANES), F32)]).T for x in pairs[0]]
+    rows = [tuple(x[at : at + 8] for x in wide) for at in range(0, LANES, 8)]
+    while len(rows) > 1:
+        rows = [pair_add(rows[i], rows[i + 1]) for i in range(0, len(rows), 2)]
+    total = rows[0]
     for shift in (4, 2, 1):
-        row = row + pltpu.roll(row, shift, 0)
+        total = pair_add(total, tuple(pltpu.roll(x, shift, 0) for x in total))
+    row = total[0] + roll(total[1], MOMENTS)
     for at in range(0, sums_ref.shape[0], 8):
         sums_ref[pl.ds(at, 8)] = row
 
@@ -684,7 +713,7 @@
 
 VM = pl.BlockSpec(memory_space=pltpu.VMEM)
 SM = pl.BlockSpec(memory_space=pltpu.SMEM)
-ANY = pl.BlockSpec(memory_space=pl.ANY)
+HBM = pl.BlockSpec(memory_space=pltpu.HBM)
 
 
 def params(**kwargs):
@@ -719,28 +748,22 @@
         top = ring(to_down, "bx", 1)
         bottom = ring(to_up, "bx", -1)
     with jax.named_scope("columns"):
-        edges = (
-            shape(planes, EXT, LANES),
-            shape(EXT, LANES, dtype=I32),
-            shape(2, TILES, EXT, LANES),
-            shape(TILES, EXT, LANES),
-            shape(TILES, EXT, LANES),
-        )
+        edges = (shape(2, TILES, EXT, LANES), shape(TILES, EXT, LANES), shape(TILES, EXT, LANES))
         own = pl.pallas_call(
             own_edges_kernel,
             out_shape=edges,
-            in_specs=[ANY, VM, VM],
-            out_specs=(VM,) * 5,
-            scratch_shapes=[pltpu.SemaphoreType.DMA((LOADS,))],
+            in_specs=[HBM, VM],
+            out_specs=(VM,) * 3,
+            scratch_shapes=[scratch(planes, rows=ROWS), pltpu.SemaphoreType.DMA((LOADS,))],
             compiler_params=params(),
             cost_estimate=cost(10_000_000, 7_000_000),
-        )(flat, levels, land)
-        ext, eff, edge, to_right, to_left = pl.pallas_call(
+        )(flat, wet)
+        edge, to_right, to_left = pl.pallas_call(
             halo_edges_kernel,
             out_shape=edges,
-            in_specs=[VM] * 7,
-            out_specs=(VM,) * 5,
-            input_output_aliases={i + 2: i for i in range(5)},
+            in_specs=[VM] * 5,
+            out_specs=(VM,) * 3,
+            input_output_aliases={i + 2: i for i in range(3)},
             compiler_params=params(),
             cost_estimate=cost(1_000_000, 700_000),
         )(top, bottom, *own)
@@ -750,19 +773,22 @@
         new, fx, fy = pl.pallas_call(
             block_kernel,
             out_shape=(shape(planes, ROWS, LANES), shape(EXT, LANES), shape(EXT, LANES)),
-            in_specs=[SM, SM, VM, VM],
-            out_specs=(VM,) * 3,
+            in_specs=[SM, SM, HBM, VM, VM, VM],
+            out_specs=(HBM, VM, VM),
             scratch_shapes=[
+                scratch(planes, rows=EXT),
                 scratch(dtype=I32),
                 scratch(2, rows=EXT, dtype=I32),
                 scratch(3, rows=EXT, dtype=I32),
                 scratch(2),
                 scratch(2),
                 scratch(),
+                pltpu.SemaphoreType.DMA((KL,)),
+                pltpu.SemaphoreType.DMA((KL,)),
             ],
             compiler_params=params(),
             cost_estimate=cost(50_000_000, 12_000_000),
-        )(mixing, thickness, ext, eff)
+        )(mixing, thickness, flat, top, bottom, wet)
     with jax.named_scope("powers"):
         powers, depth, sums, new_edge = pl.pallas_call(
             solve_kernel,
@@ -772,7 +798,7 @@
                 shape(devices, LANES),
                 shape(2, TILES, ROWS, LANES),
             ),
-            in_specs=[SM, SM] + [VM] * 6,
+            in_specs=[SM, SM] + [VM] * 8,
             out_specs=(VM,) * 4,
             scratch_shapes=[
                 scratch(2, dtype=I32),
@@ -794,15 +820,17 @@
             ],
             compiler_params=params(),
             cost_estimate=cost(50_000_000, 6_000_000),
-        )(mixing, thickness, fx, fy, from_left, from_right, edge, eff)
+        )(mixing, thickness, fx, fy, from_left, from_right, edge, top, bottom, wet)
     with jax.named_scope("sums"):
         everyone = lax.all_to_all(sums, ("bx", "by"), 0, 0, tiled=True)
     with jax.named_scope("patch"):
+        level_block = pl.BlockSpec((2 * PATCH_LEVELS, ROWS, LANES), lambda i: (i, 0, 0))
         tracers_new = pl.pallas_call(
             patch_kernel,
+            grid=(KL // PATCH_LEVELS,),
             out_shape=shape(planes, ROWS, LANES),
-            in_specs=[VM, VM],
-            out_specs=VM,
+            in_specs=[level_block, VM],
+            out_specs=level_block,
             input_output_aliases={0: 0},
             compiler_params=params(),
             cost_estimate=cost(10_000_000, 12_000_000),

time: 76.5 us -> 61.2 us (0.80)
  local copies, waits for them, and re-layouts: 15.1 us -> 5.55 us
  Pallas kernels: 42.5 us -> 38 us
  waiting for transfers between devices: 1.41 us -> 0.45 us
    unnamed x25 -> x15, local copies, waits for them, and re-layouts: 14 us -> 4.51 us
    pallas_call x1, Pallas kernels: 14.1 us -> 9.19 us  [shards(): pl.pallas_call(solve_kernel, out_shape=(shape(5, 2, BUF, LANES), shape(2,...]
    pallas_call x3, Pallas kernels: 12.4 us -> 14.3 us  [the longest x1 9.62 us: shards(): pl.pallas_call(patch_kernel, grid=(KL // PATCH_LEVELS,), out_shape=shape(...]
    pallas_call x1, Pallas kernels: 14.7 us -> 13.1 us  [shards(): pl.pallas_call(block_kernel, out_shape=(shape(planes, ROWS, LANES), shape...]
    all_to_all x1, waiting for transfers between devices: 1.4 us -> 0.01 us  [shards(): everyone = lax.all_to_all(sums, ('bx', 'by'), 0, 0, tiled=True)]
  transfers between devices with their start and end apart: 5 -> 5, of which waited for: 1 -> 1; matrix products, arithmetic and copies ran while one was open for 0% -> 0% of each run, Pallas kernels for 35% -> 45%
where the time goes in v3:
time: 61.2 us; the launch traced here: 60.7 us
  Pallas kernels  38 us (62%)
  starting transfers between devices  14.9 us (24%)
  local copies, waits for them, and re-layouts  5.55 us (9%)
  other arithmetic  1.02 us (2%)
  between operations  0.75 us (1%)
    pallas_call x1, Pallas kernels, shards(): pl.pallas_call(block_kernel, out_shape=(shape(planes, ROWS, LANES), shape...  13.1 us
    pallas_call x1, Pallas kernels, shards(): pl.pallas_call(patch_kernel, grid=(KL // PATCH_LEVELS,), out_shape=shape(...  9.62 us
    pallas_call x1, Pallas kernels, shards(): pl.pallas_call(solve_kernel, out_shape=(shape(5, 2, BUF, LANES), shape(2,...  9.19 us
    ppermute x4, starting transfers between devices, ring(): lax.ppermute(x, axis, [(i, (i + step) % count) for i in range(count)])  8.82 us
    all_to_all x1, starting transfers between devices, shards(): everyone = lax.all_to_all(sums, ('bx', 'by'), 0, 0, tiled=True)  6.1 us
    unnamed x15, local copies, waits for them, and re-layouts  4.51 us
    pallas_call x1, Pallas kernels, shards(): pl.pallas_call(own_edges_kernel, out_shape=edges, in_specs=[HBM, VM], out...  4.49 us
    pallas_call x1, Pallas kernels, shards(): pl.pallas_call(finish_kernel, out_shape=(shape(ROWS, LANES), shape(2, ROW...  1.44 us
  transfers between devices with their start and end apart: 5, of which 1 were waited for; matrix products, arithmetic and copies ran while one was open for 0% of the time, Pallas kernels for 45%

profile of v3, /device:TPU:1, one launch (start us, length us, event | category | flops | bytes accessed | tf_op | source)
XLA Modules:
  0.0 60.7 jit_solution(2525543449901541164)
XLA Ops:
  0.6 0.0 copy-start.6
  0.6 0.0 copy-start.5
  0.7 1.0 %select_convert_fusion.wet_ref = f32[256,128]{1,0:T(8,128)S(1)} fusion(s32[256,128]{1,0:T(8,128)} %param.8, s32[256,128]{1,0:T(8,128)} %param.9), kind=kLoop, calls=%fused_computation.2 | loop fusion | flops 98304 | bytes 393216 | tf_op jit(solution)/shard_map/convert_element_type | solution.py:743
  1.7 1.0 %fusion = (f32[44,8,128]{2,1,0:T(8,128)S(1)}, f32[44,8,128]{2,1,0:T(8,128)S(1)}) fusion(f32[44,256,128]{2,1,0:T(8,128)} %bitcast.12), kind=kLoop, calls=%fused_computation.5 | loop fusion | bytes 720896 | tf_op jit(solution)/shard_map/rows/slice | solution.py:746
  2.7 2.7 %collective-permute-start = (f32[45,8,128]{2,1,0:T(8,128)S(1)}, f32[45,8,128]{2,1,0:T(8,128)S(1)}, u32[]{:S(2)}, u32[]{:S(2)}) collective-permute-start(f32[45,8,128]{2,1,0:T(8,128)S(1)} %pad_maximum_fusion), channel_id=1, source_target_pairs={{0,16},{16,32},{32,48},{48,64},{64,80},{80,96},{96,112},{112,0},{1... | collective-permute-start | bytes 552968 | tf_op jit(solution)/shard_map/rows/ppermute | solution.py:729
  5.4 0.0 collective-permute-start.1
  5.5 4.5 %columns.2 = (f32[2,3,272,128]{3,2,1,0:T(8,128)S(1)}, f32[3,272,128]{2,1,0:T(8,128)S(1)}, f32[3,272,128]{2,1,0:T(8,128)S(1)}) custom-call(f32[44,256,128]{2,1,0:T(8,128)} %bitcast.13, f32[256,128]{1,0:T(8,128)S(1)} %select_convert_fusion.wet_ref), custom_call_target="tpu_custom_call" | custom-call | flops 10000000 | bytes 7000000 | tf_op jit(solution)/shard_map/columns/pallas_call | solution.py:752
  10.0 0.0 collective-permute-done.top_ref
  10.0 0.4 collective-permute-done.1.bottom_ref
  10.4 0.2 columns.3
  10.6 1.3 %collective-permute-start.2 = (f32[3,272,128]{2,1,0:T(8,128)S(1)}, f32[3,272,128]{2,1,0:T(8,128)S(1)}, u32[]{:S(2)}, u32[]{:S(2)}) collective-permute-start(f32[3,272,128]{2,1,0:T(8,128)S(1)} %get-tuple-element.24), channel_id=1, source_target_pairs={{0,1},{1,2},{2,3},{3,4},{4,5},{5,6},{6,7},{7,8},{8,9},{9,10},{10,1... | collective-permute-start | bytes 1253384 | tf_op jit(solution)/shard_map/columns/ppermute | solution.py:729
  11.9 4.8 %collective-permute-start.3 = (f32[3,272,128]{2,1,0:T(8,128)S(1)}, f32[3,272,128]{2,1,0:T(8,128)S(1)}, u32[]{:S(2)}, u32[]{:S(2)}) collective-permute-start(f32[3,272,128]{2,1,0:T(8,128)S(1)} %get-tuple-element.25), channel_id=1, source_target_pairs={{0,15},{1,0},{2,1},{3,2},{4,3},{5,4},{6,5},{7,6},{8,7},{9,8},{10,9... | collective-permute-start | bytes 1253384 | tf_op jit(solution)/shard_map/columns/ppermute | solution.py:729
  16.7 0.0 copy-done.6
  16.7 0.1 copy.14.mixing_ref
  16.8 0.0 copy-done.5
  16.8 13.1 %block.1 = (f32[44,256,128]{2,1,0:T(8,128)}, f32[272,128]{1,0:T(8,128)S(1)}, f32[272,128]{1,0:T(8,128)S(1)}) custom-call(f32[22,2]{1,0:T(8,128)S(1)} %copy.14.mixing_ref, f32[22]{0:T(128)S(1)} %copy-done.5, f32[44,256,128]{2,1,0:T(8,128)} %bitcast.14, f32[45,8,128]{2,1,0:T(8,128)S(1)} %collective-permute-done.top_ref, ...), custom_call_target="tpu_custom_call" | custom-call | flops 50000000 | bytes 12000000 | tf_op jit(solution)/shard_map/block/pallas_call | solution.py:773
  29.9 0.0 collective-permute-done.2.from_left_ref
  29.9 0.0 collective-permute-done.3.from_right_ref
  29.9 0.0 copy-start.2
  29.9 0.8 %copy-done.2 = f32[3,272,128]{2,1,0:T(8,128)} copy-done((f32[3,272,128]{2,1,0:T(8,128)}, f32[3,272,128]{2,1,0:T(8,128)S(1)}, u32[]{:S(2)}) %copy-start.2) | copy-done | bytes 417816
  30.7 0.0 copy-start.3
  30.7 1.0 %copy-done.3 = f32[3,272,128]{2,1,0:T(8,128)S(1)} copy-done((f32[3,272,128]{2,1,0:T(8,128)S(1)}, f32[3,272,128]{2,1,0:T(8,128)}, u32[]{:S(2)}) %copy-start.3) | copy-done | bytes 417816
  31.7 9.2 %powers.1 = (f32[5,2,288,128]{3,2,1,0:T(8,128)S(1)}, f32[2,288,128]{2,1,0:T(8,128)S(1)}, f32[128,128]{1,0:T(8,128)S(1)}, f32[2,3,256,128]{3,2,1,0:T(8,128)S(1)}) custom-call(f32[22,2]{1,0:T(8,128)S(1)} %copy.14.mixing_ref, f32[22]{0:T(128)S(1)} %copy-done.5, f32[272,128]{1,0:T(8,128)S(1)} %get-tuple-element.19.fx_ref, ...), custom_call_target="tpu_custom_call" | custom-call | flops 50000000 | bytes 6000000 | tf_op jit(solution)/shard_map/powers/pallas_call | solution.py:793
  40.9 0.0 copy-start
  40.9 0.9 %copy-done = f32[2,3,256,128]{3,2,1,0:T(8,128)} copy-done((f32[2,3,256,128]{3,2,1,0:T(8,128)}, f32[2,3,256,128]{3,2,1,0:T(8,128)S(1)}, u32[]{:S(2)}) %copy-start) | copy-done | bytes 786456
  41.8 0.0 copy-start.4
  41.8 0.6 %copy-done.4 = f32[128,128]{1,0:T(8,128)} copy-done((f32[128,128]{1,0:T(8,128)}, f32[128,128]{1,0:T(8,128)S(1)}, u32[]{:S(2)}) %copy-start.4) | copy-done | bytes 65560
  42.4 6.1 %all-to-all-start = ((f32[128,1,128]{2,1,0:T(1,128)}), f32[128,1,128]{2,1,0:T(1,128)S(1)}, u32[]{:S(2)}, u32[]{:S(2)}) async-start(f32[128,1,128]{2,1,0:T(1,128)} %bitcast.11), calls=%async_computation | async-start | bytes 131072 | tf_op jit(solution)/shard_map/sums/all_to_all | solution.py:825
  48.5 0.0 copy-start.1
  48.5 1.1 %copy-done.1 = f32[2,3,256,128]{3,2,1,0:T(8,128)S(1)} copy-done((f32[2,3,256,128]{3,2,1,0:T(8,128)S(1)}, f32[2,3,256,128]{3,2,1,0:T(8,128)}, u32[]{:S(2)}) %copy-start.1) | copy-done | bytes 786456
  49.6 9.6 %patch.1 = f32[44,256,128]{2,1,0:T(8,128)} custom-call(f32[44,256,128]{2,1,0:T(8,128)} %get-tuple-element.18.new_in, f32[2,3,256,128]{3,2,1,0:T(8,128)S(1)} %copy-done.1), custom_call_target="tpu_custom_call", output_to_operand_aliasing={{}: (0, {})} | custom-call | flops 10000000 | bytes 12000000 | tf_op jit(solution)/shard_map/patch/pallas_call | solution.py:828
  59.3 0.0 all-to-all-done
  59.3 1.4 %surface.1 = (f32[256,128]{1,0:T(8,128)}, f32[2,256,128]{2,1,0:T(8,128)}) custom-call(f32[128,128]{1,0:T(8,128)S(1)} %bitcast.10, f32[5,2,288,128]{3,2,1,0:T(8,128)S(1)} %get-tuple-element.29.v_ref, f32[2,288,128]{2,1,0:T(8,128)S(1)} %get-tuple-element.30.d_ref), custom_call_target="tpu_custom_call" | custom-call | flops 1000000 | bytes 3000000 | tf_op jit(solution)/shard_map/surface/pallas_call | solution.py:839
  (3 shorter events, 0.0 us)
Async XLA Ops:
  0.6 16.1 %copy-start.6 = (f32[22,2]{0,1:T(2,128)S(1)}, f32[22,2]{0,1:T(2,128)}, u32[]{:S(2)}) copy-start(f32[22,2]{0,1:T(2,128)} %param.6) | copy-start | bytes 532
  0.6 16.2 %copy-start.5 = (f32[22]{0:T(128)S(1)}, f32[22]{0:T(128)}, u32[]{:S(2)}) copy-start(f32[22]{0:T(128)} %thick_ref.3) | copy-start | bytes 268
  2.7 7.2 %collective-permute-start = (f32[45,8,128]{2,1,0:T(8,128)S(1)}, f32[45,8,128]{2,1,0:T(8,128)S(1)}, u32[]{:S(2)}, u32[]{:S(2)}) collective-permute-start(f32[45,8,128]{2,1,0:T(8,128)S(1)} %pad_maximum_fusion), channel_id=1, source_target_pairs={{0,16},{16,32},{32,48},{48,64},{64,80},{80,96},{96,112},{112,0},{1... | collective-permute-start | bytes 552968 | tf_op jit(solution)/shard_map/rows/ppermute | solution.py:729
  5.4 5.0 %collective-permute-start.1 = (f32[45,8,128]{2,1,0:T(8,128)S(1)}, f32[45,8,128]{2,1,0:T(8,128)S(1)}, u32[]{:S(2)}, u32[]{:S(2)}) collective-permute-start(f32[45,8,128]{2,1,0:T(8,128)S(1)} %pad_maximum_fusion.1), channel_id=1, source_target_pairs={{0,112},{16,0},{32,16},{48,32},{64,48},{80,64},{96,80},{112,96},{1... | collective-permute-start | bytes 552968 | tf_op jit(solution)/shard_map/rows/ppermute | solution.py:729
  10.6 19.3 %collective-permute-start.2 = (f32[3,272,128]{2,1,0:T(8,128)S(1)}, f32[3,272,128]{2,1,0:T(8,128)S(1)}, u32[]{:S(2)}, u32[]{:S(2)}) collective-permute-start(f32[3,272,128]{2,1,0:T(8,128)S(1)} %get-tuple-element.24), channel_id=1, source_target_pairs={{0,1},{1,2},{2,3},{3,4},{4,5},{5,6},{6,7},{7,8},{8,9},{9,10},{10,1... | collective-permute-start | bytes 1253384 | tf_op jit(solution)/shard_map/columns/ppermute | solution.py:729
  11.9 18.0 %collective-permute-start.3 = (f32[3,272,128]{2,1,0:T(8,128)S(1)}, f32[3,272,128]{2,1,0:T(8,128)S(1)}, u32[]{:S(2)}, u32[]{:S(2)}) collective-permute-start(f32[3,272,128]{2,1,0:T(8,128)S(1)} %get-tuple-element.25), channel_id=1, source_target_pairs={{0,15},{1,0},{2,1},{3,2},{4,3},{5,4},{6,5},{7,6},{8,7},{9,8},{10,9... | collective-permute-start | bytes 1253384 | tf_op jit(solution)/shard_map/columns/ppermute | solution.py:729
  29.9 0.8 %copy-start.2 = (f32[3,272,128]{2,1,0:T(8,128)}, f32[3,272,128]{2,1,0:T(8,128)S(1)}, u32[]{:S(2)}) copy-start(f32[3,272,128]{2,1,0:T(8,128)S(1)} %collective-permute-done.3.from_right_ref) | copy-start | bytes 1253380
  30.7 1.0 %copy-start.3 = (f32[3,272,128]{2,1,0:T(8,128)S(1)}, f32[3,272,128]{2,1,0:T(8,128)}, u32[]{:S(2)}) copy-start(f32[3,272,128]{2,1,0:T(8,128)} %copy-done.2) | copy-start | bytes 1253380
  40.9 0.9 %copy-start = (f32[2,3,256,128]{3,2,1,0:T(8,128)}, f32[2,3,256,128]{3,2,1,0:T(8,128)S(1)}, u32[]{:S(2)}) copy-start(f32[2,3,256,128]{3,2,1,0:T(8,128)S(1)} %get-tuple-element.27.edge_ref) | copy-start | bytes 2359300
  41.8 0.6 %copy-start.4 = (f32[128,128]{1,0:T(8,128)}, f32[128,128]{1,0:T(8,128)S(1)}, u32[]{:S(2)}) copy-start(f32[128,128]{1,0:T(8,128)S(1)} %get-tuple-element.28) | copy-start | bytes 196612
  42.4 16.9 %all-to-all-start = ((f32[128,1,128]{2,1,0:T(1,128)}), f32[128,1,128]{2,1,0:T(1,128)S(1)}, u32[]{:S(2)}, u32[]{:S(2)}) async-start(f32[128,1,128]{2,1,0:T(1,128)} %bitcast.11), calls=%async_computation | async-start | bytes 131072 | tf_op jit(solution)/shard_map/sums/all_to_all | solution.py:825
  48.5 1.1 %copy-start.1 = (f32[2,3,256,128]{3,2,1,0:T(8,128)S(1)}, f32[2,3,256,128]{3,2,1,0:T(8,128)}, u32[]{:S(2)}) copy-start(f32[2,3,256,128]{3,2,1,0:T(8,128)} %copy-done) | copy-start | bytes 2359300

commit v4 on v3

--- a/solution.py
+++ b/solution.py
@@ -17,10 +17,12 @@
 TILES = 3
 LOADS = 4
 MOMENTS = 8
-PATCH_LEVELS = 2
+PATCH = 2
+GRAVITY = 10.0
+SEEN = HALO + ROWS
 F32 = jnp.float32
 I32 = jnp.int32
-VMEM_LIMIT = 48 * 1024 * 1024
+MIB = 1024 * 1024
 
 
 def lane_iota(rows):
@@ -81,7 +83,7 @@
 
     for i in range(len(parts)):
         copy(i).start()
-    size = 64
+    size = 128
     tile_eff, _ = edge_slot(KL)
 
     def rows_of(step):
@@ -158,8 +160,8 @@
     bottom_ref,
     wet_ref,
     new_ref,
-    fx_ref,
-    fy_ref,
+    source_ref,
+    wet_ext_ref,
     ext_ref,
     eff_ref,
     min_ref,
@@ -167,6 +169,8 @@
     u_ref,
     l_ref,
     acc_ref,
+    fx_ref,
+    fy_ref,
     in_sems,
     out_sems,
 ):
@@ -206,33 +210,20 @@
         shift = jnp.full((n, LANES), 3 * (k % 10), I32)
         return (lax.shift_right_logical(words, shift) & 7).astype(F32)
 
-    def stage(step, late):
-        k = jnp.clip(step - late, 0, KL - 1)
-        valid = jnp.logical_and(step >= late, step < KL + late)
-        return k, jnp.where(valid, thick_ref[k], 0.0)
-
-    def body(step, carry):
-        @pl.when(step < KL)
-        def _():
+    def body(step, stages):
+        if 0 in stages:
             load(step).wait()
-
-        @pl.when(step >= 4)
-        def _():
-            store(step - 4).start()
-
-        ku, _ = stage(step, 0)
-        kl, _ = stage(step, 1)
-        kd, thick_d = stage(step, 2)
-        kf, thick_f = stage(step, 3)
-        mix = [jnp.where(step < KL + 2, mixing_ref[kd, c], 0.0) for c in range(2)]
+        if 3 in stages:
+            store(step - 3).start()
+        ku, kl, kd, kf = (step - late for late in range(4))
 
         def flux(r0, n):
             here = acc_ref[pl.ds(PAD + r0, n)]
             up = acc_ref[pl.ds(PAD + r0 - 1, n)]
             face_x = min_ref[0, pl.ds(r0, n)] > kf
             face_y = min_ref[1, pl.ds(r0, n)] > kf
-            fx_ref[pl.ds(r0, n)] += thick_f * jnp.where(face_x, here - up, 0.0)
-            fy_ref[pl.ds(r0, n)] += thick_f * jnp.where(face_y, here - roll(here, 1), 0.0)
+            fx_ref[pl.ds(PAD + r0, n)] += thick_ref[kf] * jnp.where(face_x, here - up, 0.0)
+            fy_ref[pl.ds(PAD + r0, n)] += thick_ref[kf] * jnp.where(face_y, here - roll(here, 1), 0.0)
 
         def density(r0, n):
             wet = eff_ref[pl.ds(PAD + r0, n)] > kd
@@ -241,12 +232,12 @@
             for c in range(2):
                 x, around = neighbours(l_ref.at[c], r0, n)
                 second = jnp.where(wet, around, 0.0) - number * x
-                value = ext_ref[2 * kd + c, pl.ds(r0, n)] - mix[c] * second
+                value = ext_ref[2 * kd + c, pl.ds(r0, n)] - mixing_ref[kd, c] * second
                 low, high = max(r0, HALO), min(r0 + n, HALO + ROWS)
                 ext_ref[2 * kd + c, pl.ds(low, high - low)] = value[low - r0 : high - r0]
                 new.append(value)
             plain = 0.8 * new[1] - 0.2 * new[0]
-            acc_ref[pl.ds(PAD + r0, n)] += thick_d * jnp.where(wet, plain, 0.0)
+            acc_ref[pl.ds(PAD + r0, n)] += thick_ref[kd] * jnp.where(wet, plain, 0.0)
 
         def first(r0, n):
             wet = eff_ref[pl.ds(PAD + r0, n)] > kl
@@ -260,30 +251,65 @@
             for c in range(2):
                 u_ref[c, pl.ds(PAD + r0, n)] = jnp.where(wet, ext_ref[2 * ku + c, pl.ds(r0, n)], 0.0)
 
-        work = (flux, density, first, masked)
+        work = ((3, flux), (2, density), (1, first), (0, masked))
+        work = [part for late, part in work if late in stages]
         for turn in range(len(CHUNKS) + len(work) - 1):
             for late, part in enumerate(work):
                 if 0 <= turn - late < len(CHUNKS):
                     part(*CHUNKS[turn - late])
+
+    def all_stages(step, carry):
+        body(step, range(4))
         return carry
 
-    lax.fori_loop(0, KL + 3, body, 0)
-    store(KL - 1).start()
+    for step in range(3):
+        body(step, range(step + 1))
+    lax.fori_loop(3, KL, all_stages, 0)
+    for step in range(KL, KL + 3):
+        body(step, range(step - KL + 1, 4))
+    for r0, n in CHUNKS:
+        fx = fx_ref[pl.ds(PAD + r0, n)] - fx_ref[pl.ds(PAD + r0 + 1, n)]
+        fy = fy_ref[pl.ds(PAD + r0, n)]
+        source_ref[pl.ds(r0, n)] = GRAVITY * (fx + (fy - roll(fy, -1)))
+        wet_ext_ref[pl.ds(r0, n)] = eff_ref[pl.ds(PAD + r0, n)]
     each(lambda k: store(k).wait())
 
 
-def patch_kernel(new_in, edge_ref, new_ref):
-    for part in range(PATCH_LEVELS):
-        k = pl.program_id(0) * PATCH_LEVELS + part
-        tile = k % TILES
-        back = (2 * LANES - 8 - GROUP * (k // TILES)) % LANES
-        for r0, n in blocks(0, ROWS, 64):
-            lane = lane_iota(n)
-            middle = jnp.logical_and(lane >= 4, lane < LANES - 4)
-            own = pl.ds(r0, n)
-            for c in range(2):
-                edge = pltpu.roll(edge_ref[c, tile, own], back, 1)
-                new_ref[2 * part + c, own] = jnp.where(middle, new_in[2 * part + c, own], edge)
+def patch_kernel(new_ref, edge_ref, out_ref, held_ref, in_sems, out_sems):
+    def planes(k):
+        return pl.ds(2 * PATCH * k, 2 * PATCH)
+
+    def load(k):
+        return pltpu.make_async_copy(new_ref.at[planes(k)], held_ref.at[planes(k)], in_sems.at[k])
+
+    def store(k):
+        return pltpu.make_async_copy(held_ref.at[planes(k)], out_ref.at[planes(k)], out_sems.at[k])
+
+    def each(body):
+        def step(k, carry):
+            body(k)
+            return carry
+
+        lax.fori_loop(0, KL // PATCH, step, 0)
+
+    def levels(part):
+        load(part).wait()
+        for i in range(PATCH):
+            k = part * PATCH + i
+            tile = k % TILES
+            back = (2 * LANES - 8 - GROUP * (k // TILES)) % LANES
+            for c in range(2):
+                for r0, n in blocks(0, ROWS, 64):
+                    lane = lane_iota(n)
+                    middle = jnp.logical_and(lane >= 4, lane < LANES - 4)
+                    own = pl.ds(r0, n)
+                    edge = pltpu.roll(edge_ref[c, tile, own], back, 1)
+                    held_ref[2 * k + c, own] = jnp.where(middle, held_ref[2 * k + c, own], edge)
+        store(part).start()
+
+    each(lambda k: load(k).start())
+    each(levels)
+    each(lambda k: store(k).wait())
 
 
 def two_sum(a, b):
@@ -360,18 +386,18 @@
 def solve_kernel(
     mixing_ref,
     thick_ref,
-    fx_ref,
-    fy_ref,
+    source_ref,
+    wet_ext_ref,
     from_left_ref,
     from_right_ref,
     edge_ref,
-    top_ref,
-    bottom_ref,
-    wet_ref,
+    seen_ref,
+    beside_ref,
+    depth_ref,
+    sums_ref,
+    new_ref,
     v_ref,
     d_ref,
-    sums_ref,
-    new_ref,
     e_ref,
     west_ref,
     east_ref,
@@ -380,9 +406,8 @@
     l_ref,
     n_ref,
     acc_ref,
-    eff_ref,
-    full_fx_ref,
-    full_fy_ref,
+    fx_ref,
+    fy_ref,
     dl_ref,
     dr_ref,
     w_ref,
@@ -397,7 +422,7 @@
 
     for ref in (e_ref, west_ref, east_ref):
         clear(ref)
-    for ref in (u_ref, l_ref, acc_ref, d_ref, v_ref, dl_ref, dr_ref, p_ref, q_ref, full_fx_ref, full_fy_ref):
+    for ref in (u_ref, l_ref, acc_ref, d_ref, v_ref, dl_ref, dr_ref, p_ref, q_ref, fx_ref):
         rank = len(ref.shape) - 2
         lead = [()]
         for size in ref.shape[:rank]:
@@ -505,15 +530,12 @@
                 run = run + layers[tile]
                 acc_ref[side, tile, at] = run
     thick = [by_group(tile, lambda k: thick_ref[k]) for tile in range(TILES)]
-    extend_eff(eff_ref.at[0], 0, top_ref, bottom_ref, wet_ref)
     table = jnp.zeros((8, LANES), F32)
     for k in range(KL):
         table += jnp.where(lane_iota(8) > k, thick_ref[k], 0.0)
-    for r0, n in blocks(0, EXT, EXT // 2):
-        lane = lane_iota(n)
-        own = pl.ds(r0, n)
+    halves = blocks(0, EXT, EXT // 2)
+    for r0, n in halves:
         at = pl.ds(PAD + r0, n)
-        faces = []
         for side in SIDES:
             e = e_ref[side, at]
             min_x = jnp.minimum(e, e_ref[side, pl.ds(PAD + r0 - 1, n)])
@@ -526,35 +548,36 @@
                 level_of = level_lanes(tile)
                 face_x += thick[tile] * jnp.where(min_x > level_of, here - up, 0.0)
                 face_y += thick[tile] * jnp.where(min_y > level_of, here - roll(here, 1), 0.0)
-            faces += [face_x, face_y]
+            fx_ref[side, at] = face_x
+            fy_ref[side, pl.ds(r0, n)] = face_y
+    for r0, n in halves:
+        lane = lane_iota(n)
+        at = pl.ds(PAD + r0, n)
+        own = pl.ds(r0, n)
+        sources = []
+        for side in SIDES:
+            fy = fy_ref[side, own]
+            sources.append(fx_ref[side, at] - fx_ref[side, pl.ds(PAD + r0 + 1, n)] + (fy - roll(fy, -1)))
         for shift in (GROUP, 2 * GROUP, 4 * GROUP):
-            faces = [x + roll(x, shift) for x in faces]
-        faces = [roll(x, 8) for x in faces]
-        for full, main, west, east in (
-            (full_fx_ref, fx_ref, faces[0], faces[2]),
-            (full_fy_ref, fy_ref, faces[1], faces[3]),
-        ):
-            full[0, at] = jnp.where(lane < 4, west, jnp.where(lane >= LANES - 4, east, main[own]))
-            full[1, at] = jnp.where(lane < 8, east, jnp.where(lane >= LANES - 8, west, 0.0))
+            sources = [x + roll(x, shift) for x in sources]
+        west, east = (GRAVITY * roll(x, 8) for x in sources)
+        v_ref[0, 0, at] = jnp.where(lane < 3, west, jnp.where(lane >= LANES - 3, east, source_ref[own]))
+        v_ref[0, 1, at] = jnp.where(lane < 8, east, jnp.where(lane >= LANES - 8, west, 0.0))
+    for r0, n in halves:
+        lane = lane_iota(n)
+        at = pl.ds(PAD + r0, n)
         west = roll(e_ref[0, at], 8)
         east = roll(e_ref[1, at], 8)
-        eff_ref[1, own] = jnp.where(lane < 8, east, jnp.where(lane >= LANES - 8, west, 0))
-    for t in range(2):
-        for r0, n in blocks(0, EXT, 8):
-            d_ref[t, pl.ds(PAD + r0, n)] = jnp.take_along_axis(table, eff_ref[t, pl.ds(r0, n)], axis=1)
+        beside = jnp.where(lane < 8, east, jnp.where(lane >= LANES - 8, west, 0))
+        main = wet_ext_ref[pl.ds(r0, n)]
+        for t, wet in enumerate((main, beside)):
+            for i in range(0, n, 8):
+                d_ref[t, pl.ds(PAD + r0 + i, 8)] = jnp.take_along_axis(table, wet[i : i + 8], axis=1)
     for r0, n in CHUNKS:
         here = pl.ds(PAD + r0, n)
         d_main, d_side = d_ref[0, here], d_ref[1, here]
         dl_ref[0, here], dl_ref[1, here] = lane_left(d_main, d_side)
         dr_ref[0, here], dr_ref[1, here] = lane_right(d_main, d_side)
-
-    for r0, n in CHUNKS:
-        here = pl.ds(PAD + r0, n)
-        east = lane_right(full_fy_ref[0, here], full_fy_ref[1, here])
-        for t in range(2):
-            fx = full_fx_ref[t, here] - full_fx_ref[t, pl.ds(PAD + r0 + 1, n)]
-            fy = full_fy_ref[t, here] - east[t]
-            v_ref[0, t, here] = 10.0 * (fx + fy)
 
     def weights(t, carry):
         for r0, n in CHUNKS:
@@ -607,6 +630,17 @@
 
     lax.fori_loop(0, 4, power, 0)
 
+    for i in range(4):
+        seen_ref[i] = v_ref[i, 0, pl.ds(PAD, SEEN)]
+    depth_ref[...] = d_ref[0, pl.ds(PAD, SEEN)]
+    for r0, n in OWN_CHUNKS:
+        lane = lane_iota(n)
+        at = pl.ds(PAD + r0, n)
+        beside = roll(d_ref[1, at], 5)
+        for i in range(4):
+            beside = jnp.where(lane == i, roll(v_ref[i, 1, at], i + 1), beside)
+        beside_ref[pl.ds(r0 - HALO, n)] = beside
+
     def dots(step, carry):
         at = pl.ds(pl.multiple_of(PAD + HALO + 8 * step, 8), 8)
         v = [v_ref[i, 0, at] for i in range(5)]
@@ -644,7 +678,7 @@
         sums_ref[pl.ds(at, 8)] = row
 
 
-def finish_kernel(all_ref, v_ref, d_ref, surface_ref, flow_ref, s_ref):
+def finish_kernel(all_ref, seen_ref, beside_ref, depth_ref, surface_ref, flow_ref, s_ref):
     zero = jnp.zeros((8, LANES), F32)
     high, low = zero, zero
     for at in range(0, all_ref.shape[0], 8):
@@ -688,26 +722,29 @@
         for i in range(step + 2):
             direction[i] = pair_add(residual[i], pair_mul(beta, direction[i]))
     weight = [s[0][0:1] for s in surface]
-
-    def combine(side, r0, n):
-        at = pl.ds(PAD + r0, n)
-        total = weight[0] * v_ref[0, side, at]
+    lane = lane_iota(1)
+    by_lane = jnp.zeros((1, LANES), F32)
+    for i in range(4):
+        by_lane = jnp.where(lane == i, weight[i], by_lane)
+    for r0, n in blocks(0, SEEN, 88):
+        at = pl.ds(r0, n)
+        total = weight[0] * seen_ref[0, at]
         for i in range(1, 4):
-            total = total + weight[i] * v_ref[i, side, at]
-        return total
-
-    chunks = [(0, HALO)] + blocks(HALO, HALO + ROWS, 32)
-    for r0, n in chunks:
-        s_ref[pl.ds(r0, n)] = combine(0, r0, n)
-    for r0, n in chunks[1:]:
-        s = s_ref[pl.ds(r0, n)]
+            total = total + weight[i] * seen_ref[i, at]
+        s_ref[at] = total
+    for r0, n in blocks(HALO, SEEN, 128):
+        at = pl.ds(r0, n)
+        above = pl.ds(r0 - 1, n)
         own = pl.ds(r0 - HALO, n)
-        here = pl.ds(PAD + r0, n)
-        west, _ = lane_left(s, combine(1, r0, n))
-        d_west, _ = lane_left(d_ref[0, here], d_ref[1, here])
-        d = d_ref[0, here]
+        lane = lane_iota(n)
+        s, d = s_ref[at], depth_ref[at]
+        beside = beside_ref[own]
+        d_west = jnp.where(lane == 0, roll(beside, -4), roll(d, 1))
+        beside = by_lane * beside
+        beside = beside + roll(beside, -1)
+        west = jnp.where(lane == 0, beside + roll(beside, -2), roll(s, 1))
         surface_ref[own] = s
-        flow_ref[0, own] = jnp.minimum(d, d_ref[0, pl.ds(PAD + r0 - 1, n)]) * (s_ref[pl.ds(r0 - 1, n)] - s)
+        flow_ref[0, own] = jnp.minimum(d, depth_ref[above]) * (s_ref[above] - s)
         flow_ref[1, own] = jnp.minimum(d, d_west) * (west - s)
 
 
@@ -716,8 +753,8 @@
 HBM = pl.BlockSpec(memory_space=pltpu.HBM)
 
 
-def params(**kwargs):
-    return pltpu.CompilerParams(vmem_limit_bytes=VMEM_LIMIT, **kwargs)
+def params(limit):
+    return pltpu.CompilerParams(vmem_limit_bytes=limit * MIB)
 
 
 def cost(flops, moved):
@@ -755,7 +792,7 @@
             in_specs=[HBM, VM],
             out_specs=(VM,) * 3,
             scratch_shapes=[scratch(planes, rows=ROWS), pltpu.SemaphoreType.DMA((LOADS,))],
-            compiler_params=params(),
+            compiler_params=params(48),
             cost_estimate=cost(10_000_000, 7_000_000),
         )(flat, wet)
         edge, to_right, to_left = pl.pallas_call(
@@ -764,15 +801,15 @@
             in_specs=[VM] * 5,
             out_specs=(VM,) * 3,
             input_output_aliases={i + 2: i for i in range(3)},
-            compiler_params=params(),
+            compiler_params=params(16),
             cost_estimate=cost(1_000_000, 700_000),
         )(top, bottom, *own)
         from_left = ring(to_right, "by", 1)
         from_right = ring(to_left, "by", -1)
     with jax.named_scope("block"):
-        new, fx, fy = pl.pallas_call(
+        new, source, wet_ext = pl.pallas_call(
             block_kernel,
-            out_shape=(shape(planes, ROWS, LANES), shape(EXT, LANES), shape(EXT, LANES)),
+            out_shape=(shape(planes, ROWS, LANES), shape(EXT, LANES), shape(EXT, LANES, dtype=I32)),
             in_specs=[SM, SM, HBM, VM, VM, VM],
             out_specs=(HBM, VM, VM),
             scratch_shapes=[
@@ -783,24 +820,29 @@
                 scratch(2),
                 scratch(2),
                 scratch(),
+                scratch(),
+                scratch(),
                 pltpu.SemaphoreType.DMA((KL,)),
                 pltpu.SemaphoreType.DMA((KL,)),
             ],
-            compiler_params=params(),
+            compiler_params=params(48),
             cost_estimate=cost(50_000_000, 12_000_000),
         )(mixing, thickness, flat, top, bottom, wet)
     with jax.named_scope("powers"):
-        powers, depth, sums, new_edge = pl.pallas_call(
+        seen, beside, depth, sums, new_edge = pl.pallas_call(
             solve_kernel,
             out_shape=(
-                shape(5, 2, BUF, LANES),
-                shape(2, BUF, LANES),
+                shape(4, SEEN, LANES),
+                shape(ROWS, LANES),
+                shape(SEEN, LANES),
                 shape(devices, LANES),
                 shape(2, TILES, ROWS, LANES),
             ),
-            in_specs=[SM, SM] + [VM] * 8,
-            out_specs=(VM,) * 4,
+            in_specs=[SM, SM] + [VM] * 5,
+            out_specs=(VM,) * 5,
             scratch_shapes=[
+                scratch(5, 2),
+                scratch(2),
                 scratch(2, dtype=I32),
                 scratch(2, dtype=I32),
                 scratch(2, dtype=I32),
@@ -809,42 +851,43 @@
                 scratch(2, 2),
                 scratch(2, rows=EXT),
                 scratch(2, TILES),
-                scratch(2, rows=EXT, dtype=I32),
                 scratch(2),
-                scratch(2),
+                scratch(2, rows=EXT),
                 scratch(2),
                 scratch(2),
                 scratch(9, 2, rows=EXT),
                 scratch(2),
                 scratch(2),
             ],
-            compiler_params=params(),
+            compiler_params=params(20),
             cost_estimate=cost(50_000_000, 6_000_000),
-        )(mixing, thickness, fx, fy, from_left, from_right, edge, top, bottom, wet)
+        )(mixing, thickness, source, wet_ext, from_left, from_right, edge)
     with jax.named_scope("sums"):
         everyone = lax.all_to_all(sums, ("bx", "by"), 0, 0, tiled=True)
     with jax.named_scope("patch"):
-        level_block = pl.BlockSpec((2 * PATCH_LEVELS, ROWS, LANES), lambda i: (i, 0, 0))
         tracers_new = pl.pallas_call(
             patch_kernel,
-            grid=(KL // PATCH_LEVELS,),
             out_shape=shape(planes, ROWS, LANES),
-            in_specs=[level_block, VM],
-            out_specs=level_block,
-            input_output_aliases={0: 0},
-            compiler_params=params(),
+            in_specs=[HBM, VM],
+            out_specs=HBM,
+            scratch_shapes=[
+                scratch(planes, rows=ROWS),
+                pltpu.SemaphoreType.DMA((KL // PATCH,)),
+                pltpu.SemaphoreType.DMA((KL // PATCH,)),
+            ],
+            compiler_params=params(48),
             cost_estimate=cost(10_000_000, 12_000_000),
         )(new, new_edge)
     with jax.named_scope("surface"):
         surface, transports = pl.pallas_call(
             finish_kernel,
             out_shape=(shape(ROWS, LANES), shape(2, ROWS, LANES)),
-            in_specs=[VM] * 3,
+            in_specs=[VM] * 4,
             out_specs=(VM, VM),
-            scratch_shapes=[scratch(rows=HALO + ROWS)],
-            compiler_params=params(),
+            scratch_shapes=[scratch(rows=SEEN)],
+            compiler_params=params(8),
             cost_estimate=cost(1_000_000, 3_000_000),
-        )(everyone, powers, depth)
+        )(everyone, seen, beside, depth)
     return tracers_new.reshape(tracers.shape), surface, transports
 
 

time: 61.2 us -> 56.8 us (0.928)
  Pallas kernels: 38 us -> 32.1 us
  waiting for transfers between devices: 0.45 us -> 5.85 us
  local copies, waits for them, and re-layouts: 5.55 us -> 1.16 us
  starting transfers between devices: 14.9 us -> 15.8 us
    all_to_all x1, waiting for transfers between devices: 0.01 us -> 4.73 us  [shards(): everyone = lax.all_to_all(sums, ('bx', 'by'), 0, 0, tiled=True)]
    unnamed x15 -> x5, local copies, waits for them, and re-layouts: 4.51 us -> 0.1 us
    pallas_call x2, Pallas kernels: 18.8 us -> 14.9 us  [the longest x1 9.92 us: shards(): pl.pallas_call(solve_kernel, out_shape=(shape(4, SEEN, LANES), shape(ROWS...]
    pallas_call x1, Pallas kernels: 13.1 us -> 11.7 us  [shards(): pl.pallas_call(block_kernel, out_shape=(shape(planes, ROWS, LANES), shape...]
    all_to_all x1, starting transfers between devices: 6.1 us -> 6.98 us  [shards(): everyone = lax.all_to_all(sums, ('bx', 'by'), 0, 0, tiled=True)]
    pallas_call x1, Pallas kernels: 4.49 us -> 3.81 us  [shards(): pl.pallas_call(own_edges_kernel, out_shape=edges, in_specs=[HBM, VM], out...]
    ppermute x4, waiting for transfers between devices: 0.45 us -> 1.13 us  [ring(): lax.ppermute(x, axis, [(i, (i + step) % count) for i in range(count)])]
  transfers between devices with their start and end apart: 5 -> 5, of which waited for: 1 -> 2; matrix products, arithmetic and copies ran while one was open for 0% -> 0% of each run, Pallas kernels for 45% -> 36%
where the time goes in v4:
time: 56.8 us; the launch traced here: 56.7 us
  Pallas kernels  32.1 us (57%)
  starting transfers between devices  15.8 us (28%)
  waiting for transfers between devices  5.85 us (10%)
  local copies, waits for them, and re-layouts  1.16 us (2%)
  other arithmetic  1.01 us (2%)
  between operations  0.74 us (1%)
    pallas_call x1, Pallas kernels, shards(): pl.pallas_call(block_kernel, out_shape=(shape(planes, ROWS, LANES), shape...  11.7 us
    pallas_call x1, Pallas kernels, shards(): pl.pallas_call(solve_kernel, out_shape=(shape(4, SEEN, LANES), shape(ROWS...  9.92 us
    ppermute x4, starting transfers between devices, ring(): lax.ppermute(x, axis, [(i, (i + step) % count) for i in range(count)])  8.82 us
    all_to_all x1, starting transfers between devices, shards(): everyone = lax.all_to_all(sums, ('bx', 'by'), 0, 0, tiled=True)  6.98 us
    pallas_call x1, Pallas kernels, shards(): pl.pallas_call(patch_kernel, out_shape=shape(planes, ROWS, LANES), in_spe...  4.97 us
    all_to_all x1, waiting for transfers between devices, shards(): everyone = lax.all_to_all(sums, ('bx', 'by'), 0, 0, tiled=True)  4.73 us
    pallas_call x1, Pallas kernels, shards(): pl.pallas_call(own_edges_kernel, out_shape=edges, in_specs=[HBM, VM], out...  3.81 us
    pallas_call x1, Pallas kernels, shards(): pl.pallas_call(finish_kernel, out_shape=(shape(ROWS, LANES), shape(2, ROW...  1.46 us
  transfers between devices with their start and end apart: 5, of which 2 were waited for; matrix products, arithmetic and copies ran while one was open for 0% of the time, Pallas kernels for 36%

profile of v4, /device:TPU:1, one launch (start us, length us, event | category | flops | bytes accessed | tf_op | source)
XLA Modules:
  0.0 56.7 jit_solution(10690512108106736205)
XLA Ops:
  0.6 0.0 copy-start.1
  0.6 0.0 copy-start
  0.7 1.0 %fusion = (f32[44,8,128]{2,1,0:T(8,128)S(1)}, f32[44,8,128]{2,1,0:T(8,128)S(1)}) fusion(f32[44,256,128]{2,1,0:T(8,128)} %bitcast.11), kind=kLoop, calls=%fused_computation.5 | loop fusion | bytes 720896 | tf_op jit(solution)/shard_map/rows/slice | solution.py:783
  1.7 1.0 %select_convert_fusion.wet_ref = f32[256,128]{1,0:T(8,128)S(1)} fusion(s32[256,128]{1,0:T(8,128)} %param.8, s32[256,128]{1,0:T(8,128)} %param.9), kind=kLoop, calls=%fused_computation.2 | loop fusion | flops 98304 | bytes 393216 | tf_op jit(solution)/shard_map/convert_element_type | solution.py:780
  2.7 2.7 %collective-permute-start = (f32[45,8,128]{2,1,0:T(8,128)S(1)}, f32[45,8,128]{2,1,0:T(8,128)S(1)}, u32[]{:S(2)}, u32[]{:S(2)}) collective-permute-start(f32[45,8,128]{2,1,0:T(8,128)S(1)} %pad_maximum_fusion), channel_id=1, source_target_pairs={{0,16},{16,32},{32,48},{48,64},{64,80},{80,96},{96,112},{112,0},{1... | collective-permute-start | bytes 552968 | tf_op jit(solution)/shard_map/rows/ppermute | solution.py:766
  5.4 0.0 collective-permute-start.1
  5.5 3.8 %columns.2 = (f32[2,3,272,128]{3,2,1,0:T(8,128)S(1)}, f32[3,272,128]{2,1,0:T(8,128)S(1)}, f32[3,272,128]{2,1,0:T(8,128)S(1)}) custom-call(f32[44,256,128]{2,1,0:T(8,128)} %bitcast.12, f32[256,128]{1,0:T(8,128)S(1)} %select_convert_fusion.wet_ref), custom_call_target="tpu_custom_call" | custom-call | flops 10000000 | bytes 7000000 | tf_op jit(solution)/shard_map/columns/pallas_call | solution.py:789
  9.3 0.0 collective-permute-done.top_ref
  9.3 1.1 %collective-permute-done.1.bottom_ref = f32[45,8,128]{2,1,0:T(8,128)S(1)} collective-permute-done((f32[45,8,128]{2,1,0:T(8,128)S(1)}, f32[45,8,128]{2,1,0:T(8,128)S(1)}, u32[]{:S(2)}, u32[]{:S(2)}) %collective-permute-start.1) | collective-permute-done | bytes 184352 | tf_op jit(solution)/shard_map/rows/ppermute | solution.py:766
  10.4 0.2 columns.3
  10.6 1.3 %collective-permute-start.2 = (f32[3,272,128]{2,1,0:T(8,128)S(1)}, f32[3,272,128]{2,1,0:T(8,128)S(1)}, u32[]{:S(2)}, u32[]{:S(2)}) collective-permute-start(f32[3,272,128]{2,1,0:T(8,128)S(1)} %get-tuple-element.25), channel_id=1, source_target_pairs={{0,1},{1,2},{2,3},{3,4},{4,5},{5,6},{6,7},{7,8},{8,9},{9,10},{10,1... | collective-permute-start | bytes 1253384 | tf_op jit(solution)/shard_map/columns/ppermute | solution.py:766
  11.9 4.8 %collective-permute-start.3 = (f32[3,272,128]{2,1,0:T(8,128)S(1)}, f32[3,272,128]{2,1,0:T(8,128)S(1)}, u32[]{:S(2)}, u32[]{:S(2)}) collective-permute-start(f32[3,272,128]{2,1,0:T(8,128)S(1)} %get-tuple-element.26), channel_id=1, source_target_pairs={{0,15},{1,0},{2,1},{3,2},{4,3},{5,4},{6,5},{7,6},{8,7},{9,8},{10,9... | collective-permute-start | bytes 1253384 | tf_op jit(solution)/shard_map/columns/ppermute | solution.py:766
  16.7 0.0 copy-done.1
  16.7 0.1 copy.13.mixing_ref
  16.8 0.0 copy-done
  16.8 11.7 %block.1 = (f32[44,256,128]{2,1,0:T(8,128)}, f32[272,128]{1,0:T(8,128)S(1)}, s32[272,128]{1,0:T(8,128)S(1)}) custom-call(f32[22,2]{1,0:T(8,128)S(1)} %copy.13.mixing_ref, f32[22]{0:T(128)S(1)} %copy-done, f32[44,256,128]{2,1,0:T(8,128)} %bitcast.13, f32[45,8,128]{2,1,0:T(8,128)S(1)} %collective-permute-done.top_ref, ...), custom_call_target="tpu_custom_call" | custom-call | flops 50000000 | bytes 12000000 | tf_op jit(solution)/shard_map/block/pallas_call | solution.py:810
  28.6 0.0 collective-permute-done.2.from_left_ref
  28.6 0.0 collective-permute-done.3.from_right_ref
  28.6 9.9 %powers.1 = (f32[4,264,128]{2,1,0:T(8,128)S(1)}, f32[256,128]{1,0:T(8,128)S(1)}, f32[264,128]{1,0:T(8,128)S(1)}, f32[128,128]{1,0:T(8,128)}, f32[2,3,256,128]{3,2,1,0:T(8,128)S(1)}) custom-call(f32[22,2]{1,0:T(8,128)S(1)} %copy.13.mixing_ref, f32[22]{0:T(128)S(1)} %copy-done, f32[272,128]{1,0:T(8,128)S(1)} %get-tuple-element.20.source_ref, ...), custom_call_target="tpu_custom_call" | custom-call | flops 50000000 | bytes 6000000 | tf_op jit(solution)/shard_map/powers/pallas_call | solution.py:832
  38.5 7.0 %all-to-all-start = ((f32[128,1,128]{2,1,0:T(1,128)}), f32[128,1,128]{2,1,0:T(1,128)S(1)}, u32[]{:S(2)}, u32[]{:S(2)}) async-start(f32[128,1,128]{2,1,0:T(1,128)} %bitcast.5), calls=%async_computation | async-start | bytes 131072 | tf_op jit(solution)/shard_map/sums/all_to_all | solution.py:866
  45.5 5.0 %patch.1 = f32[44,256,128]{2,1,0:T(8,128)} custom-call(f32[44,256,128]{2,1,0:T(8,128)} %get-tuple-element.19.new_ref, f32[2,3,256,128]{3,2,1,0:T(8,128)S(1)} %get-tuple-element.28.edge_ref), custom_call_target="tpu_custom_call" | custom-call | flops 10000000 | bytes 12000000 | tf_op jit(solution)/shard_map/patch/pallas_call | solution.py:868
  50.5 4.7 %all-to-all-done = f32[128,1,128]{2,1,0:T(1,128)S(1)} async-done(((f32[128,1,128]{2,1,0:T(1,128)}), f32[128,1,128]{2,1,0:T(1,128)S(1)}, u32[]{:S(2)}, u32[]{:S(2)}) %all-to-all-start) | async-done | bytes 65568 | tf_op jit(solution)/shard_map/sums/all_to_all | solution.py:866
  55.2 1.5 %surface.1 = (f32[256,128]{1,0:T(8,128)}, f32[2,256,128]{2,1,0:T(8,128)}) custom-call(f32[128,128]{1,0:T(8,128)S(1)} %bitcast.10, f32[4,264,128]{2,1,0:T(8,128)S(1)} %get-tuple-element.30.seen_ref, f32[256,128]{1,0:T(8,128)S(1)} %get-tuple-element.31.beside_ref, f32[264,128]{1,0:T(8,128)S(1)} %get-tuple-element.32.depth_ref), custom_call_target="tpu_custom_call" | custom-call | flops 1000000 | bytes 3000000 | tf_op jit(solution)/shard_map/surface/pallas_call | solution.py:882
  (3 shorter events, 0.0 us)
Async XLA Ops:
  0.6 16.1 %copy-start.1 = (f32[22,2]{0,1:T(2,128)S(1)}, f32[22,2]{0,1:T(2,128)}, u32[]{:S(2)}) copy-start(f32[22,2]{0,1:T(2,128)} %param.6) | copy-start | bytes 532
  0.6 16.2 %copy-start = (f32[22]{0:T(128)S(1)}, f32[22]{0:T(128)}, u32[]{:S(2)}) copy-start(f32[22]{0:T(128)} %thick_ref.3) | copy-start | bytes 268
  2.7 6.6 %collective-permute-start = (f32[45,8,128]{2,1,0:T(8,128)S(1)}, f32[45,8,128]{2,1,0:T(8,128)S(1)}, u32[]{:S(2)}, u32[]{:S(2)}) collective-permute-start(f32[45,8,128]{2,1,0:T(8,128)S(1)} %pad_maximum_fusion), channel_id=1, source_target_pairs={{0,16},{16,32},{32,48},{48,64},{64,80},{80,96},{96,112},{112,0},{1... | collective-permute-start | bytes 552968 | tf_op jit(solution)/shard_map/rows/ppermute | solution.py:766
  5.4 5.0 %collective-permute-start.1 = (f32[45,8,128]{2,1,0:T(8,128)S(1)}, f32[45,8,128]{2,1,0:T(8,128)S(1)}, u32[]{:S(2)}, u32[]{:S(2)}) collective-permute-start(f32[45,8,128]{2,1,0:T(8,128)S(1)} %pad_maximum_fusion.1), channel_id=1, source_target_pairs={{0,112},{16,0},{32,16},{48,32},{64,48},{80,64},{96,80},{112,96},{1... | collective-permute-start | bytes 552968 | tf_op jit(solution)/shard_map/rows/ppermute | solution.py:766
  10.6 17.9 %collective-permute-start.2 = (f32[3,272,128]{2,1,0:T(8,128)S(1)}, f32[3,272,128]{2,1,0:T(8,128)S(1)}, u32[]{:S(2)}, u32[]{:S(2)}) collective-permute-start(f32[3,272,128]{2,1,0:T(8,128)S(1)} %get-tuple-element.25), channel_id=1, source_target_pairs={{0,1},{1,2},{2,3},{3,4},{4,5},{5,6},{6,7},{7,8},{8,9},{9,10},{10,1... | collective-permute-start | bytes 1253384 | tf_op jit(solution)/shard_map/columns/ppermute | solution.py:766
  11.9 16.7 %collective-permute-start.3 = (f32[3,272,128]{2,1,0:T(8,128)S(1)}, f32[3,272,128]{2,1,0:T(8,128)S(1)}, u32[]{:S(2)}, u32[]{:S(2)}) collective-permute-start(f32[3,272,128]{2,1,0:T(8,128)S(1)} %get-tuple-element.26), channel_id=1, source_target_pairs={{0,15},{1,0},{2,1},{3,2},{4,3},{5,4},{6,5},{7,6},{8,7},{9,8},{10,9... | collective-permute-start | bytes 1253384 | tf_op jit(solution)/shard_map/columns/ppermute | solution.py:766
  38.5 16.7 %all-to-all-start = ((f32[128,1,128]{2,1,0:T(1,128)}), f32[128,1,128]{2,1,0:T(1,128)S(1)}, u32[]{:S(2)}, u32[]{:S(2)}) async-start(f32[128,1,128]{2,1,0:T(1,128)} %bitcast.5), calls=%async_computation | async-start | bytes 131072 | tf_op jit(solution)/shard_map/sums/all_to_all | solution.py:866

commit v5 on v4

--- a/solution.py
+++ b/solution.py
@@ -33,6 +33,10 @@
     return (lane_iota(rows) & 8) == 0
 
 
+def tall(x, n):
+    return jnp.concatenate([x] * (n // 8)) if n > 8 else x
+
+
 def roll(x, shift):
     return pltpu.roll(x, shift % LANES, 1)
 
@@ -49,14 +53,34 @@
 OWN_CHUNKS = blocks(HALO, HALO + ROWS, 32)
 
 
+def interleave(parts):
+    for turn in range(len(CHUNKS) + len(parts) - 1):
+        for late, part in enumerate(parts):
+            if 0 <= turn - late < len(CHUNKS):
+                part(*CHUNKS[turn - late])
+
+
 def wet_levels(levels, land):
     return jnp.where(land == 0, levels, 0)
 
 
-def extend_eff(ref, base, top_ref, bottom_ref, wet_ref):
-    ref[pl.ds(base, HALO)] = top_ref[2 * KL].astype(I32)
-    ref[pl.ds(base + HALO, ROWS)] = wet_ref[...].astype(I32)
-    ref[pl.ds(base + HALO + ROWS, HALO)] = bottom_ref[2 * KL].astype(I32)
+def tops(thick_ref):
+    out = [jnp.float32(0.0)]
+    for k in range(KL):
+        out.append(out[-1] + thick_ref[k])
+    return out
+
+
+def depth_table(levels):
+    table = jnp.zeros((8, LANES), F32)
+    for k, top in enumerate(levels):
+        table = jnp.where(lane_iota(8) == k, top, table)
+    return table
+
+
+def look_up(table, index):
+    rows = [jnp.take_along_axis(table, index[i : i + 8], axis=1) for i in range(0, index.shape[0], 8)]
+    return jnp.concatenate(rows) if len(rows) > 1 else rows[0]
 
 
 def edge_slot(k):
@@ -161,16 +185,18 @@
     wet_ref,
     new_ref,
     source_ref,
-    wet_ext_ref,
+    depth_ref,
     ext_ref,
     eff_ref,
-    min_ref,
+    face_ref,
     word_ref,
     u_ref,
     l_ref,
-    acc_ref,
+    n_ref,
+    rho_ref,
     fx_ref,
     fy_ref,
+    begin_ref,
     in_sems,
     out_sems,
 ):
@@ -192,16 +218,25 @@
 
     each(lambda k: load(k).start())
     eff_ref[...] = jnp.zeros(eff_ref.shape, I32)
-    extend_eff(eff_ref, PAD, top_ref, bottom_ref, wet_ref)
+    eff_ref[pl.ds(PAD, HALO)] = top_ref[2 * KL].astype(I32)
+    eff_ref[pl.ds(PAD + HALO, ROWS)] = wet_ref[...].astype(I32)
+    eff_ref[pl.ds(PAD + HALO + ROWS, HALO)] = bottom_ref[2 * KL].astype(I32)
     ext_ref[:, pl.ds(0, HALO)] = top_ref[pl.ds(0, 2 * KL)]
     ext_ref[:, pl.ds(HALO + ROWS, HALO)] = bottom_ref[pl.ds(0, 2 * KL)]
-    for ref in (u_ref, l_ref, acc_ref, fx_ref, fy_ref):
+    for ref in (u_ref, l_ref, rho_ref, fx_ref, fy_ref):
         ref[...] = jnp.zeros(ref.shape, F32)
+    levels = tops(thick_ref)
+    table = depth_table(levels)
+    for k in range(KL):
+        begin_ref[k] = levels[k]
     for r0, n in CHUNKS:
         e = eff_ref[pl.ds(PAD + r0, n)]
-        min_ref[0, pl.ds(r0, n)] = jnp.minimum(e, eff_ref[pl.ds(PAD + r0 - 1, n)])
-        min_ref[1, pl.ds(r0, n)] = jnp.minimum(e, roll(e, 1))
-        effs = (eff_ref[pl.ds(PAD + r0 - 1, n)], eff_ref[pl.ds(PAD + r0 + 1, n)], roll(e, 1), roll(e, -1))
+        up = eff_ref[pl.ds(PAD + r0 - 1, n)]
+        west = roll(e, 1)
+        depth_ref[pl.ds(r0, n)] = look_up(table, e)
+        face_ref[0, pl.ds(r0, n)] = look_up(table, jnp.minimum(e, up))
+        face_ref[1, pl.ds(r0, n)] = look_up(table, jnp.minimum(e, west))
+        effs = (up, eff_ref[pl.ds(PAD + r0 + 1, n)], west, roll(e, -1))
         for word in range(3):
             word_ref[word, pl.ds(r0, n)] = count_word(effs, word)
 
@@ -218,16 +253,16 @@
         ku, kl, kd, kf = (step - late for late in range(4))
 
         def flux(r0, n):
-            here = acc_ref[pl.ds(PAD + r0, n)]
-            up = acc_ref[pl.ds(PAD + r0 - 1, n)]
-            face_x = min_ref[0, pl.ds(r0, n)] > kf
-            face_y = min_ref[1, pl.ds(r0, n)] > kf
-            fx_ref[pl.ds(PAD + r0, n)] += thick_ref[kf] * jnp.where(face_x, here - up, 0.0)
-            fy_ref[pl.ds(PAD + r0, n)] += thick_ref[kf] * jnp.where(face_y, here - roll(here, 1), 0.0)
+            here = rho_ref[pl.ds(PAD + r0, n)]
+            up = rho_ref[pl.ds(PAD + r0 - 1, n)]
+            below_x = jnp.maximum(face_ref[0, pl.ds(r0, n)] - begin_ref[kf], 0.0)
+            below_y = jnp.maximum(face_ref[1, pl.ds(r0, n)] - begin_ref[kf], 0.0)
+            fx_ref[pl.ds(PAD + r0, n)] += below_x * (here - up)
+            fy_ref[pl.ds(PAD + r0, n)] += below_y * (here - roll(here, 1))
 
         def density(r0, n):
             wet = eff_ref[pl.ds(PAD + r0, n)] > kd
-            number = count(kd, r0, n)
+            number = n_ref[pl.ds(r0, n)]
             new = []
             for c in range(2):
                 x, around = neighbours(l_ref.at[c], r0, n)
@@ -236,12 +271,12 @@
                 low, high = max(r0, HALO), min(r0 + n, HALO + ROWS)
                 ext_ref[2 * kd + c, pl.ds(low, high - low)] = value[low - r0 : high - r0]
                 new.append(value)
-            plain = 0.8 * new[1] - 0.2 * new[0]
-            acc_ref[pl.ds(PAD + r0, n)] += thick_ref[kd] * jnp.where(wet, plain, 0.0)
+            rho_ref[pl.ds(PAD + r0, n)] = (0.8 * thick_ref[kd]) * new[1] - (0.2 * thick_ref[kd]) * new[0]
 
         def first(r0, n):
             wet = eff_ref[pl.ds(PAD + r0, n)] > kl
             number = count(kl, r0, n)
+            n_ref[pl.ds(r0, n)] = number
             for c in range(2):
                 x, around = neighbours(u_ref.at[c], r0, n)
                 l_ref[c, pl.ds(PAD + r0, n)] = jnp.where(wet, around, 0.0) - number * x
@@ -252,11 +287,7 @@
                 u_ref[c, pl.ds(PAD + r0, n)] = jnp.where(wet, ext_ref[2 * ku + c, pl.ds(r0, n)], 0.0)
 
         work = ((3, flux), (2, density), (1, first), (0, masked))
-        work = [part for late, part in work if late in stages]
-        for turn in range(len(CHUNKS) + len(work) - 1):
-            for late, part in enumerate(work):
-                if 0 <= turn - late < len(CHUNKS):
-                    part(*CHUNKS[turn - late])
+        interleave([part for late, part in work if late in stages])
 
     def all_stages(step, carry):
         body(step, range(4))
@@ -271,7 +302,6 @@
         fx = fx_ref[pl.ds(PAD + r0, n)] - fx_ref[pl.ds(PAD + r0 + 1, n)]
         fy = fy_ref[pl.ds(PAD + r0, n)]
         source_ref[pl.ds(r0, n)] = GRAVITY * (fx + (fy - roll(fy, -1)))
-        wet_ext_ref[pl.ds(r0, n)] = eff_ref[pl.ds(PAD + r0, n)]
     each(lambda k: store(k).wait())
 
 
@@ -341,6 +371,11 @@
     return quick_sum(s, e + (x[1] + y[1]))
 
 
+def loose_add(x, y):
+    s, e = two_sum(x[0], y[0])
+    return s, e + (x[1] + y[1])
+
+
 def pair_mul(x, y):
     p, e = two_prod(x[0], y[0], split(x[0]), split(y[0]))
     return quick_sum(p, e + (x[0] * y[1] + x[1] * y[0]))
@@ -387,7 +422,7 @@
     mixing_ref,
     thick_ref,
     source_ref,
-    wet_ext_ref,
+    depth_in,
     from_left_ref,
     from_right_ref,
     edge_ref,
@@ -405,9 +440,11 @@
     u_ref,
     l_ref,
     n_ref,
-    acc_ref,
+    rho_ref,
     fx_ref,
     fy_ref,
+    face_ref,
+    lanes_ref,
     dl_ref,
     dr_ref,
     w_ref,
@@ -422,7 +459,7 @@
 
     for ref in (e_ref, west_ref, east_ref):
         clear(ref)
-    for ref in (u_ref, l_ref, acc_ref, d_ref, v_ref, dl_ref, dr_ref, p_ref, q_ref, fx_ref):
+    for ref in (u_ref, l_ref, rho_ref, d_ref, v_ref, dl_ref, dr_ref, p_ref, q_ref, fx_ref):
         rank = len(ref.shape) - 2
         lead = [()]
         for size in ref.shape[:rank]:
@@ -453,54 +490,65 @@
             west_ref[side, at] = roll(e, 1)
             east_ref[side, at] = roll(e, -1)
 
+    levels = tops(thick_ref)
+    table = depth_table(levels)
     group8 = lane_iota(8) // GROUP
-
-    def by_group(tile, values):
-        out = jnp.zeros((8, LANES), F32)
+    for tile in range(TILES):
+        held = [jnp.zeros((8, LANES), F32) for _ in range(4)]
         for g in range(GROUPS):
             k = TILES * g + tile
-            value = values(jnp.minimum(k, KL - 1))
-            out = jnp.where(group8 == g, jnp.where(k < KL, value, 0.0), out)
-        return out[0:1]
-
-    def level_lanes(tile):
-        return (group8 * TILES + tile)[0:1]
-
-    def tile_step(tile, carry):
-        level_of = level_lanes(tile)
-        mix = [by_group(tile, lambda k, c=c: mixing_ref[k, c]) for c in range(2)]
-        thick = by_group(tile, lambda k: thick_ref[k])
-
-        def masked(side, r0, n):
+            if k < KL:
+                values = (mixing_ref[k, 0], mixing_ref[k, 1], thick_ref[k], levels[k])
+            else:
+                values = (0.0, 0.0, 0.0, levels[KL])
+            held = [jnp.where(group8 == g, x, old) for x, old in zip(values, held)]
+        for i in range(4):
+            lanes_ref[tile, i] = held[i]
+    for side in SIDES:
+        for r0, n in CHUNKS:
+            e = e_ref[side, pl.ds(PAD + r0, n)]
+            face_ref[side, 0, pl.ds(r0, n)] = look_up(table, jnp.minimum(e, e_ref[side, pl.ds(PAD + r0 - 1, n)]))
+            face_ref[side, 1, pl.ds(r0, n)] = look_up(table, jnp.minimum(e, west_ref[side, pl.ds(PAD + r0, n)]))
+    pieces = [(tile, side) for tile in range(TILES) for side in SIDES]
+
+    def stages(piece):
+        tile, side = pieces[piece]
+        slot = piece % 3
+        level_of = group8 * TILES + tile
+        mix = [lanes_ref[tile, c] for c in range(2)]
+        thick = lanes_ref[tile, 2]
+        begin = lanes_ref[tile, 3]
+
+        def masked(r0, n):
             at = pl.ds(PAD + r0, n)
-            wet = e_ref[side, at] > level_of
+            wet = e_ref[side, at] > tall(level_of, n)
             for c in range(2):
                 x = field(side, c, tile, r0, n)
-                f_ref[side, c, pl.ds(r0, n)] = x
-                u_ref[side, c, at] = jnp.where(wet, x, 0.0)
-
-        def first(side, r0, n):
+                f_ref[slot, c, pl.ds(r0, n)] = x
+                u_ref[c, at] = jnp.where(wet, x, 0.0)
+
+        def first(r0, n):
             at = pl.ds(PAD + r0, n)
-            wet = e_ref[side, at] > level_of
-            number = jnp.where(e_ref[side, pl.ds(PAD + r0 - 1, n)] > level_of, 1.0, 0.0)
-            number += jnp.where(e_ref[side, pl.ds(PAD + r0 + 1, n)] > level_of, 1.0, 0.0)
-            number += jnp.where(west_ref[side, at] > level_of, 1.0, 0.0)
-            number += jnp.where(east_ref[side, at] > level_of, 1.0, 0.0)
-            n_ref[side, pl.ds(r0, n)] = number
+            wet = e_ref[side, at] > tall(level_of, n)
+            number = jnp.where(e_ref[side, pl.ds(PAD + r0 - 1, n)] > tall(level_of, n), 1.0, 0.0)
+            number += jnp.where(e_ref[side, pl.ds(PAD + r0 + 1, n)] > tall(level_of, n), 1.0, 0.0)
+            number += jnp.where(west_ref[side, at] > tall(level_of, n), 1.0, 0.0)
+            number += jnp.where(east_ref[side, at] > tall(level_of, n), 1.0, 0.0)
+            n_ref[pl.ds(r0, n)] = number
             for c in range(2):
-                x, around = neighbours(u_ref.at[side, c], r0, n)
-                l_ref[side, c, at] = jnp.where(wet, around, 0.0) - number * x
-
-        def density(side, r0, n):
+                x, around = neighbours(u_ref.at[c], r0, n)
+                l_ref[c, at] = jnp.where(wet, around, 0.0) - number * x
+
+        def density(r0, n):
             at = pl.ds(PAD + r0, n)
-            wet = e_ref[side, at] > level_of
-            number = n_ref[side, pl.ds(r0, n)]
+            wet = e_ref[side, at] > tall(level_of, n)
+            number = n_ref[pl.ds(r0, n)]
             new = []
             for c in range(2):
-                x, around = neighbours(l_ref.at[side, c], r0, n)
+                x, around = neighbours(l_ref.at[c], r0, n)
                 second = jnp.where(wet, around, 0.0) - number * x
-                new.append(f_ref[side, c, pl.ds(r0, n)] - mix[c] * second)
-            acc_ref[side, tile, at] = thick * jnp.where(wet, 0.8 * new[1] - 0.2 * new[0], 0.0)
+                new.append(f_ref[slot, c, pl.ds(r0, n)] - tall(mix[c], n) * second)
+            rho_ref[at] = tall(thick, n) * (0.8 * new[1] - 0.2 * new[0])
             low, high = max(r0, HALO), min(r0 + n, HALO + ROWS)
             own = pl.ds(low - HALO, high - low)
             for c in range(2):
@@ -509,47 +557,26 @@
                     value = jnp.where(first_half(high - low), value, new_ref[c, tile, own])
                 new_ref[c, tile, own] = value
 
-        for part in (masked, first, density):
-            for side in SIDES:
-                for r0, n in CHUNKS:
-                    part(side, r0, n)
-        return carry
-
-    lax.fori_loop(0, TILES, tile_step, 0)
-
-    for side in SIDES:
-        for r0, n in CHUNKS:
-            lane = lane_iota(n)
-            at = pl.ds(PAD + r0, n)
-            layers = [acc_ref[side, tile, at] for tile in range(TILES)]
-            run = (layers[0] + layers[1]) + layers[2]
-            run = jnp.where(lane >= GROUP, roll(run, GROUP), 0.0)
-            for step in (1, 2, 4):
-                run = run + jnp.where(lane >= step * GROUP, roll(run, step * GROUP), 0.0)
-            for tile in range(TILES):
-                run = run + layers[tile]
-                acc_ref[side, tile, at] = run
-    thick = [by_group(tile, lambda k: thick_ref[k]) for tile in range(TILES)]
-    table = jnp.zeros((8, LANES), F32)
-    for k in range(KL):
-        table += jnp.where(lane_iota(8) > k, thick_ref[k], 0.0)
+        def flux(r0, n):
+            here = rho_ref[pl.ds(PAD + r0, n)]
+            up = rho_ref[pl.ds(PAD + r0 - 1, n)]
+            below_x = jnp.maximum(face_ref[side, 0, pl.ds(r0, n)] - tall(begin, n), 0.0)
+            below_y = jnp.maximum(face_ref[side, 1, pl.ds(r0, n)] - tall(begin, n), 0.0)
+            face_x = below_x * (here - up)
+            face_y = below_y * (here - roll(here, 1))
+            if tile > 0:
+                face_x += fx_ref[side, pl.ds(PAD + r0, n)]
+                face_y += fy_ref[side, pl.ds(r0, n)]
+            fx_ref[side, pl.ds(PAD + r0, n)] = face_x
+            fy_ref[side, pl.ds(r0, n)] = face_y
+
+        return masked, first, density, flux
+
+    for step in range(len(pieces) + 3):
+        parts = [stages(step - late)[late] for late in (3, 2, 1, 0) if 0 <= step - late < len(pieces)]
+        interleave(parts)
+
     halves = blocks(0, EXT, EXT // 2)
-    for r0, n in halves:
-        at = pl.ds(PAD + r0, n)
-        for side in SIDES:
-            e = e_ref[side, at]
-            min_x = jnp.minimum(e, e_ref[side, pl.ds(PAD + r0 - 1, n)])
-            min_y = jnp.minimum(e, west_ref[side, at])
-            face_x = jnp.zeros((n, LANES), F32)
-            face_y = face_x
-            for tile in range(TILES):
-                here = acc_ref[side, tile, at]
-                up = acc_ref[side, tile, pl.ds(PAD + r0 - 1, n)]
-                level_of = level_lanes(tile)
-                face_x += thick[tile] * jnp.where(min_x > level_of, here - up, 0.0)
-                face_y += thick[tile] * jnp.where(min_y > level_of, here - roll(here, 1), 0.0)
-            fx_ref[side, at] = face_x
-            fy_ref[side, pl.ds(r0, n)] = face_y
     for r0, n in halves:
         lane = lane_iota(n)
         at = pl.ds(PAD + r0, n)
@@ -569,10 +596,8 @@
         west = roll(e_ref[0, at], 8)
         east = roll(e_ref[1, at], 8)
         beside = jnp.where(lane < 8, east, jnp.where(lane >= LANES - 8, west, 0))
-        main = wet_ext_ref[pl.ds(r0, n)]
-        for t, wet in enumerate((main, beside)):
-            for i in range(0, n, 8):
-                d_ref[t, pl.ds(PAD + r0 + i, 8)] = jnp.take_along_axis(table, wet[i : i + 8], axis=1)
+        d_ref[0, at] = depth_in[pl.ds(r0, n)]
+        d_ref[1, at] = look_up(table, beside)
     for r0, n in CHUNKS:
         here = pl.ds(PAD + r0, n)
         d_main, d_side = d_ref[0, here], d_ref[1, here]
@@ -633,7 +658,7 @@
     for i in range(4):
         seen_ref[i] = v_ref[i, 0, pl.ds(PAD, SEEN)]
     depth_ref[...] = d_ref[0, pl.ds(PAD, SEEN)]
-    for r0, n in OWN_CHUNKS:
+    for r0, n in blocks(HALO, HALO + ROWS, 128):
         lane = lane_iota(n)
         at = pl.ds(PAD + r0, n)
         beside = roll(d_ref[1, at], 5)
@@ -664,15 +689,16 @@
             upper = (sub & half) == 0
             keep = tuple(jnp.where(upper, x, y) for x, y in zip(a, b))
             other = tuple(jnp.where(upper, pltpu.roll(x, 8 - half, 0), pltpu.roll(y, half, 0)) for x, y in zip(a, b))
-            merged.append(pair_add(keep, other))
+            merged.append(loose_add(keep, other))
         pairs = merged
     wide = [jnp.concatenate([x, jnp.zeros((LANES - 8, LANES), F32)]).T for x in pairs[0]]
     rows = [tuple(x[at : at + 8] for x in wide) for at in range(0, LANES, 8)]
     while len(rows) > 1:
-        rows = [pair_add(rows[i], rows[i + 1]) for i in range(0, len(rows), 2)]
+        rows = [loose_add(rows[i], rows[i + 1]) for i in range(0, len(rows), 2)]
     total = rows[0]
     for shift in (4, 2, 1):
-        total = pair_add(total, tuple(pltpu.roll(x, shift, 0) for x in total))
+        total = loose_add(total, tuple(pltpu.roll(x, shift, 0) for x in total))
+    total = quick_sum(*total)
     row = total[0] + roll(total[1], MOMENTS)
     for at in range(0, sums_ref.shape[0], 8):
         sums_ref[pl.ds(at, 8)] = row
@@ -680,13 +706,12 @@
 
 def finish_kernel(all_ref, seen_ref, beside_ref, depth_ref, surface_ref, flow_ref, s_ref):
     zero = jnp.zeros((8, LANES), F32)
-    high, low = zero, zero
-    for at in range(0, all_ref.shape[0], 8):
-        high, e = two_sum(high, all_ref[pl.ds(at, 8)])
-        low = low + e
-    total = (high, low)
+    rows = [(all_ref[pl.ds(at, 8)], zero) for at in range(0, all_ref.shape[0], 8)]
+    while len(rows) > 1:
+        rows = [loose_add(rows[i], rows[i + 1]) for i in range(0, len(rows), 2)]
+    total = rows[0]
     for shift in (4, 2, 1):
-        total = pair_add(total, tuple(pltpu.roll(x, shift, 0) for x in total))
+        total = loose_add(total, tuple(pltpu.roll(x, shift, 0) for x in total))
     total = pair_add(total, tuple(roll(x, -MOMENTS) for x in total))
     lane = lane_iota(8)
 
@@ -721,16 +746,16 @@
             residual[i] = pair_add(residual[i], pair_mul(minus, direction[i - 1]))
         for i in range(step + 2):
             direction[i] = pair_add(residual[i], pair_mul(beta, direction[i]))
-    weight = [s[0][0:1] for s in surface]
-    lane = lane_iota(1)
-    by_lane = jnp.zeros((1, LANES), F32)
+    weight = [s[0] for s in surface]
+    lane = lane_iota(8)
+    by_lane = zero
     for i in range(4):
         by_lane = jnp.where(lane == i, weight[i], by_lane)
     for r0, n in blocks(0, SEEN, 88):
         at = pl.ds(r0, n)
-        total = weight[0] * seen_ref[0, at]
+        total = tall(weight[0], n) * seen_ref[0, at]
         for i in range(1, 4):
-            total = total + weight[i] * seen_ref[i, at]
+            total = total + tall(weight[i], n) * seen_ref[i, at]
         s_ref[at] = total
     for r0, n in blocks(HALO, SEEN, 128):
         at = pl.ds(r0, n)
@@ -740,7 +765,7 @@
         s, d = s_ref[at], depth_ref[at]
         beside = beside_ref[own]
         d_west = jnp.where(lane == 0, roll(beside, -4), roll(d, 1))
-        beside = by_lane * beside
+        beside = tall(by_lane, n) * beside
         beside = beside + roll(beside, -1)
         west = jnp.where(lane == 0, beside + roll(beside, -2), roll(s, 1))
         surface_ref[own] = s
@@ -807,21 +832,23 @@
         from_left = ring(to_right, "by", 1)
         from_right = ring(to_left, "by", -1)
     with jax.named_scope("block"):
-        new, source, wet_ext = pl.pallas_call(
+        new, source, depth = pl.pallas_call(
             block_kernel,
-            out_shape=(shape(planes, ROWS, LANES), shape(EXT, LANES), shape(EXT, LANES, dtype=I32)),
+            out_shape=(shape(planes, ROWS, LANES), shape(EXT, LANES), shape(EXT, LANES)),
             in_specs=[SM, SM, HBM, VM, VM, VM],
             out_specs=(HBM, VM, VM),
             scratch_shapes=[
                 scratch(planes, rows=EXT),
                 scratch(dtype=I32),
-                scratch(2, rows=EXT, dtype=I32),
+                scratch(2, rows=EXT),
                 scratch(3, rows=EXT, dtype=I32),
                 scratch(2),
                 scratch(2),
+                scratch(rows=EXT),
                 scratch(),
                 scratch(),
                 scratch(),
+                pltpu.SMEM((KL,), F32),
                 pltpu.SemaphoreType.DMA((KL,)),
                 pltpu.SemaphoreType.DMA((KL,)),
             ],
@@ -829,7 +856,7 @@
             cost_estimate=cost(50_000_000, 12_000_000),
         )(mixing, thickness, flat, top, bottom, wet)
     with jax.named_scope("powers"):
-        seen, beside, depth, sums, new_edge = pl.pallas_call(
+        seen, beside, near_depth, sums, new_edge = pl.pallas_call(
             solve_kernel,
             out_shape=(
                 shape(4, SEEN, LANES),
@@ -846,13 +873,15 @@
                 scratch(2, dtype=I32),
                 scratch(2, dtype=I32),
                 scratch(2, dtype=I32),
-                scratch(2, 2, rows=EXT),
-                scratch(2, 2),
-                scratch(2, 2),
-                scratch(2, rows=EXT),
-                scratch(2, TILES),
+                scratch(3, 2, rows=EXT),
+                scratch(2),
+                scratch(2),
+                scratch(rows=EXT),
+                scratch(),
                 scratch(2),
                 scratch(2, rows=EXT),
+                scratch(2, 2, rows=EXT),
+                scratch(TILES, 4, rows=8),
                 scratch(2),
                 scratch(2),
                 scratch(9, 2, rows=EXT),
@@ -861,7 +890,7 @@
             ],
             compiler_params=params(20),
             cost_estimate=cost(50_000_000, 6_000_000),
-        )(mixing, thickness, source, wet_ext, from_left, from_right, edge)
+        )(mixing, thickness, source, depth, from_left, from_right, edge)
     with jax.named_scope("sums"):
         everyone = lax.all_to_all(sums, ("bx", "by"), 0, 0, tiled=True)
     with jax.named_scope("patch"):
@@ -887,7 +916,7 @@
             scratch_shapes=[scratch(rows=SEEN)],
             compiler_params=params(8),
             cost_estimate=cost(1_000_000, 3_000_000),
-        )(everyone, seen, beside, depth)
+        )(everyone, seen, beside, near_depth)
     return tracers_new.reshape(tracers.shape), surface, transports
 
 

time: 56.8 us -> 56.5 us (level)
  no operation moved by 1% of the time
where the time goes in v5:
time: 56.5 us; the launch traced here: 56.4 us
  Pallas kernels  31.7 us (56%)
  starting transfers between devices  15.9 us (28%)
  waiting for transfers between devices  5.85 us (10%)
  local copies, waits for them, and re-layouts  1.16 us (2%)
  other arithmetic  1.01 us (2%)
  between operations  0.74 us (1%)
    pallas_call x1, Pallas kernels, shards(): pl.pallas_call(block_kernel, out_shape=(shape(planes, ROWS, LANES), shape...  11.6 us
    pallas_call x1, Pallas kernels, shards(): pl.pallas_call(solve_kernel, out_shape=(shape(4, SEEN, LANES), shape(ROWS...  9.64 us
    ppermute x4, starting transfers between devices, ring(): lax.ppermute(x, axis, [(i, (i + step) % count) for i in range(count)])  8.82 us
    all_to_all x1, starting transfers between devices, shards(): everyone = lax.all_to_all(sums, ('bx', 'by'), 0, 0, tiled=True)  7.13 us
    pallas_call x1, Pallas kernels, shards(): pl.pallas_call(patch_kernel, out_shape=shape(planes, ROWS, LANES), in_spe...  4.97 us
    all_to_all x1, waiting for transfers between devices, shards(): everyone = lax.all_to_all(sums, ('bx', 'by'), 0, 0, tiled=True)  4.73 us
    pallas_call x1, Pallas kernels, shards(): pl.pallas_call(own_edges_kernel, out_shape=edges, in_specs=[HBM, VM], out...  3.81 us
    pallas_call x1, Pallas kernels, shards(): pl.pallas_call(finish_kernel, out_shape=(shape(ROWS, LANES), shape(2, ROW...  1.44 us
  transfers between devices with their start and end apart: 5, of which 2 were waited for; matrix products, arithmetic and copies ran while one was open for 0% of the time, Pallas kernels for 36%

profile of v5, /device:TPU:1, one launch (start us, length us, event | category | flops | bytes accessed | tf_op | source)
XLA Modules:
  0.0 56.4 jit_solution(3575983585298465425)
XLA Ops:
  0.6 0.0 copy-start.1
  0.6 0.0 copy-start
  0.7 1.0 %fusion = (f32[44,8,128]{2,1,0:T(8,128)S(1)}, f32[44,8,128]{2,1,0:T(8,128)S(1)}) fusion(f32[44,256,128]{2,1,0:T(8,128)} %bitcast.11), kind=kLoop, calls=%fused_computation.5 | loop fusion | bytes 720896 | tf_op jit(solution)/shard_map/rows/slice | solution.py:808
  1.7 1.0 %select_convert_fusion.wet_ref = f32[256,128]{1,0:T(8,128)S(1)} fusion(s32[256,128]{1,0:T(8,128)} %param.8, s32[256,128]{1,0:T(8,128)} %param.9), kind=kLoop, calls=%fused_computation.2 | loop fusion | flops 98304 | bytes 393216 | tf_op jit(solution)/shard_map/convert_element_type | solution.py:805
  2.7 2.7 %collective-permute-start = (f32[45,8,128]{2,1,0:T(8,128)S(1)}, f32[45,8,128]{2,1,0:T(8,128)S(1)}, u32[]{:S(2)}, u32[]{:S(2)}) collective-permute-start(f32[45,8,128]{2,1,0:T(8,128)S(1)} %pad_maximum_fusion), channel_id=1, source_target_pairs={{0,16},{16,32},{32,48},{48,64},{64,80},{80,96},{96,112},{112,0},{1... | collective-permute-start | bytes 552968 | tf_op jit(solution)/shard_map/rows/ppermute | solution.py:791
  5.4 0.0 collective-permute-start.1
  5.5 3.8 %columns.2 = (f32[2,3,272,128]{3,2,1,0:T(8,128)S(1)}, f32[3,272,128]{2,1,0:T(8,128)S(1)}, f32[3,272,128]{2,1,0:T(8,128)S(1)}) custom-call(f32[44,256,128]{2,1,0:T(8,128)} %bitcast.12, f32[256,128]{1,0:T(8,128)S(1)} %select_convert_fusion.wet_ref), custom_call_target="tpu_custom_call" | custom-call | flops 10000000 | bytes 7000000 | tf_op jit(solution)/shard_map/columns/pallas_call | solution.py:814
  9.3 0.0 collective-permute-done.top_ref
  9.3 1.1 %collective-permute-done.1.bottom_ref = f32[45,8,128]{2,1,0:T(8,128)S(1)} collective-permute-done((f32[45,8,128]{2,1,0:T(8,128)S(1)}, f32[45,8,128]{2,1,0:T(8,128)S(1)}, u32[]{:S(2)}, u32[]{:S(2)}) %collective-permute-start.1) | collective-permute-done | bytes 184352 | tf_op jit(solution)/shard_map/rows/ppermute | solution.py:791
  10.4 0.2 columns.3
  10.6 1.3 %collective-permute-start.2 = (f32[3,272,128]{2,1,0:T(8,128)S(1)}, f32[3,272,128]{2,1,0:T(8,128)S(1)}, u32[]{:S(2)}, u32[]{:S(2)}) collective-permute-start(f32[3,272,128]{2,1,0:T(8,128)S(1)} %get-tuple-element.25), channel_id=1, source_target_pairs={{0,1},{1,2},{2,3},{3,4},{4,5},{5,6},{6,7},{7,8},{8,9},{9,10},{10,1... | collective-permute-start | bytes 1253384 | tf_op jit(solution)/shard_map/columns/ppermute | solution.py:791
  11.9 4.8 %collective-permute-start.3 = (f32[3,272,128]{2,1,0:T(8,128)S(1)}, f32[3,272,128]{2,1,0:T(8,128)S(1)}, u32[]{:S(2)}, u32[]{:S(2)}) collective-permute-start(f32[3,272,128]{2,1,0:T(8,128)S(1)} %get-tuple-element.26), channel_id=1, source_target_pairs={{0,15},{1,0},{2,1},{3,2},{4,3},{5,4},{6,5},{7,6},{8,7},{9,8},{10,9... | collective-permute-start | bytes 1253384 | tf_op jit(solution)/shard_map/columns/ppermute | solution.py:791
  16.7 0.0 copy-done.1
  16.7 0.1 copy.13.mixing_ref
  16.8 0.0 copy-done
  16.8 11.6 %block.1 = (f32[44,256,128]{2,1,0:T(8,128)}, f32[272,128]{1,0:T(8,128)S(1)}, f32[272,128]{1,0:T(8,128)S(1)}) custom-call(f32[22,2]{1,0:T(8,128)S(1)} %copy.13.mixing_ref, f32[22]{0:T(128)S(1)} %copy-done, f32[44,256,128]{2,1,0:T(8,128)} %bitcast.13, f32[45,8,128]{2,1,0:T(8,128)S(1)} %collective-permute-done.top_ref, ...), custom_call_target="tpu_custom_call" | custom-call | flops 50000000 | bytes 12000000 | tf_op jit(solution)/shard_map/block/pallas_call | solution.py:835
  28.4 0.0 collective-permute-done.2.from_left_ref
  28.4 0.0 collective-permute-done.3.from_right_ref
  28.4 9.6 %powers.1 = (f32[4,264,128]{2,1,0:T(8,128)S(1)}, f32[256,128]{1,0:T(8,128)S(1)}, f32[264,128]{1,0:T(8,128)S(1)}, f32[128,128]{1,0:T(8,128)}, f32[2,3,256,128]{3,2,1,0:T(8,128)S(1)}) custom-call(f32[22,2]{1,0:T(8,128)S(1)} %copy.13.mixing_ref, f32[22]{0:T(128)S(1)} %copy-done, f32[272,128]{1,0:T(8,128)S(1)} %get-tuple-element.20.source_ref, ...), custom_call_target="tpu_custom_call" | custom-call | flops 50000000 | bytes 6000000 | tf_op jit(solution)/shard_map/powers/pallas_call | solution.py:859
  38.1 7.1 %all-to-all-start = ((f32[128,1,128]{2,1,0:T(1,128)}), f32[128,1,128]{2,1,0:T(1,128)S(1)}, u32[]{:S(2)}, u32[]{:S(2)}) async-start(f32[128,1,128]{2,1,0:T(1,128)} %bitcast.5), calls=%async_computation | async-start | bytes 131072 | tf_op jit(solution)/shard_map/sums/all_to_all | solution.py:895
  45.2 5.0 %patch.1 = f32[44,256,128]{2,1,0:T(8,128)} custom-call(f32[44,256,128]{2,1,0:T(8,128)} %get-tuple-element.19.new_ref, f32[2,3,256,128]{3,2,1,0:T(8,128)S(1)} %get-tuple-element.28.edge_ref), custom_call_target="tpu_custom_call" | custom-call | flops 10000000 | bytes 12000000 | tf_op jit(solution)/shard_map/patch/pallas_call | solution.py:897
  50.2 4.7 %all-to-all-done = f32[128,1,128]{2,1,0:T(1,128)S(1)} async-done(((f32[128,1,128]{2,1,0:T(1,128)}), f32[128,1,128]{2,1,0:T(1,128)S(1)}, u32[]{:S(2)}, u32[]{:S(2)}) %all-to-all-start) | async-done | bytes 65568 | tf_op jit(solution)/shard_map/sums/all_to_all | solution.py:895
  54.9 1.4 %surface.1 = (f32[256,128]{1,0:T(8,128)}, f32[2,256,128]{2,1,0:T(8,128)}) custom-call(f32[128,128]{1,0:T(8,128)S(1)} %bitcast.10, f32[4,264,128]{2,1,0:T(8,128)S(1)} %get-tuple-element.30.seen_ref, f32[256,128]{1,0:T(8,128)S(1)} %get-tuple-element.31.beside_ref, f32[264,128]{1,0:T(8,128)S(1)} %get-tuple-element.32.depth_ref), custom_call_target="tpu_custom_call" | custom-call | flops 1000000 | bytes 3000000 | tf_op jit(solution)/shard_map/surface/pallas_call | solution.py:911
  (3 shorter events, 0.0 us)
Async XLA Ops:
  0.6 16.1 %copy-start.1 = (f32[22,2]{0,1:T(2,128)S(1)}, f32[22,2]{0,1:T(2,128)}, u32[]{:S(2)}) copy-start(f32[22,2]{0,1:T(2,128)} %param.6) | copy-start | bytes 532
  0.6 16.2 %copy-start = (f32[22]{0:T(128)S(1)}, f32[22]{0:T(128)}, u32[]{:S(2)}) copy-start(f32[22]{0:T(128)} %thick_ref.3) | copy-start | bytes 268
  2.7 6.6 %collective-permute-start = (f32[45,8,128]{2,1,0:T(8,128)S(1)}, f32[45,8,128]{2,1,0:T(8,128)S(1)}, u32[]{:S(2)}, u32[]{:S(2)}) collective-permute-start(f32[45,8,128]{2,1,0:T(8,128)S(1)} %pad_maximum_fusion), channel_id=1, source_target_pairs={{0,16},{16,32},{32,48},{48,64},{64,80},{80,96},{96,112},{112,0},{1... | collective-permute-start | bytes 552968 | tf_op jit(solution)/shard_map/rows/ppermute | solution.py:791
  5.4 5.0 %collective-permute-start.1 = (f32[45,8,128]{2,1,0:T(8,128)S(1)}, f32[45,8,128]{2,1,0:T(8,128)S(1)}, u32[]{:S(2)}, u32[]{:S(2)}) collective-permute-start(f32[45,8,128]{2,1,0:T(8,128)S(1)} %pad_maximum_fusion.1), channel_id=1, source_target_pairs={{0,112},{16,0},{32,16},{48,32},{64,48},{80,64},{96,80},{112,96},{1... | collective-permute-start | bytes 552968 | tf_op jit(solution)/shard_map/rows/ppermute | solution.py:791
  10.6 17.8 %collective-permute-start.2 = (f32[3,272,128]{2,1,0:T(8,128)S(1)}, f32[3,272,128]{2,1,0:T(8,128)S(1)}, u32[]{:S(2)}, u32[]{:S(2)}) collective-permute-start(f32[3,272,128]{2,1,0:T(8,128)S(1)} %get-tuple-element.25), channel_id=1, source_target_pairs={{0,1},{1,2},{2,3},{3,4},{4,5},{5,6},{6,7},{7,8},{8,9},{9,10},{10,1... | collective-permute-start | bytes 1253384 | tf_op jit(solution)/shard_map/columns/ppermute | solution.py:791
  11.9 16.5 %collective-permute-start.3 = (f32[3,272,128]{2,1,0:T(8,128)S(1)}, f32[3,272,128]{2,1,0:T(8,128)S(1)}, u32[]{:S(2)}, u32[]{:S(2)}) collective-permute-start(f32[3,272,128]{2,1,0:T(8,128)S(1)} %get-tuple-element.26), channel_id=1, source_target_pairs={{0,15},{1,0},{2,1},{3,2},{4,3},{5,4},{6,5},{7,6},{8,7},{9,8},{10,9... | collective-permute-start | bytes 1253384 | tf_op jit(solution)/shard_map/columns/ppermute | solution.py:791
  38.1 16.8 %all-to-all-start = ((f32[128,1,128]{2,1,0:T(1,128)}), f32[128,1,128]{2,1,0:T(1,128)S(1)}, u32[]{:S(2)}, u32[]{:S(2)}) async-start(f32[128,1,128]{2,1,0:T(1,128)} %bitcast.5), calls=%async_computation | async-start | bytes 131072 | tf_op jit(solution)/shard_map/sums/all_to_all | solution.py:895

commit v6 on v5

--- a/solution.py
+++ b/solution.py
@@ -17,7 +17,6 @@
 TILES = 3
 LOADS = 4
 MOMENTS = 8
-PATCH = 2
 GRAVITY = 10.0
 SEEN = HALO + ROWS
 F32 = jnp.float32
@@ -107,7 +106,7 @@
 
     for i in range(len(parts)):
         copy(i).start()
-    size = 128
+    size = ROWS
     tile_eff, _ = edge_slot(KL)
 
     def rows_of(step):
@@ -146,7 +145,10 @@
     lax.fori_loop(0, ROWS // size, send, 0)
 
 
-def halo_edges_kernel(top_ref, bottom_ref, edge_in, right_in, left_in, edge_ref, right_ref, left_ref):
+def halo_edges_kernel(top_ref, bottom_ref, edge_in, right_in, left_in, edge_ref, right_ref, left_ref, near_ref):
+    after = lax.broadcasted_iota(I32, (HALO, LANES), 0) < HALO // 2
+    for i in range(2 * KL + 1):
+        near_ref[i] = jnp.where(after, bottom_ref[i], top_ref[i])
     for r0, ref in ((0, top_ref), (HALO + ROWS, bottom_ref)):
         at = pl.ds(r0, HALO)
         held = [[jnp.zeros((HALO, LANES), F32) for _ in range(TILES)] for _ in range(2)]
@@ -176,6 +178,32 @@
     return x, around + (roll(x, 1) + roll(x, -1))
 
 
+def wet_count(word_ref, k, r0, n):
+    words = word_ref[k // 10, pl.ds(r0, n)]
+    shift = jnp.full((n, LANES), 3 * (k % 10), I32)
+    return (lax.shift_right_logical(words, shift) & 7).astype(F32)
+
+
+def level_copies(t_ref, out_ref, ext_ref, in_sems, out_sems):
+    def held(k):
+        return ext_ref.at[pl.ds(2 * k, 2), pl.ds(HALO, ROWS)]
+
+    def load(k):
+        return pltpu.make_async_copy(t_ref.at[pl.ds(2 * k, 2)], held(k), in_sems.at[k])
+
+    def store(k):
+        return pltpu.make_async_copy(held(k), out_ref.at[pl.ds(2 * k, 2)], out_sems.at[k])
+
+    def each(body):
+        def step(k, carry):
+            body(k)
+            return carry
+
+        lax.fori_loop(0, KL, step, 0)
+
+    return load, store, each
+
+
 def block_kernel(
     mixing_ref,
     thick_ref,
@@ -183,7 +211,6 @@
     top_ref,
     bottom_ref,
     wet_ref,
-    new_ref,
     source_ref,
     depth_ref,
     ext_ref,
@@ -198,26 +225,9 @@
     fy_ref,
     begin_ref,
     in_sems,
-    out_sems,
 ):
-    def held(k):
-        return ext_ref.at[pl.ds(2 * k, 2), pl.ds(HALO, ROWS)]
-
-    def load(k):
-        return pltpu.make_async_copy(t_ref.at[pl.ds(2 * k, 2)], held(k), in_sems.at[k])
-
-    def store(k):
-        return pltpu.make_async_copy(held(k), new_ref.at[pl.ds(2 * k, 2)], out_sems.at[k])
-
-    def each(body):
-        def step(k, carry):
-            body(k)
-            return carry
-
-        lax.fori_loop(0, KL, step, 0)
-
+    load, _, each = level_copies(t_ref, None, ext_ref, in_sems, None)
     each(lambda k: load(k).start())
-    eff_ref[...] = jnp.zeros(eff_ref.shape, I32)
     eff_ref[pl.ds(PAD, HALO)] = top_ref[2 * KL].astype(I32)
     eff_ref[pl.ds(PAD + HALO, ROWS)] = wet_ref[...].astype(I32)
     eff_ref[pl.ds(PAD + HALO + ROWS, HALO)] = bottom_ref[2 * KL].astype(I32)
@@ -240,16 +250,9 @@
         for word in range(3):
             word_ref[word, pl.ds(r0, n)] = count_word(effs, word)
 
-    def count(k, r0, n):
-        words = word_ref[k // 10, pl.ds(r0, n)]
-        shift = jnp.full((n, LANES), 3 * (k % 10), I32)
-        return (lax.shift_right_logical(words, shift) & 7).astype(F32)
-
     def body(step, stages):
         if 0 in stages:
             load(step).wait()
-        if 3 in stages:
-            store(step - 3).start()
         ku, kl, kd, kf = (step - late for late in range(4))
 
         def flux(r0, n):
@@ -262,29 +265,23 @@
 
         def density(r0, n):
             wet = eff_ref[pl.ds(PAD + r0, n)] > kd
-            number = n_ref[pl.ds(r0, n)]
-            new = []
-            for c in range(2):
-                x, around = neighbours(l_ref.at[c], r0, n)
-                second = jnp.where(wet, around, 0.0) - number * x
-                value = ext_ref[2 * kd + c, pl.ds(r0, n)] - mixing_ref[kd, c] * second
-                low, high = max(r0, HALO), min(r0 + n, HALO + ROWS)
-                ext_ref[2 * kd + c, pl.ds(low, high - low)] = value[low - r0 : high - r0]
-                new.append(value)
-            rho_ref[pl.ds(PAD + r0, n)] = (0.8 * thick_ref[kd]) * new[1] - (0.2 * thick_ref[kd]) * new[0]
+            x, around = neighbours(l_ref, r0, n)
+            second = jnp.where(wet, around, 0.0) - n_ref[pl.ds(r0, n)] * x
+            a, b = (ext_ref[2 * kd + c, pl.ds(r0, n)] for c in range(2))
+            rho_ref[pl.ds(PAD + r0, n)] = thick_ref[kd] * ((0.8 * b - 0.2 * a) - second)
 
         def first(r0, n):
             wet = eff_ref[pl.ds(PAD + r0, n)] > kl
-            number = count(kl, r0, n)
+            number = wet_count(word_ref, kl, r0, n)
             n_ref[pl.ds(r0, n)] = number
-            for c in range(2):
-                x, around = neighbours(u_ref.at[c], r0, n)
-                l_ref[c, pl.ds(PAD + r0, n)] = jnp.where(wet, around, 0.0) - number * x
+            x, around = neighbours(u_ref, r0, n)
+            l_ref[pl.ds(PAD + r0, n)] = jnp.where(wet, around, 0.0) - number * x
 
         def masked(r0, n):
             wet = eff_ref[pl.ds(PAD + r0, n)] > ku
-            for c in range(2):
-                u_ref[c, pl.ds(PAD + r0, n)] = jnp.where(wet, ext_ref[2 * ku + c, pl.ds(r0, n)], 0.0)
+            a, b = (ext_ref[2 * ku + c, pl.ds(r0, n)] for c in range(2))
+            mixed = (0.8 * mixing_ref[ku, 1]) * b - (0.2 * mixing_ref[ku, 0]) * a
+            u_ref[pl.ds(PAD + r0, n)] = jnp.where(wet, mixed, 0.0)
 
         work = ((3, flux), (2, density), (1, first), (0, masked))
         interleave([part for late, part in work if late in stages])
@@ -302,43 +299,89 @@
         fx = fx_ref[pl.ds(PAD + r0, n)] - fx_ref[pl.ds(PAD + r0 + 1, n)]
         fy = fy_ref[pl.ds(PAD + r0, n)]
         source_ref[pl.ds(r0, n)] = GRAVITY * (fx + (fy - roll(fy, -1)))
-    each(lambda k: store(k).wait())
-
-
-def patch_kernel(new_ref, edge_ref, out_ref, held_ref, in_sems, out_sems):
-    def planes(k):
-        return pl.ds(2 * PATCH * k, 2 * PATCH)
-
-    def load(k):
-        return pltpu.make_async_copy(new_ref.at[planes(k)], held_ref.at[planes(k)], in_sems.at[k])
-
-    def store(k):
-        return pltpu.make_async_copy(held_ref.at[planes(k)], out_ref.at[planes(k)], out_sems.at[k])
-
-    def each(body):
-        def step(k, carry):
-            body(k)
-            return carry
-
-        lax.fori_loop(0, KL // PATCH, step, 0)
-
-    def levels(part):
-        load(part).wait()
-        for i in range(PATCH):
-            k = part * PATCH + i
-            tile = k % TILES
-            back = (2 * LANES - 8 - GROUP * (k // TILES)) % LANES
+
+
+def tracer_kernel(
+    mixing_ref,
+    t_ref,
+    near_ref,
+    wet_ref,
+    edge_ref,
+    out_ref,
+    ext_ref,
+    eff_ref,
+    word_ref,
+    u_ref,
+    l_ref,
+    n_ref,
+    in_sems,
+    out_sems,
+):
+    load, store, each = level_copies(t_ref, out_ref, ext_ref, in_sems, out_sems)
+    each(lambda k: load(k).start())
+    eff_ref[...] = jnp.zeros(eff_ref.shape, I32)
+    eff_ref[pl.ds(PAD, HALO)] = near_ref[2 * KL].astype(I32)
+    eff_ref[pl.ds(PAD + HALO, ROWS)] = wet_ref[...].astype(I32)
+    eff_ref[pl.ds(PAD + HALO + ROWS, HALO)] = near_ref[2 * KL].astype(I32)
+    ext_ref[:, pl.ds(0, HALO)] = near_ref[pl.ds(0, 2 * KL)]
+    ext_ref[:, pl.ds(HALO + ROWS, HALO)] = near_ref[pl.ds(0, 2 * KL)]
+    for ref in (u_ref, l_ref):
+        ref[...] = jnp.zeros(ref.shape, F32)
+    for r0, n in CHUNKS:
+        e = eff_ref[pl.ds(PAD + r0, n)]
+        effs = (eff_ref[pl.ds(PAD + r0 - 1, n)], eff_ref[pl.ds(PAD + r0 + 1, n)], roll(e, 1), roll(e, -1))
+        for word in range(3):
+            word_ref[word, pl.ds(r0, n)] = count_word(effs, word)
+
+    def body(step, stages, ready):
+        if 0 in stages:
+            load(step).wait()
+        if ready:
+            store(step - 3).start()
+        ku, kl, kd = (step - late for late in range(3))
+        tile = kd % TILES
+        back = (2 * LANES - 8 - GROUP * (kd // TILES)) % LANES
+
+        def second(r0, n):
+            low, high = max(r0, HALO), min(r0 + n, HALO + ROWS)
+            size = high - low
+            lane = lane_iota(size)
+            middle = jnp.logical_and(lane >= 4, lane < LANES - 4)
+            wet = eff_ref[pl.ds(PAD + low, size)] > kd
+            number = n_ref[pl.ds(low, size)]
             for c in range(2):
-                for r0, n in blocks(0, ROWS, 64):
-                    lane = lane_iota(n)
-                    middle = jnp.logical_and(lane >= 4, lane < LANES - 4)
-                    own = pl.ds(r0, n)
-                    edge = pltpu.roll(edge_ref[c, tile, own], back, 1)
-                    held_ref[2 * k + c, own] = jnp.where(middle, held_ref[2 * k + c, own], edge)
-        store(part).start()
-
-    each(lambda k: load(k).start())
-    each(levels)
+                x, around = neighbours(l_ref.at[c], low, size)
+                twice = jnp.where(wet, around, 0.0) - number * x
+                value = ext_ref[2 * kd + c, pl.ds(low, size)] - mixing_ref[kd, c] * twice
+                edge = pltpu.roll(edge_ref[c, tile, pl.ds(low - HALO, size)], back, 1)
+                ext_ref[2 * kd + c, pl.ds(low, size)] = jnp.where(middle, value, edge)
+
+        def first(r0, n):
+            wet = eff_ref[pl.ds(PAD + r0, n)] > kl
+            number = wet_count(word_ref, kl, r0, n)
+            n_ref[pl.ds(r0, n)] = number
+            for c in range(2):
+                x, around = neighbours(u_ref.at[c], r0, n)
+                l_ref[c, pl.ds(PAD + r0, n)] = jnp.where(wet, around, 0.0) - number * x
+
+        def masked(r0, n):
+            wet = eff_ref[pl.ds(PAD + r0, n)] > ku
+            for c in range(2):
+                u_ref[c, pl.ds(PAD + r0, n)] = jnp.where(wet, ext_ref[2 * ku + c, pl.ds(r0, n)], 0.0)
+
+        work = ((2, second), (1, first), (0, masked))
+        interleave([part for late, part in work if late in stages])
+
+    def all_stages(step, carry):
+        body(step, range(3), True)
+        return carry
+
+    for step in range(3):
+        body(step, range(step + 1), False)
+    lax.fori_loop(3, KL, all_stages, 0)
+    for step in range(KL, KL + 2):
+        body(step, range(step - KL + 1, 3), True)
+    store(KL - 1).start()
     each(lambda k: store(k).wait())
 
 
@@ -428,7 +471,6 @@
     edge_ref,
     seen_ref,
     beside_ref,
-    depth_ref,
     sums_ref,
     new_ref,
     v_ref,
@@ -657,7 +699,6 @@
 
     for i in range(4):
         seen_ref[i] = v_ref[i, 0, pl.ds(PAD, SEEN)]
-    depth_ref[...] = d_ref[0, pl.ds(PAD, SEEN)]
     for r0, n in blocks(HALO, HALO + ROWS, 128):
         lane = lane_iota(n)
         at = pl.ds(PAD + r0, n)
@@ -704,7 +745,7 @@
         sums_ref[pl.ds(at, 8)] = row
 
 
-def finish_kernel(all_ref, seen_ref, beside_ref, depth_ref, surface_ref, flow_ref, s_ref):
+def finish_kernel(thick_ref, all_ref, seen_ref, beside_ref, near_ref, wet_ref, surface_ref, flow_ref, s_ref, depth_ref):
     zero = jnp.zeros((8, LANES), F32)
     rows = [(all_ref[pl.ds(at, 8)], zero) for at in range(0, all_ref.shape[0], 8)]
     while len(rows) > 1:
@@ -746,6 +787,9 @@
             residual[i] = pair_add(residual[i], pair_mul(minus, direction[i - 1]))
         for i in range(step + 2):
             direction[i] = pair_add(residual[i], pair_mul(beta, direction[i]))
+    table = depth_table(tops(thick_ref))
+    depth_ref[pl.ds(0, HALO)] = look_up(table, near_ref[2 * KL].astype(I32))
+    depth_ref[pl.ds(HALO, ROWS)] = look_up(table, wet_ref[...].astype(I32))
     weight = [s[0] for s in surface]
     lane = lane_iota(8)
     by_lane = zero
@@ -820,11 +864,11 @@
             compiler_params=params(48),
             cost_estimate=cost(10_000_000, 7_000_000),
         )(flat, wet)
-        edge, to_right, to_left = pl.pallas_call(
+        edge, to_right, to_left, near = pl.pallas_call(
             halo_edges_kernel,
-            out_shape=edges,
+            out_shape=edges + (shape(planes + 1, HALO, LANES),),
             in_specs=[VM] * 5,
-            out_specs=(VM,) * 3,
+            out_specs=(VM,) * 4,
             input_output_aliases={i + 2: i for i in range(3)},
             compiler_params=params(16),
             cost_estimate=cost(1_000_000, 700_000),
@@ -832,41 +876,39 @@
         from_left = ring(to_right, "by", 1)
         from_right = ring(to_left, "by", -1)
     with jax.named_scope("block"):
-        new, source, depth = pl.pallas_call(
+        source, depth = pl.pallas_call(
             block_kernel,
-            out_shape=(shape(planes, ROWS, LANES), shape(EXT, LANES), shape(EXT, LANES)),
+            out_shape=(shape(EXT, LANES), shape(EXT, LANES)),
             in_specs=[SM, SM, HBM, VM, VM, VM],
-            out_specs=(HBM, VM, VM),
+            out_specs=(VM, VM),
             scratch_shapes=[
                 scratch(planes, rows=EXT),
                 scratch(dtype=I32),
                 scratch(2, rows=EXT),
                 scratch(3, rows=EXT, dtype=I32),
-                scratch(2),
-                scratch(2),
+                scratch(),
+                scratch(),
                 scratch(rows=EXT),
                 scratch(),
                 scratch(),
                 scratch(),
                 pltpu.SMEM((KL,), F32),
                 pltpu.SemaphoreType.DMA((KL,)),
-                pltpu.SemaphoreType.DMA((KL,)),
             ],
             compiler_params=params(48),
             cost_estimate=cost(50_000_000, 12_000_000),
         )(mixing, thickness, flat, top, bottom, wet)
     with jax.named_scope("powers"):
-        seen, beside, near_depth, sums, new_edge = pl.pallas_call(
+        seen, beside, sums, new_edge = pl.pallas_call(
             solve_kernel,
             out_shape=(
                 shape(4, SEEN, LANES),
                 shape(ROWS, LANES),
-                shape(SEEN, LANES),
                 shape(devices, LANES),
                 shape(2, TILES, ROWS, LANES),
             ),
             in_specs=[SM, SM] + [VM] * 5,
-            out_specs=(VM,) * 5,
+            out_specs=(VM,) * 4,
             scratch_shapes=[
                 scratch(5, 2),
                 scratch(2),
@@ -893,30 +935,35 @@
         )(mixing, thickness, source, depth, from_left, from_right, edge)
     with jax.named_scope("sums"):
         everyone = lax.all_to_all(sums, ("bx", "by"), 0, 0, tiled=True)
-    with jax.named_scope("patch"):
+    with jax.named_scope("tracers"):
         tracers_new = pl.pallas_call(
-            patch_kernel,
+            tracer_kernel,
             out_shape=shape(planes, ROWS, LANES),
-            in_specs=[HBM, VM],
+            in_specs=[SM, HBM, VM, VM, VM],
             out_specs=HBM,
             scratch_shapes=[
-                scratch(planes, rows=ROWS),
-                pltpu.SemaphoreType.DMA((KL // PATCH,)),
-                pltpu.SemaphoreType.DMA((KL // PATCH,)),
+                scratch(planes, rows=EXT),
+                scratch(dtype=I32),
+                scratch(3, rows=EXT, dtype=I32),
+                scratch(2),
+                scratch(2),
+                scratch(rows=EXT),
+                pltpu.SemaphoreType.DMA((KL,)),
+                pltpu.SemaphoreType.DMA((KL,)),
             ],
             compiler_params=params(48),
-            cost_estimate=cost(10_000_000, 12_000_000),
-        )(new, new_edge)
+            cost_estimate=cost(80_000_000, 12_000_000),
+        )(mixing, flat, near, wet, new_edge)
     with jax.named_scope("surface"):
         surface, transports = pl.pallas_call(
             finish_kernel,
             out_shape=(shape(ROWS, LANES), shape(2, ROWS, LANES)),
-            in_specs=[VM] * 4,
+            in_specs=[SM] + [VM] * 5,
             out_specs=(VM, VM),
-            scratch_shapes=[scratch(rows=SEEN)],
+            scratch_shapes=[scratch(rows=SEEN), scratch(rows=SEEN)],
             compiler_params=params(8),
             cost_estimate=cost(1_000_000, 3_000_000),
-        )(everyone, seen, beside, near_depth)
+        )(thickness, everyone, seen, beside, near, wet)
     return tracers_new.reshape(tracers.shape), surface, transports
 
 

time: 56.5 us -> 59.5 us (1.053)
  Pallas kernels: 31.7 us -> 35.4 us
  waiting for transfers between devices: 5.85 us -> 3.26 us
  starting transfers between devices: 15.9 us -> 17.8 us
    all_to_all x1, waiting for transfers between devices: 4.73 us -> 0.01 us  [shards(): everyone = lax.all_to_all(sums, ('bx', 'by'), 0, 0, tiled=True)]
    pallas_call x3, Pallas kernels: 16.8 us -> 20.3 us  [the longest x1 12.2 us: shards(): pl.pallas_call(tracer_kernel, out_shape=shape(planes, ROWS, LANES), in_sp...]
    ppermute x4, waiting for transfers between devices: 1.13 us -> 3.26 us  [ring(): lax.ppermute(x, axis, [(i, (i + step) % count) for i in range(count)])]
    all_to_all x1, starting transfers between devices: 7.13 us -> 8.94 us  [shards(): everyone = lax.all_to_all(sums, ('bx', 'by'), 0, 0, tiled=True)]
  transfers between devices with their start and end apart: 5 -> 5, of which waited for: 2 -> 2; matrix products, arithmetic and copies ran while one was open for 0% -> 0% of each run, Pallas kernels for 36% -> 40%
where the time goes in v6:
time: 59.5 us; the launch traced here: 59.3 us
  Pallas kernels  35.4 us (59%)
  starting transfers between devices  17.8 us (30%)
  waiting for transfers between devices  3.26 us (5%)
  local copies, waits for them, and re-layouts  1.15 us (2%)
  other arithmetic  1.02 us (2%)
  between operations  0.73 us (1%)
    pallas_call x1, Pallas kernels, shards(): pl.pallas_call(tracer_kernel, out_shape=shape(planes, ROWS, LANES), in_sp...  12.2 us
    pallas_call x1, Pallas kernels, shards(): pl.pallas_call(solve_kernel, out_shape=(shape(4, SEEN, LANES), shape(ROWS...  9.65 us
    all_to_all x1, starting transfers between devices, shards(): everyone = lax.all_to_all(sums, ('bx', 'by'), 0, 0, tiled=True)  8.94 us
    ppermute x4, starting transfers between devices, ring(): lax.ppermute(x, axis, [(i, (i + step) % count) for i in range(count)])  8.82 us
    pallas_call x1, Pallas kernels, shards(): pl.pallas_call(block_kernel, out_shape=(shape(EXT, LANES), shape(EXT, LAN...  7.85 us
    pallas_call x1, Pallas kernels, shards(): pl.pallas_call(own_edges_kernel, out_shape=edges, in_specs=[HBM, VM], out...  3.45 us
    ppermute x4, waiting for transfers between devices, ring(): lax.ppermute(x, axis, [(i, (i + step) % count) for i in range(count)])  3.26 us
    pallas_call x1, Pallas kernels, shards(): pl.pallas_call(finish_kernel, out_shape=(shape(ROWS, LANES), shape(2, ROW...  1.99 us
  transfers between devices with their start and end apart: 5, of which 2 were waited for; matrix products, arithmetic and copies ran while one was open for 0% of the time, Pallas kernels for 40%

profile of v6, /device:TPU:1, one launch (start us, length us, event | category | flops | bytes accessed | tf_op | source)
XLA Modules:
  0.0 59.3 jit_solution(7321685825165438915)
XLA Ops:
  0.6 0.0 copy-start.1
  0.6 0.0 copy-start
  0.7 1.0 %select_convert_fusion.wet_ref = f32[256,128]{1,0:T(8,128)S(1)} fusion(s32[256,128]{1,0:T(8,128)} %param.8, s32[256,128]{1,0:T(8,128)} %param.9), kind=kLoop, calls=%fused_computation.2 | loop fusion | flops 98304 | bytes 393216 | tf_op jit(solution)/shard_map/convert_element_type | solution.py:849
  1.7 1.0 %fusion = (f32[44,8,128]{2,1,0:T(8,128)S(1)}, f32[44,8,128]{2,1,0:T(8,128)S(1)}) fusion(f32[44,256,128]{2,1,0:T(8,128)} %bitcast.11), kind=kLoop, calls=%fused_computation.5 | loop fusion | bytes 720896 | tf_op jit(solution)/shard_map/rows/slice | solution.py:852
  2.7 2.7 %collective-permute-start = (f32[45,8,128]{2,1,0:T(8,128)S(1)}, f32[45,8,128]{2,1,0:T(8,128)S(1)}, u32[]{:S(2)}, u32[]{:S(2)}) collective-permute-start(f32[45,8,128]{2,1,0:T(8,128)S(1)} %pad_maximum_fusion), channel_id=1, source_target_pairs={{0,16},{16,32},{32,48},{48,64},{64,80},{80,96},{96,112},{112,0},{1... | collective-permute-start | bytes 552968 | tf_op jit(solution)/shard_map/rows/ppermute | solution.py:835
  5.4 0.0 collective-permute-start.1
  5.5 3.4 %columns.2 = (f32[2,3,272,128]{3,2,1,0:T(8,128)S(1)}, f32[3,272,128]{2,1,0:T(8,128)S(1)}, f32[3,272,128]{2,1,0:T(8,128)S(1)}) custom-call(f32[44,256,128]{2,1,0:T(8,128)} %bitcast.12, f32[256,128]{1,0:T(8,128)S(1)} %select_convert_fusion.wet_ref), custom_call_target="tpu_custom_call" | custom-call | flops 10000000 | bytes 7000000 | tf_op jit(solution)/shard_map/columns/pallas_call | solution.py:858
  8.9 0.0 collective-permute-done.top_ref
  8.9 1.5 %collective-permute-done.1.bottom_ref = f32[45,8,128]{2,1,0:T(8,128)S(1)} collective-permute-done((f32[45,8,128]{2,1,0:T(8,128)S(1)}, f32[45,8,128]{2,1,0:T(8,128)S(1)}, u32[]{:S(2)}, u32[]{:S(2)}) %collective-permute-start.1) | collective-permute-done | bytes 184352 | tf_op jit(solution)/shard_map/rows/ppermute | solution.py:835
  10.4 0.2 columns.3
  10.6 1.3 %collective-permute-start.2 = (f32[3,272,128]{2,1,0:T(8,128)S(1)}, f32[3,272,128]{2,1,0:T(8,128)S(1)}, u32[]{:S(2)}, u32[]{:S(2)}) collective-permute-start(f32[3,272,128]{2,1,0:T(8,128)S(1)} %get-tuple-element.24), channel_id=1, source_target_pairs={{0,1},{1,2},{2,3},{3,4},{4,5},{5,6},{6,7},{7,8},{8,9},{9,10},{10,1... | collective-permute-start | bytes 1253384 | tf_op jit(solution)/shard_map/columns/ppermute | solution.py:835
  11.9 4.8 %collective-permute-start.3 = (f32[3,272,128]{2,1,0:T(8,128)S(1)}, f32[3,272,128]{2,1,0:T(8,128)S(1)}, u32[]{:S(2)}, u32[]{:S(2)}) collective-permute-start(f32[3,272,128]{2,1,0:T(8,128)S(1)} %get-tuple-element.25), channel_id=1, source_target_pairs={{0,15},{1,0},{2,1},{3,2},{4,3},{5,4},{6,5},{7,6},{8,7},{9,8},{10,9... | collective-permute-start | bytes 1253384 | tf_op jit(solution)/shard_map/columns/ppermute | solution.py:835
  16.7 0.0 copy-done.1
  16.7 0.1 copy.16.mixing_ref
  16.8 0.0 copy-done
  16.8 7.8 %block.1 = (f32[272,128]{1,0:T(8,128)S(1)}, f32[272,128]{1,0:T(8,128)S(1)}) custom-call(f32[22,2]{1,0:T(8,128)S(1)} %copy.16.mixing_ref, f32[22]{0:T(128)S(1)} %copy-done, f32[44,256,128]{2,1,0:T(8,128)} %bitcast.13, f32[45,8,128]{2,1,0:T(8,128)S(1)} %collective-permute-done.top_ref, f32[45,8,128]{2,1,0:T(8,128)S(1)} %collective-permute-done.1.bottom_ref, ...), custom_call_target="tpu_custom_call" | custom-call | flops 50000000 | bytes 12000000 | tf_op jit(solution)/shard_map/block/pallas_call | solution.py:879
  24.7 1.8 %collective-permute-done.2.from_left_ref = f32[3,272,128]{2,1,0:T(8,128)S(1)} collective-permute-done((f32[3,272,128]{2,1,0:T(8,128)S(1)}, f32[3,272,128]{2,1,0:T(8,128)S(1)}, u32[]{:S(2)}, u32[]{:S(2)}) %collective-permute-start.2) | collective-permute-done | bytes 417824 | tf_op jit(solution)/shard_map/columns/ppermute | solution.py:835
  26.5 0.0 collective-permute-done.3.from_right_ref
  26.5 9.6 %powers.1 = (f32[4,264,128]{2,1,0:T(8,128)S(1)}, f32[256,128]{1,0:T(8,128)S(1)}, f32[128,128]{1,0:T(8,128)}, f32[2,3,256,128]{3,2,1,0:T(8,128)S(1)}) custom-call(f32[22,2]{1,0:T(8,128)S(1)} %copy.16.mixing_ref, f32[22]{0:T(128)S(1)} %copy-done, f32[272,128]{1,0:T(8,128)S(1)} %get-tuple-element.22.source_ref, f32[272,128]{1,0:T(8,128)S(1)} %get-tuple-element.23.depth_in, ...), custom_call_target="tpu_custom_call" | custom-call | flops 50000000 | bytes 6000000 | tf_op jit(solution)/shard_map/powers/pallas_call | solution.py:902
  36.1 8.9 %all-to-all-start = ((f32[128,1,128]{2,1,0:T(1,128)}), f32[128,1,128]{2,1,0:T(1,128)S(1)}, u32[]{:S(2)}, u32[]{:S(2)}) async-start(f32[128,1,128]{2,1,0:T(1,128)} %bitcast.5), calls=%async_computation | async-start | bytes 131072 | tf_op jit(solution)/shard_map/sums/all_to_all | solution.py:937
  45.0 12.2 %tracers.1 = f32[44,256,128]{2,1,0:T(8,128)} custom-call(f32[22,2]{1,0:T(8,128)S(1)} %copy.16.mixing_ref, f32[44,256,128]{2,1,0:T(8,128)} %bitcast.14, f32[45,8,128]{2,1,0:T(8,128)S(1)} %get-tuple-element.21.near_ref, f32[256,128]{1,0:T(8,128)S(1)} %select_convert_fusion.wet_ref, f32[2,3,256,128]{3,2,1,0:T(8,128)S(1)} %get-tuple-element.27.edge_ref), custom_call_target="tpu_custom_call" | custom-call | flops 80000000 | bytes 12000000 | tf_op jit(solution)/shard_map/tracers/pallas_call | solution.py:939
  57.3 0.0 all-to-all-done
  57.3 2.0 %surface.1 = (f32[256,128]{1,0:T(8,128)}, f32[2,256,128]{2,1,0:T(8,128)}) custom-call(f32[22]{0:T(128)S(1)} %copy-done, f32[128,128]{1,0:T(8,128)S(1)} %bitcast.10, f32[4,264,128]{2,1,0:T(8,128)S(1)} %get-tuple-element.29.seen_ref, f32[256,128]{1,0:T(8,128)S(1)} %get-tuple-element.30.beside_ref, f32[45,8,128]{2,1,0:T(8,128)S(1)} %get-tuple-element.21.near_ref, ...), custom_call_target="tpu_custom_call" | custom-call | flops 1000000 | bytes 3000000 | tf_op jit(solution)/shard_map/surface/pallas_call | solution.py:958
  (3 shorter events, 0.0 us)
Async XLA Ops:
  0.6 16.1 %copy-start.1 = (f32[22,2]{0,1:T(2,128)S(1)}, f32[22,2]{0,1:T(2,128)}, u32[]{:S(2)}) copy-start(f32[22,2]{0,1:T(2,128)} %param.6) | copy-start | bytes 532
  0.6 16.2 %copy-start = (f32[22]{0:T(128)S(1)}, f32[22]{0:T(128)}, u32[]{:S(2)}) copy-start(f32[22]{0:T(128)} %thick_ref.5) | copy-start | bytes 268
  2.7 6.2 %collective-permute-start = (f32[45,8,128]{2,1,0:T(8,128)S(1)}, f32[45,8,128]{2,1,0:T(8,128)S(1)}, u32[]{:S(2)}, u32[]{:S(2)}) collective-permute-start(f32[45,8,128]{2,1,0:T(8,128)S(1)} %pad_maximum_fusion), channel_id=1, source_target_pairs={{0,16},{16,32},{32,48},{48,64},{64,80},{80,96},{96,112},{112,0},{1... | collective-permute-start | bytes 552968 | tf_op jit(solution)/shard_map/rows/ppermute | solution.py:835
  5.4 5.0 %collective-permute-start.1 = (f32[45,8,128]{2,1,0:T(8,128)S(1)}, f32[45,8,128]{2,1,0:T(8,128)S(1)}, u32[]{:S(2)}, u32[]{:S(2)}) collective-permute-start(f32[45,8,128]{2,1,0:T(8,128)S(1)} %pad_maximum_fusion.1), channel_id=1, source_target_pairs={{0,112},{16,0},{32,16},{48,32},{64,48},{80,64},{96,80},{112,96},{1... | collective-permute-start | bytes 552968 | tf_op jit(solution)/shard_map/rows/ppermute | solution.py:835
  10.6 15.8 %collective-permute-start.2 = (f32[3,272,128]{2,1,0:T(8,128)S(1)}, f32[3,272,128]{2,1,0:T(8,128)S(1)}, u32[]{:S(2)}, u32[]{:S(2)}) collective-permute-start(f32[3,272,128]{2,1,0:T(8,128)S(1)} %get-tuple-element.24), channel_id=1, source_target_pairs={{0,1},{1,2},{2,3},{3,4},{4,5},{5,6},{6,7},{7,8},{8,9},{9,10},{10,1... | collective-permute-start | bytes 1253384 | tf_op jit(solution)/shard_map/columns/ppermute | solution.py:835
  11.9 14.6 %collective-permute-start.3 = (f32[3,272,128]{2,1,0:T(8,128)S(1)}, f32[3,272,128]{2,1,0:T(8,128)S(1)}, u32[]{:S(2)}, u32[]{:S(2)}) collective-permute-start(f32[3,272,128]{2,1,0:T(8,128)S(1)} %get-tuple-element.25), channel_id=1, source_target_pairs={{0,15},{1,0},{2,1},{3,2},{4,3},{5,4},{6,5},{7,6},{8,7},{9,8},{10,9... | collective-permute-start | bytes 1253384 | tf_op jit(solution)/shard_map/columns/ppermute | solution.py:835
  36.1 21.2 %all-to-all-start = ((f32[128,1,128]{2,1,0:T(1,128)}), f32[128,1,128]{2,1,0:T(1,128)S(1)}, u32[]{:S(2)}, u32[]{:S(2)}) async-start(f32[128,1,128]{2,1,0:T(1,128)} %bitcast.5), calls=%async_computation | async-start | bytes 131072 | tf_op jit(solution)/shard_map/sums/all_to_all | solution.py:937

commit v7 on v5

--- a/solution.py
+++ b/solution.py
@@ -107,7 +107,7 @@
 
     for i in range(len(parts)):
         copy(i).start()
-    size = 128
+    size = ROWS
     tile_eff, _ = edge_slot(KL)
 
     def rows_of(step):

time: 56.5 us -> 56.4 us (level)
  no operation moved by 1% of the time
where the time goes in v7:
time: 56.4 us; the launch traced here: 56.2 us
  Pallas kernels  31.3 us (55%)
  starting transfers between devices  15.8 us (28%)
  waiting for transfers between devices  6.22 us (11%)
  local copies, waits for them, and re-layouts  1.16 us (2%)
  other arithmetic  1.01 us (2%)
  between operations  0.74 us (1%)
    pallas_call x1, Pallas kernels, shards(): pl.pallas_call(block_kernel, out_shape=(shape(planes, ROWS, LANES), shape...  11.6 us
    pallas_call x1, Pallas kernels, shards(): pl.pallas_call(solve_kernel, out_shape=(shape(4, SEEN, LANES), shape(ROWS...  9.64 us
    ppermute x4, starting transfers between devices, ring(): lax.ppermute(x, axis, [(i, (i + step) % count) for i in range(count)])  8.82 us
    all_to_all x1, starting transfers between devices, shards(): everyone = lax.all_to_all(sums, ('bx', 'by'), 0, 0, tiled=True)  6.93 us
    pallas_call x1, Pallas kernels, shards(): pl.pallas_call(patch_kernel, out_shape=shape(planes, ROWS, LANES), in_spe...  4.97 us
    all_to_all x1, waiting for transfers between devices, shards(): everyone = lax.all_to_all(sums, ('bx', 'by'), 0, 0, tiled=True)  4.73 us
    pallas_call x1, Pallas kernels, shards(): pl.pallas_call(own_edges_kernel, out_shape=edges, in_specs=[HBM, VM], out...  3.45 us
    ppermute x4, waiting for transfers between devices, ring(): lax.ppermute(x, axis, [(i, (i + step) % count) for i in range(count)])  1.49 us
  transfers between devices with their start and end apart: 5, of which 2 were waited for; matrix products, arithmetic and copies ran while one was open for 0% of the time, Pallas kernels for 36%

profile of v7, /device:TPU:1, one launch (start us, length us, event | category | flops | bytes accessed | tf_op | source)
XLA Modules:
  0.0 56.2 jit_solution(13906303011081652806)
XLA Ops:
  0.6 0.0 copy-start.1
  0.6 0.0 copy-start
  0.7 1.0 %fusion = (f32[44,8,128]{2,1,0:T(8,128)S(1)}, f32[44,8,128]{2,1,0:T(8,128)S(1)}) fusion(f32[44,256,128]{2,1,0:T(8,128)} %bitcast.11), kind=kLoop, calls=%fused_computation.5 | loop fusion | bytes 720896 | tf_op jit(solution)/shard_map/rows/slice | solution.py:808
  1.7 1.0 %select_convert_fusion.wet_ref = f32[256,128]{1,0:T(8,128)S(1)} fusion(s32[256,128]{1,0:T(8,128)} %param.8, s32[256,128]{1,0:T(8,128)} %param.9), kind=kLoop, calls=%fused_computation.2 | loop fusion | flops 98304 | bytes 393216 | tf_op jit(solution)/shard_map/convert_element_type | solution.py:805
  2.7 2.7 %collective-permute-start = (f32[45,8,128]{2,1,0:T(8,128)S(1)}, f32[45,8,128]{2,1,0:T(8,128)S(1)}, u32[]{:S(2)}, u32[]{:S(2)}) collective-permute-start(f32[45,8,128]{2,1,0:T(8,128)S(1)} %pad_maximum_fusion), channel_id=1, source_target_pairs={{0,16},{16,32},{32,48},{48,64},{64,80},{80,96},{96,112},{112,0},{1... | collective-permute-start | bytes 552968 | tf_op jit(solution)/shard_map/rows/ppermute | solution.py:791
  5.4 0.0 collective-permute-start.1
  5.5 3.4 %columns.2 = (f32[2,3,272,128]{3,2,1,0:T(8,128)S(1)}, f32[3,272,128]{2,1,0:T(8,128)S(1)}, f32[3,272,128]{2,1,0:T(8,128)S(1)}) custom-call(f32[44,256,128]{2,1,0:T(8,128)} %bitcast.12, f32[256,128]{1,0:T(8,128)S(1)} %select_convert_fusion.wet_ref), custom_call_target="tpu_custom_call" | custom-call | flops 10000000 | bytes 7000000 | tf_op jit(solution)/shard_map/columns/pallas_call | solution.py:814
  8.9 0.0 collective-permute-done.top_ref
  8.9 1.5 %collective-permute-done.1.bottom_ref = f32[45,8,128]{2,1,0:T(8,128)S(1)} collective-permute-done((f32[45,8,128]{2,1,0:T(8,128)S(1)}, f32[45,8,128]{2,1,0:T(8,128)S(1)}, u32[]{:S(2)}, u32[]{:S(2)}) %collective-permute-start.1) | collective-permute-done | bytes 184352 | tf_op jit(solution)/shard_map/rows/ppermute | solution.py:791
  10.4 0.2 columns.3
  10.6 1.3 %collective-permute-start.2 = (f32[3,272,128]{2,1,0:T(8,128)S(1)}, f32[3,272,128]{2,1,0:T(8,128)S(1)}, u32[]{:S(2)}, u32[]{:S(2)}) collective-permute-start(f32[3,272,128]{2,1,0:T(8,128)S(1)} %get-tuple-element.25), channel_id=1, source_target_pairs={{0,1},{1,2},{2,3},{3,4},{4,5},{5,6},{6,7},{7,8},{8,9},{9,10},{10,1... | collective-permute-start | bytes 1253384 | tf_op jit(solution)/shard_map/columns/ppermute | solution.py:791
  11.9 4.8 %collective-permute-start.3 = (f32[3,272,128]{2,1,0:T(8,128)S(1)}, f32[3,272,128]{2,1,0:T(8,128)S(1)}, u32[]{:S(2)}, u32[]{:S(2)}) collective-permute-start(f32[3,272,128]{2,1,0:T(8,128)S(1)} %get-tuple-element.26), channel_id=1, source_target_pairs={{0,15},{1,0},{2,1},{3,2},{4,3},{5,4},{6,5},{7,6},{8,7},{9,8},{10,9... | collective-permute-start | bytes 1253384 | tf_op jit(solution)/shard_map/columns/ppermute | solution.py:791
  16.7 0.0 copy-done.1
  16.7 0.1 copy.13.mixing_ref
  16.8 0.0 copy-done
  16.8 11.6 %block.1 = (f32[44,256,128]{2,1,0:T(8,128)}, f32[272,128]{1,0:T(8,128)S(1)}, f32[272,128]{1,0:T(8,128)S(1)}) custom-call(f32[22,2]{1,0:T(8,128)S(1)} %copy.13.mixing_ref, f32[22]{0:T(128)S(1)} %copy-done, f32[44,256,128]{2,1,0:T(8,128)} %bitcast.13, f32[45,8,128]{2,1,0:T(8,128)S(1)} %collective-permute-done.top_ref, ...), custom_call_target="tpu_custom_call" | custom-call | flops 50000000 | bytes 12000000 | tf_op jit(solution)/shard_map/block/pallas_call | solution.py:835
  28.4 0.0 collective-permute-done.2.from_left_ref
  28.4 0.0 collective-permute-done.3.from_right_ref
  28.4 9.6 %powers.1 = (f32[4,264,128]{2,1,0:T(8,128)S(1)}, f32[256,128]{1,0:T(8,128)S(1)}, f32[264,128]{1,0:T(8,128)S(1)}, f32[128,128]{1,0:T(8,128)}, f32[2,3,256,128]{3,2,1,0:T(8,128)S(1)}) custom-call(f32[22,2]{1,0:T(8,128)S(1)} %copy.13.mixing_ref, f32[22]{0:T(128)S(1)} %copy-done, f32[272,128]{1,0:T(8,128)S(1)} %get-tuple-element.20.source_ref, ...), custom_call_target="tpu_custom_call" | custom-call | flops 50000000 | bytes 6000000 | tf_op jit(solution)/shard_map/powers/pallas_call | solution.py:859
  38.1 6.9 %all-to-all-start = ((f32[128,1,128]{2,1,0:T(1,128)}), f32[128,1,128]{2,1,0:T(1,128)S(1)}, u32[]{:S(2)}, u32[]{:S(2)}) async-start(f32[128,1,128]{2,1,0:T(1,128)} %bitcast.5), calls=%async_computation | async-start | bytes 131072 | tf_op jit(solution)/shard_map/sums/all_to_all | solution.py:895
  45.0 5.0 %patch.1 = f32[44,256,128]{2,1,0:T(8,128)} custom-call(f32[44,256,128]{2,1,0:T(8,128)} %get-tuple-element.19.new_ref, f32[2,3,256,128]{3,2,1,0:T(8,128)S(1)} %get-tuple-element.28.edge_ref), custom_call_target="tpu_custom_call" | custom-call | flops 10000000 | bytes 12000000 | tf_op jit(solution)/shard_map/patch/pallas_call | solution.py:897
  50.0 4.7 %all-to-all-done = f32[128,1,128]{2,1,0:T(1,128)S(1)} async-done(((f32[128,1,128]{2,1,0:T(1,128)}), f32[128,1,128]{2,1,0:T(1,128)S(1)}, u32[]{:S(2)}, u32[]{:S(2)}) %all-to-all-start) | async-done | bytes 65568 | tf_op jit(solution)/shard_map/sums/all_to_all | solution.py:895
  54.7 1.4 %surface.1 = (f32[256,128]{1,0:T(8,128)}, f32[2,256,128]{2,1,0:T(8,128)}) custom-call(f32[128,128]{1,0:T(8,128)S(1)} %bitcast.10, f32[4,264,128]{2,1,0:T(8,128)S(1)} %get-tuple-element.30.seen_ref, f32[256,128]{1,0:T(8,128)S(1)} %get-tuple-element.31.beside_ref, f32[264,128]{1,0:T(8,128)S(1)} %get-tuple-element.32.depth_ref), custom_call_target="tpu_custom_call" | custom-call | flops 1000000 | bytes 3000000 | tf_op jit(solution)/shard_map/surface/pallas_call | solution.py:911
  (3 shorter events, 0.0 us)
Async XLA Ops:
  0.6 16.1 %copy-start.1 = (f32[22,2]{0,1:T(2,128)S(1)}, f32[22,2]{0,1:T(2,128)}, u32[]{:S(2)}) copy-start(f32[22,2]{0,1:T(2,128)} %param.6) | copy-start | bytes 532
  0.6 16.2 %copy-start = (f32[22]{0:T(128)S(1)}, f32[22]{0:T(128)}, u32[]{:S(2)}) copy-start(f32[22]{0:T(128)} %thick_ref.3) | copy-start | bytes 268
  2.7 6.2 %collective-permute-start = (f32[45,8,128]{2,1,0:T(8,128)S(1)}, f32[45,8,128]{2,1,0:T(8,128)S(1)}, u32[]{:S(2)}, u32[]{:S(2)}) collective-permute-start(f32[45,8,128]{2,1,0:T(8,128)S(1)} %pad_maximum_fusion), channel_id=1, source_target_pairs={{0,16},{16,32},{32,48},{48,64},{64,80},{80,96},{96,112},{112,0},{1... | collective-permute-start | bytes 552968 | tf_op jit(solution)/shard_map/rows/ppermute | solution.py:791
  5.4 5.0 %collective-permute-start.1 = (f32[45,8,128]{2,1,0:T(8,128)S(1)}, f32[45,8,128]{2,1,0:T(8,128)S(1)}, u32[]{:S(2)}, u32[]{:S(2)}) collective-permute-start(f32[45,8,128]{2,1,0:T(8,128)S(1)} %pad_maximum_fusion.1), channel_id=1, source_target_pairs={{0,112},{16,0},{32,16},{48,32},{64,48},{80,64},{96,80},{112,96},{1... | collective-permute-start | bytes 552968 | tf_op jit(solution)/shard_map/rows/ppermute | solution.py:791
  10.6 17.8 %collective-permute-start.2 = (f32[3,272,128]{2,1,0:T(8,128)S(1)}, f32[3,272,128]{2,1,0:T(8,128)S(1)}, u32[]{:S(2)}, u32[]{:S(2)}) collective-permute-start(f32[3,272,128]{2,1,0:T(8,128)S(1)} %get-tuple-element.25), channel_id=1, source_target_pairs={{0,1},{1,2},{2,3},{3,4},{4,5},{5,6},{6,7},{7,8},{8,9},{9,10},{10,1... | collective-permute-start | bytes 1253384 | tf_op jit(solution)/shard_map/columns/ppermute | solution.py:791
  11.9 16.5 %collective-permute-start.3 = (f32[3,272,128]{2,1,0:T(8,128)S(1)}, f32[3,272,128]{2,1,0:T(8,128)S(1)}, u32[]{:S(2)}, u32[]{:S(2)}) collective-permute-start(f32[3,272,128]{2,1,0:T(8,128)S(1)} %get-tuple-element.26), channel_id=1, source_target_pairs={{0,15},{1,0},{2,1},{3,2},{4,3},{5,4},{6,5},{7,6},{8,7},{9,8},{10,9... | collective-permute-start | bytes 1253384 | tf_op jit(solution)/shard_map/columns/ppermute | solution.py:791
  38.1 16.6 %all-to-all-start = ((f32[128,1,128]{2,1,0:T(1,128)}), f32[128,1,128]{2,1,0:T(1,128)S(1)}, u32[]{:S(2)}, u32[]{:S(2)}) async-start(f32[128,1,128]{2,1,0:T(1,128)} %bitcast.5), calls=%async_computation | async-start | bytes 131072 | tf_op jit(solution)/shard_map/sums/all_to_all | solution.py:895

commit v8 on v7

--- a/solution.py
+++ b/solution.py
@@ -805,8 +805,10 @@
     wet = wet_levels(levels, land).astype(F32)
     flat = tracers.reshape(planes, ROWS, LANES)
     with jax.named_scope("rows"):
-        to_up = jnp.concatenate([flat[:, :HALO], wet[None, :HALO]])
-        to_down = jnp.concatenate([flat[:, -HALO:], wet[None, -HALO:]])
+        wet_up = wet_levels(levels[:HALO], land[:HALO]).astype(F32)
+        wet_down = wet_levels(levels[-HALO:], land[-HALO:]).astype(F32)
+        to_up = jnp.concatenate([flat[:, :HALO], wet_up[None]])
+        to_down = jnp.concatenate([flat[:, -HALO:], wet_down[None]])
         top = ring(to_down, "bx", 1)
         bottom = ring(to_up, "bx", -1)
     with jax.named_scope("columns"):

time: 56.4 us -> 56.3 us (level)
  waiting for transfers between devices: 6.22 us -> 5.23 us
  other arithmetic: 1.01 us -> 1.76 us
    ppermute x4, waiting for transfers between devices: 1.49 us -> 0.5 us  [ring(): lax.ppermute(x, axis, [(i, (i + step) % count) for i in range(count)])]
    broadcast_in_dim x0 -> x1, other arithmetic: none -> 0.74 us  [shards(): to_up = jnp.concatenate([flat[:, :HALO], wet_up[None]])]
  transfers between devices with their start and end apart: 5 -> 5, of which waited for: 2 -> 2; matrix products, arithmetic and copies ran while one was open for 0% -> 2% of each run, Pallas kernels for 36% -> 36%
where the time goes in v8:
time: 56.3 us; the launch traced here: 56.1 us
  Pallas kernels  31.3 us (56%)
  starting transfers between devices  15.9 us (28%)
  waiting for transfers between devices  5.23 us (9%)
  other arithmetic  1.76 us (3%)
  local copies, waits for them, and re-layouts  1.15 us (2%)
  between operations  0.73 us (1%)
    pallas_call x1, Pallas kernels, shards(): pl.pallas_call(block_kernel, out_shape=(shape(planes, ROWS, LANES), shape...  11.6 us
    pallas_call x1, Pallas kernels, shards(): pl.pallas_call(solve_kernel, out_shape=(shape(4, SEEN, LANES), shape(ROWS...  9.64 us
    ppermute x4, starting transfers between devices, ring(): lax.ppermute(x, axis, [(i, (i + step) % count) for i in range(count)])  8.82 us
    all_to_all x1, starting transfers between devices, shards(): everyone = lax.all_to_all(sums, ('bx', 'by'), 0, 0, tiled=True)  7.13 us
    pallas_call x1, Pallas kernels, shards(): pl.pallas_call(patch_kernel, out_shape=shape(planes, ROWS, LANES), in_spe...  4.97 us
    all_to_all x1, waiting for transfers between devices, shards(): everyone = lax.all_to_all(sums, ('bx', 'by'), 0, 0, tiled=True)  4.73 us
    pallas_call x1, Pallas kernels, shards(): pl.pallas_call(own_edges_kernel, out_shape=edges, in_specs=[HBM, VM], out...  3.45 us
    pallas_call x1, Pallas kernels, shards(): pl.pallas_call(finish_kernel, out_shape=(shape(ROWS, LANES), shape(2, ROW...  1.44 us
  transfers between devices with their start and end apart: 5, of which 2 were waited for; matrix products, arithmetic and copies ran while one was open for 2% of the time, Pallas kernels for 36%

profile of v8, /device:TPU:1, one launch (start us, length us, event | category | flops | bytes accessed | tf_op | source)
XLA Modules:
  0.0 56.1 jit_solution(18281544380417835455)
XLA Ops:
  0.6 0.0 copy-start.1
  0.6 0.0 copy-start
  0.7 1.0 %fusion = (f32[44,8,128]{2,1,0:T(8,128)S(1)}, f32[44,8,128]{2,1,0:T(8,128)S(1)}) fusion(f32[44,256,128]{2,1,0:T(8,128)} %bitcast.11), kind=kLoop, calls=%fused_computation.7 | loop fusion | bytes 720896 | tf_op jit(solution)/shard_map/rows/slice | solution.py:810
  1.7 0.7 %convert_bitcast_fusion = (f32[1,8,128]{2,1,0:T(8,128)S(1)}, f32[1,8,128]{2,1,0:T(8,128)S(1)}) fusion(s32[256,128]{1,0:T(8,128)} %param.8, s32[256,128]{1,0:T(8,128)} %param.9), kind=kLoop, calls=%fused_computation.3 | loop fusion | flops 6144 | bytes 24576 | tf_op jit(solution)/shard_map/rows/broadcast_in_dim | solution.py:810
  2.5 2.7 %collective-permute-start = (f32[45,8,128]{2,1,0:T(8,128)S(1)}, f32[45,8,128]{2,1,0:T(8,128)S(1)}, u32[]{:S(2)}, u32[]{:S(2)}) collective-permute-start(f32[45,8,128]{2,1,0:T(8,128)S(1)} %pad_maximum_fusion), channel_id=1, source_target_pairs={{0,16},{16,32},{32,48},{48,64},{64,80},{80,96},{96,112},{112,0},{1... | collective-permute-start | bytes 552968 | tf_op jit(solution)/shard_map/rows/ppermute | solution.py:791
  5.2 0.0 collective-permute-start.1
  5.2 1.0 %select_convert_fusion.wet_ref = f32[256,128]{1,0:T(8,128)S(1)} fusion(s32[256,128]{1,0:T(8,128)} %param.8, s32[256,128]{1,0:T(8,128)} %param.9), kind=kLoop, calls=%fused_computation.2 | loop fusion | flops 98304 | bytes 393216 | tf_op jit(solution)/shard_map/convert_element_type | solution.py:805
  6.2 3.4 %columns.2 = (f32[2,3,272,128]{3,2,1,0:T(8,128)S(1)}, f32[3,272,128]{2,1,0:T(8,128)S(1)}, f32[3,272,128]{2,1,0:T(8,128)S(1)}) custom-call(f32[44,256,128]{2,1,0:T(8,128)} %bitcast.12, f32[256,128]{1,0:T(8,128)S(1)} %select_convert_fusion.wet_ref), custom_call_target="tpu_custom_call" | custom-call | flops 10000000 | bytes 7000000 | tf_op jit(solution)/shard_map/columns/pallas_call | solution.py:816
  9.7 0.0 collective-permute-done.top_ref
  9.7 0.5 collective-permute-done.1.bottom_ref
  10.2 0.2 columns.3
  10.4 1.3 %collective-permute-start.2 = (f32[3,272,128]{2,1,0:T(8,128)S(1)}, f32[3,272,128]{2,1,0:T(8,128)S(1)}, u32[]{:S(2)}, u32[]{:S(2)}) collective-permute-start(f32[3,272,128]{2,1,0:T(8,128)S(1)} %get-tuple-element.25), channel_id=1, source_target_pairs={{0,1},{1,2},{2,3},{3,4},{4,5},{5,6},{6,7},{7,8},{8,9},{9,10},{10,1... | collective-permute-start | bytes 1253384 | tf_op jit(solution)/shard_map/columns/ppermute | solution.py:791
  11.6 4.8 %collective-permute-start.3 = (f32[3,272,128]{2,1,0:T(8,128)S(1)}, f32[3,272,128]{2,1,0:T(8,128)S(1)}, u32[]{:S(2)}, u32[]{:S(2)}) collective-permute-start(f32[3,272,128]{2,1,0:T(8,128)S(1)} %get-tuple-element.26), channel_id=1, source_target_pairs={{0,15},{1,0},{2,1},{3,2},{4,3},{5,4},{6,5},{7,6},{8,7},{9,8},{10,9... | collective-permute-start | bytes 1253384 | tf_op jit(solution)/shard_map/columns/ppermute | solution.py:791
  16.5 0.0 copy-done.1
  16.5 0.1 copy.13.mixing_ref
  16.6 0.0 copy-done
  16.6 11.6 %block.1 = (f32[44,256,128]{2,1,0:T(8,128)}, f32[272,128]{1,0:T(8,128)S(1)}, f32[272,128]{1,0:T(8,128)S(1)}) custom-call(f32[22,2]{1,0:T(8,128)S(1)} %copy.13.mixing_ref, f32[22]{0:T(128)S(1)} %copy-done, f32[44,256,128]{2,1,0:T(8,128)} %bitcast.13, f32[45,8,128]{2,1,0:T(8,128)S(1)} %collective-permute-done.top_ref, ...), custom_call_target="tpu_custom_call" | custom-call | flops 50000000 | bytes 12000000 | tf_op jit(solution)/shard_map/block/pallas_call | solution.py:837
  28.2 0.0 collective-permute-done.2.from_left_ref
  28.2 0.0 collective-permute-done.3.from_right_ref
  28.2 9.6 %powers.1 = (f32[4,264,128]{2,1,0:T(8,128)S(1)}, f32[256,128]{1,0:T(8,128)S(1)}, f32[264,128]{1,0:T(8,128)S(1)}, f32[128,128]{1,0:T(8,128)}, f32[2,3,256,128]{3,2,1,0:T(8,128)S(1)}) custom-call(f32[22,2]{1,0:T(8,128)S(1)} %copy.13.mixing_ref, f32[22]{0:T(128)S(1)} %copy-done, f32[272,128]{1,0:T(8,128)S(1)} %get-tuple-element.20.source_ref, ...), custom_call_target="tpu_custom_call" | custom-call | flops 50000000 | bytes 6000000 | tf_op jit(solution)/shard_map/powers/pallas_call | solution.py:861
  37.8 7.1 %all-to-all-start = ((f32[128,1,128]{2,1,0:T(1,128)}), f32[128,1,128]{2,1,0:T(1,128)S(1)}, u32[]{:S(2)}, u32[]{:S(2)}) async-start(f32[128,1,128]{2,1,0:T(1,128)} %bitcast.5), calls=%async_computation | async-start | bytes 131072 | tf_op jit(solution)/shard_map/sums/all_to_all | solution.py:897
  45.0 5.0 %patch.1 = f32[44,256,128]{2,1,0:T(8,128)} custom-call(f32[44,256,128]{2,1,0:T(8,128)} %get-tuple-element.19.new_ref, f32[2,3,256,128]{3,2,1,0:T(8,128)S(1)} %get-tuple-element.28.edge_ref), custom_call_target="tpu_custom_call" | custom-call | flops 10000000 | bytes 12000000 | tf_op jit(solution)/shard_map/patch/pallas_call | solution.py:899
  49.9 4.7 %all-to-all-done = f32[128,1,128]{2,1,0:T(1,128)S(1)} async-done(((f32[128,1,128]{2,1,0:T(1,128)}), f32[128,1,128]{2,1,0:T(1,128)S(1)}, u32[]{:S(2)}, u32[]{:S(2)}) %all-to-all-start) | async-done | bytes 65568 | tf_op jit(solution)/shard_map/sums/all_to_all | solution.py:897
  54.7 1.4 %surface.1 = (f32[256,128]{1,0:T(8,128)}, f32[2,256,128]{2,1,0:T(8,128)}) custom-call(f32[128,128]{1,0:T(8,128)S(1)} %bitcast.10, f32[4,264,128]{2,1,0:T(8,128)S(1)} %get-tuple-element.30.seen_ref, f32[256,128]{1,0:T(8,128)S(1)} %get-tuple-element.31.beside_ref, f32[264,128]{1,0:T(8,128)S(1)} %get-tuple-element.32.depth_ref), custom_call_target="tpu_custom_call" | custom-call | flops 1000000 | bytes 3000000 | tf_op jit(solution)/shard_map/surface/pallas_call | solution.py:913
  (2 shorter events, 0.0 us)
Async XLA Ops:
  0.6 15.8 %copy-start.1 = (f32[22,2]{0,1:T(2,128)S(1)}, f32[22,2]{0,1:T(2,128)}, u32[]{:S(2)}) copy-start(f32[22,2]{0,1:T(2,128)} %param.6) | copy-start | bytes 532
  0.6 15.9 %copy-start = (f32[22]{0:T(128)S(1)}, f32[22]{0:T(128)}, u32[]{:S(2)}) copy-start(f32[22]{0:T(128)} %thick_ref.3) | copy-start | bytes 268
  2.5 7.2 %collective-permute-start = (f32[45,8,128]{2,1,0:T(8,128)S(1)}, f32[45,8,128]{2,1,0:T(8,128)S(1)}, u32[]{:S(2)}, u32[]{:S(2)}) collective-permute-start(f32[45,8,128]{2,1,0:T(8,128)S(1)} %pad_maximum_fusion), channel_id=1, source_target_pairs={{0,16},{16,32},{32,48},{48,64},{64,80},{80,96},{96,112},{112,0},{1... | collective-permute-start | bytes 552968 | tf_op jit(solution)/shard_map/rows/ppermute | solution.py:791
  5.2 5.0 %collective-permute-start.1 = (f32[45,8,128]{2,1,0:T(8,128)S(1)}, f32[45,8,128]{2,1,0:T(8,128)S(1)}, u32[]{:S(2)}, u32[]{:S(2)}) collective-permute-start(f32[45,8,128]{2,1,0:T(8,128)S(1)} %pad_maximum_fusion.1), channel_id=1, source_target_pairs={{0,112},{16,0},{32,16},{48,32},{64,48},{80,64},{96,80},{112,96},{1... | collective-permute-start | bytes 552968 | tf_op jit(solution)/shard_map/rows/ppermute | solution.py:791
  10.4 17.8 %collective-permute-start.2 = (f32[3,272,128]{2,1,0:T(8,128)S(1)}, f32[3,272,128]{2,1,0:T(8,128)S(1)}, u32[]{:S(2)}, u32[]{:S(2)}) collective-permute-start(f32[3,272,128]{2,1,0:T(8,128)S(1)} %get-tuple-element.25), channel_id=1, source_target_pairs={{0,1},{1,2},{2,3},{3,4},{4,5},{5,6},{6,7},{7,8},{8,9},{9,10},{10,1... | collective-permute-start | bytes 1253384 | tf_op jit(solution)/shard_map/columns/ppermute | solution.py:791
  11.6 16.5 %collective-permute-start.3 = (f32[3,272,128]{2,1,0:T(8,128)S(1)}, f32[3,272,128]{2,1,0:T(8,128)S(1)}, u32[]{:S(2)}, u32[]{:S(2)}) collective-permute-start(f32[3,272,128]{2,1,0:T(8,128)S(1)} %get-tuple-element.26), channel_id=1, source_target_pairs={{0,15},{1,0},{2,1},{3,2},{4,3},{5,4},{6,5},{7,6},{8,7},{9,8},{10,9... | collective-permute-start | bytes 1253384 | tf_op jit(solution)/shard_map/columns/ppermute | solution.py:791
  37.8 16.8 %all-to-all-start = ((f32[128,1,128]{2,1,0:T(1,128)}), f32[128,1,128]{2,1,0:T(1,128)S(1)}, u32[]{:S(2)}, u32[]{:S(2)}) async-start(f32[128,1,128]{2,1,0:T(1,128)} %bitcast.5), calls=%async_computation | async-start | bytes 131072 | tf_op jit(solution)/shard_map/sums/all_to_all | solution.py:897
